TPU v7x, 32 devices: a whole 2x2x4 slice. The times are simulated.
32 devices in a mesh: group: 4 (over z), local: 8 (over y, x, core).
Axes of the slice: x: 2, y: 2, z: 4, core: 2. Of those that a mesh axis runs over, the one named last changes fastest.
Arguments:
- features: bfloat16 [65536, 512], P(('group', 'local')), may hold values from -6 to 6
- weight: bfloat16 [512, 512], replicated, may hold values from -0.25 to 0.25
- cotangent: bfloat16 [65536, 512], P(('group', 'local')), may hold values from -6 to 6
- tile_vals: bfloat16 [8192, 128, 128], P(('group', 'local')), may hold values from -0.125 to 0.125
- tile_rows: int32 [8192], P(('group', 'local')), may hold values from 0 to 15
- tile_cols: int32 [8192], P(('group', 'local')), may hold values from 0 to 23
- send_rows: int32 [32, 32, 32], P(('group', 'local')), may hold values from 0 to 2047, as said below
- counts: int32 [32, 32], P(('group', 'local')), may hold values from 1 to 32, as said below
Outputs:
- activated: bfloat16 [65536, 512], P(('group', 'local'))
- feature_grad: bfloat16 [65536, 512], P(('group', 'local'))
- weight_grad: float32 [512, 512], replicated
Inputs may be any that keep to these rules, and one draw needn't show every extreme that they name: Each list send_rows[s, d] holds 32 distinct local row numbers of device s. `counts`: some destinations are busy: every source sends them 32 rows; at least one such destination exists.
All inputs are finite; a program needn't handle non-finite values.
Results may differ from a plain program's by a relative error of at most 0.006.
Values may be sent and summed in bfloat16 or wider, within the bound.
No kernel may reach another device: no remote copies, remote signals or barrier semaphores. Data moves between devices by JAX's collectives and lax.ppermute only.
A program may use at most 192 MiB of HBM per device.

v0:
```python
import functools

import jax
import jax.numpy as jnp
from jax import lax
from jax.experimental import pallas as pl
from jax.experimental.pallas import tpu as pltpu
from jax.sharding import PartitionSpec as P

AXES = ("group", "local")
BF16 = jnp.bfloat16
F32 = jnp.float32
ROWS = 256
LIMIT = 56 * 1024 * 1024


def params():
    return pltpu.CompilerParams(vmem_limit_bytes=LIMIT)


def dot(a, b, contract=((1,), (0,))):
    return lax.dot_general(a, b, (contract, ((), ())), preferred_element_type=F32)


def whole(shape):
    return pl.BlockSpec(shape, lambda i, *unused: (0,) * len(shape))


def collect_kernel(index_ref, x_ref, out_ref):
    slots, width = index_ref.shape[0], x_ref.shape[0]
    dests = out_ref.shape[0] // slots
    step = ROWS // slots
    lane = lax.broadcasted_iota(jnp.int32, (slots, width), 1)
    for first in range(0, dests, step):
        parts = []
        for d in range(first, first + step):
            hit = index_ref[:, d : d + 1] == lane
            parts.append(jnp.where(hit, 1.0, 0.0).astype(BF16))
        pick = jnp.concatenate(parts, axis=0)
        out_ref[first * slots : (first + step) * slots, :] = dot(pick, x_ref[...]).astype(BF16)


def collect(index, x):
    slots, dests = index.shape
    return pl.pallas_call(
        collect_kernel,
        out_shape=jax.ShapeDtypeStruct((dests * slots, x.shape[1]), BF16),
        compiler_params=params(),
        name="collect",
    )(index, x)


def build_kernel(rows_ref, cols_ref, tiles_ref, x_ref, adj_ref, own_ref, total, order, starts, cursor):
    num_tiles, edge = tiles_ref.shape[0], tiles_ref.shape[1]
    per = ROWS // edge
    blocks = pl.num_programs(0)
    i = pl.program_id(0)

    @pl.when(i == 0)
    def _():
        def clear(b, unused):
            starts[b] = 0
            return unused

        lax.fori_loop(0, blocks + 1, clear, 0)

        def count(t, unused):
            k = rows_ref[t] // per + 1
            starts[k] = starts[k] + 1
            return unused

        lax.fori_loop(0, num_tiles, count, 0, unroll=4)

        def add(b, running):
            running = running + starts[b]
            starts[b] = running
            cursor[b] = running
            return running

        lax.fori_loop(0, blocks + 1, add, 0)

        def place(t, unused):
            k = rows_ref[t] // per
            at = cursor[k]
            cursor[k] = at + 1
            order[at] = t
            return unused

        lax.fori_loop(0, num_tiles, place, 0, unroll=4)

    total[...] = jnp.zeros_like(total)

    def one(j, unused):
        t = order[j]
        r = pl.multiple_of((rows_ref[t] % per) * edge, edge)
        c = pl.multiple_of(cols_ref[t] * edge, edge)
        at = (pl.ds(r, edge), pl.ds(c, edge))
        total[at] = total[at] + tiles_ref[t].astype(F32)
        return unused

    lax.fori_loop(starts[i], starts[i + 1], one, 0)
    adj_ref[...] = total[...].astype(BF16)
    owned = x_ref.shape[0]
    own_ref[...] = dot(adj_ref[:, :owned], x_ref[...])


def build(tile_rows, tile_cols, tile_vals, x, extended):
    owned, width = x.shape
    num_tiles = tile_vals.shape[0]
    blocks = owned // ROWS
    return pl.pallas_call(
        build_kernel,
        grid_spec=pltpu.PrefetchScalarGridSpec(
            num_scalar_prefetch=2,
            grid=(blocks,),
            in_specs=[whole(tile_vals.shape), whole(x.shape)],
            out_specs=[
                pl.BlockSpec((ROWS, extended), lambda i, *unused: (i, 0)),
                pl.BlockSpec((ROWS, width), lambda i, *unused: (i, 0)),
            ],
            scratch_shapes=[
                pltpu.VMEM((ROWS, extended), F32),
                pltpu.SMEM((num_tiles,), jnp.int32),
                pltpu.SMEM((blocks + 1,), jnp.int32),
                pltpu.SMEM((blocks + 1,), jnp.int32),
            ],
        ),
        out_shape=[
            jax.ShapeDtypeStruct((owned, extended), BF16),
            jax.ShapeDtypeStruct((owned, width), F32),
        ],
        compiler_params=params(),
        cost_estimate=pl.CostEstimate(
            flops=2 * owned * owned * width, bytes_accessed=40 * 1024 * 1024, transcendentals=0
        ),
        name="build",
    )(tile_rows, tile_cols, tile_vals, x)


def layer_kernel(adj_ref, own_ref, far_ref, cot_ref, w_ref, act_ref, hid_ref, slope_ref, grad_ref, back_ref, total):
    i = pl.program_id(0)
    hidden = (own_ref[...] + dot(adj_ref[...], far_ref[...])).astype(BF16)
    hid_ref[...] = hidden
    w = w_ref[...]
    preact = dot(hidden, w)
    gate = 0.5 + 0.5 * jnp.tanh(0.5 * preact)
    act_ref[...] = (preact * gate).astype(BF16)
    slope = (cot_ref[...].astype(F32) * gate * (1.0 + preact * (1.0 - gate))).astype(BF16)
    slope_ref[...] = slope
    grad = dot(w, slope, ((1,), (1,))).astype(BF16)
    grad_ref[...] = grad
    part = dot(grad, adj_ref[...])

    @pl.when(i == 0)
    def _():
        total[...] = part

    @pl.when(i > 0)
    def _():
        total[...] += part

    @pl.when(i == pl.num_programs(0) - 1)
    def _():
        back_ref[...] = total[...].astype(BF16).T


def layer(adjacency, own, far, cotangent, weight):
    owned, width = own.shape
    remote = far.shape[0]
    assert owned % remote == 0 or remote % owned == 0
    rows = pl.BlockSpec((ROWS, width), lambda i: (i, 0))
    rows_type = jax.ShapeDtypeStruct((owned, width), BF16)
    return pl.pallas_call(
        layer_kernel,
        grid=(owned // ROWS,),
        in_specs=[
            pl.BlockSpec((pl.Element(ROWS), pl.Element(remote)), lambda i: (i * ROWS, owned)),
            rows,
            whole(far.shape),
            rows,
            whole(weight.shape),
        ],
        out_specs=[
            rows,
            rows,
            rows,
            pl.BlockSpec((width, ROWS), lambda i: (0, i)),
            whole(far.shape),
        ],
        out_shape=[
            rows_type,
            rows_type,
            rows_type,
            jax.ShapeDtypeStruct((width, owned), BF16),
            jax.ShapeDtypeStruct(far.shape, BF16),
        ],
        scratch_shapes=[pltpu.VMEM((width, remote), F32)],
        compiler_params=params(),
        name="layer",
    )(adjacency, own, far, cotangent, weight)


def spread_kernel(adj_ref, grad_ref, out_ref):
    out_ref[...] = dot(grad_ref[...], adj_ref[...]).T


def spread(adjacency, grad):
    width, owned = grad.shape
    return pl.pallas_call(
        spread_kernel,
        grid=(owned // ROWS,),
        in_specs=[pl.BlockSpec((owned, ROWS), lambda i: (0, i)), whole(grad.shape)],
        out_specs=pl.BlockSpec((ROWS, width), lambda i: (i, 0)),
        out_shape=jax.ShapeDtypeStruct((owned, width), F32),
        compiler_params=params(),
        cost_estimate=pl.CostEstimate(
            flops=2 * owned * owned * width, bytes_accessed=16 * 1024 * 1024, transcendentals=0
        ),
        name="spread",
    )(adjacency, grad)


def return_kernel(index_ref, owned_ref, back_ref, out_ref):
    base = pl.program_id(0) * ROWS
    row = lax.broadcasted_iota(jnp.int32, (ROWS, index_ref.shape[1]), 0) + base
    pick = jnp.where(row == index_ref[...], 1.0, 0.0).astype(BF16)
    out_ref[...] = (owned_ref[...] + dot(pick, back_ref[...])).astype(BF16)


def give_back(index, owned, back):
    rows, width = owned.shape
    block = pl.BlockSpec((ROWS, width), lambda i: (i, 0))
    return pl.pallas_call(
        return_kernel,
        grid=(rows // ROWS,),
        in_specs=[whole(index.shape), block, whole(back.shape)],
        out_specs=block,
        out_shape=jax.ShapeDtypeStruct((rows, width), BF16),
        compiler_params=params(),
        name="give_back",
    )(index, owned, back)


def exchange(x, axes):
    return lax.all_to_all(x, axes, split_axis=0, concat_axis=0, tiled=True)


def reduce_everywhere(partial, groups, locals_):
    height, width = partial.shape
    pieces = exchange(partial.astype(BF16).reshape(locals_, height // locals_, width), "local")
    piece = jnp.sum(pieces.astype(F32), axis=0).astype(BF16)
    pieces = exchange(jnp.broadcast_to(piece[None], (groups,) + piece.shape), "group")
    piece = jnp.sum(pieces.astype(F32), axis=0).astype(BF16)
    pieces = exchange(jnp.broadcast_to(piece[None], (locals_,) + piece.shape), "local")
    return pieces.reshape(height, width).astype(F32)


def per_device(groups, locals_, features, weight, cotangent, tile_vals, tile_rows, tile_cols, send_rows, counts):
    rows_own, width = features.shape
    lists = send_rows[0]
    peers, slots = lists.shape
    live = jnp.arange(slots)[None, :] < counts[0][:, None]
    index = jnp.where(live, lists, -1)
    outgoing = collect(index.T, features)
    arrived = exchange(outgoing.reshape(peers, slots, width), AXES).reshape(peers * slots, width)
    adjacency, own = build(tile_rows, tile_cols, tile_vals, features, rows_own + peers * slots)
    activated, hidden, slope, grad, back = layer(adjacency, own, arrived, cotangent, weight)
    returned = exchange(back.reshape(peers, slots, width), AXES).reshape(peers * slots, width)
    partial = dot(hidden, slope, ((0,), (0,)))
    weight_grad = reduce_everywhere(partial, groups, locals_)
    owned = spread(adjacency, grad)
    feature_grad = give_back(index.reshape(1, peers * slots), owned, returned)
    return activated, feature_grad, weight_grad


def solution(mesh):
    return jax.shard_map(
        functools.partial(per_device, mesh.shape["group"], mesh.shape["local"]),
        mesh=mesh,
        in_specs=(
            P(AXES, None),
            P(),
            P(AXES, None),
            P(AXES, None, None),
            P(AXES),
            P(AXES),
            P(AXES, None, None),
            P(AXES, None),
        ),
        out_specs=(P(AXES, None), P(AXES, None), P()),
        check_vma=False,
    )
```

profile of v0, /device:TPU:0, one launch (start us, length us, event | category | flops | bytes accessed | tf_op | source)
XLA Modules:
  0.0 137.8 jit_solution(10210408490350532894)
XLA Ops:
  0.6 0.8 copy.13
  1.4 1.3 fusion.index_ref
  2.7 4.9 %collect.1 = bf16[1024,512]{1,0:T(8,128)(2,1)} custom-call(s32[32,32]{1,0:T(8,128)} %fusion.index_ref, bf16[2048,512]{1,0:T(8,128)(2,1)} %x_ref.3), custom_call_target="tpu_custom_call" | custom-call | tf_op jit(solution)/shard_map/collect/pallas_call | solution.py:45
  7.6 7.3 %all-to-all-start = ((bf16[32,32,512]{2,1,0:T(8,128)(2,1)}), bf16[32,32,512]{2,1,0:T(8,128)(2,1)S(1)}, u32[]{:S(2)}, u32[]{:S(2)}) async-start(bf16[32,32,512]{2,1,0:T(8,128)(2,1)} %bitcast.19), calls=%async_computation | async-start | bytes 2097152 | tf_op jit(solution)/shard_map/all_to_all | solution.py:245
  14.9 19.7 %build.1 = (bf16[2048,3072]{1,0:T(8,128)(2,1)}, f32[2048,512]{1,0:T(8,128)}) custom-call(s32[256]{0:T(256)} %rows_ref.1, s32[256]{0:T(256)} %cols_ref.1, bf16[256,128,128]{2,1,0:T(8,128)(2,1)} %tiles_ref.1, bf16[2048,512]{1,0:T(8,128)(2,1)} %x_ref.3), custom_call_target="tpu_custom_call" | custom-call | flops 4294967296 | bytes 41943040 | tf_op jit(solution)/shard_map/build/pallas_call | solution.py:111
  34.6 6.5 %all-to-all-done = bf16[32,32,512]{2,1,0:T(8,128)(2,1)S(1)} async-done(((bf16[32,32,512]{2,1,0:T(8,128)(2,1)}), bf16[32,32,512]{2,1,0:T(8,128)(2,1)S(1)}, u32[]{:S(2)}, u32[]{:S(2)}) %all-to-all-start) | async-done | bytes 1048608 | tf_op jit(solution)/shard_map/all_to_all | solution.py:245
  41.2 0.0 copy-start.1
  41.2 1.0 copy-done.1
  42.1 17.8 %layer.1 = (bf16[2048,512]{1,0:T(8,128)(2,1)}, bf16[2048,512]{1,0:T(8,128)(2,1)}, bf16[2048,512]{1,0:T(8,128)(2,1)}, bf16[512,2048]{1,0:T(8,128)(2,1)}, bf16[1024,512]{1,0:T(8,128)(2,1)}) custom-call(bf16[2048,3072]{1,0:T(8,128)(2,1)} %get-tuple-element.10.adj_ref, f32[2048,512]{1,0:T(8,128)} %get-tuple-element.11.own_ref, bf16[1024,512]{1,0:T(8,128)(2,1)} %bitcast.18, ...), custom_call_target="tpu_custom_call" | custom-call | tf_op jit(solution)/shard_map/layer/pallas_call | solution.py:173
  60.0 3.5 %convolution_convert_fusion = bf16[512,512]{1,0:T(8,128)(2,1)S(1)} fusion(bf16[2048,512]{1,0:T(8,128)(2,1)} %get-tuple-element.15, bf16[2048,512]{1,0:T(8,128)(2,1)} %get-tuple-element.16), kind=kOutput, calls=%fused_computation | convolution fusion | flops 1074003968 | bytes 4718592 | tf_op jit(solution)/shard_map/dot_general | solution.py:22
  63.5 13.2 %all_to_all.25 = bf16[8,64,512]{2,1,0:T(8,128)(2,1)S(1)} all-to-all(bf16[8,64,512]{2,1,0:T(8,128)(2,1)S(1)} %bitcast.20), channel_id=1, replica_groups=mesh['group'=4,'local'=8] {'local'}, dimensions={0} | all-to-all | bytes 1048576 | tf_op jit(solution)/shard_map/all_to_all | solution.py:245
  76.7 0.1 reduce_sum.24
  76.8 10.9 %all_to_all.26 = bf16[4,64,512]{2,1,0:T(8,128)(2,1)S(1)} all-to-all(bf16[4,64,512]{2,1,0:T(8,128)(2,1)S(1)} %broadcast_in_dim.21), channel_id=1, replica_groups=mesh['group'=4,'local'=8] {'group'}, dimensions={0} | all-to-all | bytes 524288 | tf_op jit(solution)/shard_map/all_to_all | solution.py:245
  87.7 0.0 copy-start.2
  87.7 0.0 copy-start.3
  87.8 12.2 %all_to_all.27 = bf16[8,64,512]{2,1,0:T(8,128)(2,1)S(1)} all-to-all(bf16[8,64,512]{2,1,0:T(8,128)(2,1)S(1)} %broadcast_in_dim.22), channel_id=1, replica_groups=mesh['group'=4,'local'=8] {'local'}, dimensions={0} | all-to-all | bytes 1048576 | tf_op jit(solution)/shard_map/all_to_all | solution.py:245
  100.0 2.6 %all-to-all-start.1 = ((bf16[32,32,512]{2,1,0:T(8,128)(2,1)}), bf16[32,32,512]{2,1,0:T(8,128)(2,1)S(1)}, u32[]{:S(2)}, u32[]{:S(2)}) async-start(bf16[32,32,512]{2,1,0:T(8,128)(2,1)} %bitcast.5), calls=%async_computation.1 | async-start | bytes 2097152 | tf_op jit(solution)/shard_map/all_to_all | solution.py:245
  102.6 0.0 copy-done.2
  102.6 0.1 squeeze.6
  102.7 0.0 copy-done.3
  102.7 0.1 copy.14
  102.8 0.1 lt.29
  102.9 0.6 broadcast_select_fusion.index_ref
  103.5 11.2 %spread.1.owned_ref = f32[2048,512]{1,0:T(8,128)} custom-call(bf16[2048,3072]{1,0:T(8,128)(2,1)} %get-tuple-element.10.adj_ref, bf16[512,2048]{1,0:T(8,128)(2,1)} %get-tuple-element.13.grad_ref), custom_call_target="tpu_custom_call" | custom-call | flops 4294967296 | bytes 16777216 | tf_op jit(solution)/shard_map/spread/pallas_call | solution.py:209
  114.7 1.1 bitcast_convert_fusion
  115.8 13.0 %all-to-all-done.1 = bf16[32,32,512]{2,1,0:T(8,128)(2,1)S(1)} async-done(((bf16[32,32,512]{2,1,0:T(8,128)(2,1)}), bf16[32,32,512]{2,1,0:T(8,128)(2,1)S(1)}, u32[]{:S(2)}, u32[]{:S(2)}) %all-to-all-start.1) | async-done | bytes 1048608 | tf_op jit(solution)/shard_map/all_to_all | solution.py:245
  128.8 0.0 copy-start
  128.8 1.0 copy-done
  129.8 8.0 %give_back.1 = bf16[2048,512]{1,0:T(8,128)(2,1)} custom-call(s32[1,1024]{1,0:T(1,128)} %broadcast_select_fusion.index_ref, f32[2048,512]{1,0:T(8,128)} %spread.1.owned_ref, bf16[1024,512]{1,0:T(8,128)(2,1)} %bitcast.17), custom_call_target="tpu_custom_call" | custom-call | tf_op jit(solution)/shard_map/give_back/pallas_call | solution.py:233
  (4 shorter events, 0.1 us)
Async XLA Ops:
  7.6 33.5 %all-to-all-start = ((bf16[32,32,512]{2,1,0:T(8,128)(2,1)}), bf16[32,32,512]{2,1,0:T(8,128)(2,1)S(1)}, u32[]{:S(2)}, u32[]{:S(2)}) async-start(bf16[32,32,512]{2,1,0:T(8,128)(2,1)} %bitcast.19), calls=%async_computation | async-start | bytes 2097152 | tf_op jit(solution)/shard_map/all_to_all | solution.py:245
  41.2 1.0 copy-start.1
  87.7 14.9 %copy-start.2 = (s32[1,32,32]{2,1,0:T(8,128)S(1)}, s32[1,32,32]{2,1,0:T(8,128)}, u32[]{:S(2)}) copy-start(s32[1,32,32]{2,1,0:T(8,128)} %param.14) | copy-start | bytes 12292
  87.7 15.0 %copy-start.3 = (s32[1,32]{1,0:T(1,128)S(1)}, s32[1,32]{1,0:T(1,128)}, u32[]{:S(2)}) copy-start(s32[1,32]{1,0:T(1,128)} %param.15) | copy-start | bytes 388
  100.0 28.9 %all-to-all-start.1 = ((bf16[32,32,512]{2,1,0:T(8,128)(2,1)}), bf16[32,32,512]{2,1,0:T(8,128)(2,1)S(1)}, u32[]{:S(2)}, u32[]{:S(2)}) async-start(bf16[32,32,512]{2,1,0:T(8,128)(2,1)} %bitcast.5), calls=%async_computation.1 | async-start | bytes 2097152 | tf_op jit(solution)/shard_map/all_to_all | solution.py:245
  128.8 1.0 copy-start
where the time goes:
time: 139 us; the launch traced here: 138 us
  Pallas kernels  61.7 us (44%)
  blocking collectives  36.3 us (26%)
  waiting for transfers between devices  19.5 us (14%)
  starting transfers between devices  9.94 us (7%)
  matrix products  3.49 us (3%)
  other arithmetic  3.14 us (2%)
  local copies, waits for them, and re-layouts  3.04 us (2%)
    all_to_all x3, blocking collectives, exchange(): return lax.all_to_all(x, axes, split_axis=0, concat_axis=0, tiled=True)  36.3 us
    pallas_call x1, Pallas kernels, build(): pl.pallas_call(build_kernel, grid_spec=pltpu.PrefetchScalarGridSpec(num_s...  19.7 us
    all_to_all x2, waiting for transfers between devices, exchange(): return lax.all_to_all(x, axes, split_axis=0, concat_axis=0, tiled=True)  19.5 us
    pallas_call x1, Pallas kernels, layer(): pl.pallas_call(layer_kernel, grid=(owned // ROWS,), in_specs=[pl.BlockSpe...  17.8 us
    pallas_call x1, Pallas kernels, spread(): pl.pallas_call(spread_kernel, grid=(owned // ROWS,), in_specs=[pl.BlockSp...  11.2 us
    all_to_all x2, starting transfers between devices, exchange(): return lax.all_to_all(x, axes, split_axis=0, concat_axis=0, tiled=True)  9.94 us
    pallas_call x1, Pallas kernels, give_back(): pl.pallas_call(return_kernel, grid=(rows // ROWS,), in_specs=[whole(index...  8.01 us
    pallas_call x1, Pallas kernels, collect(): pl.pallas_call(collect_kernel, out_shape=jax.ShapeDtypeStruct((dests * sl...  4.94 us
  transfers between devices with their start and end apart: 2, of which 2 were waited for; matrix products, arithmetic and copies ran while one was open for 1% of the time, Pallas kernels for 22%

commit v1 on v0

v1 whole, which is shorter than its diff:
```python
import functools

import jax
import jax.numpy as jnp
from jax import lax
from jax.experimental import pallas as pl
from jax.experimental.pallas import tpu as pltpu
from jax.sharding import PartitionSpec as P

AXES = ("group", "local")
BF16 = jnp.bfloat16
F32 = jnp.float32
ROWS = 256
BIG = 512
MIB = 1024 * 1024


def params(mib):
    return pltpu.CompilerParams(vmem_limit_bytes=mib * MIB)


VMEM = pl.BlockSpec(memory_space=pltpu.VMEM)
SMEM = pl.BlockSpec(memory_space=pltpu.SMEM)
HBM = pl.BlockSpec(memory_space=pl.ANY)


def made(keep, shape, dtype):
    return pltpu.VMEM(shape, dtype) if keep else jax.ShapeDtypeStruct(shape, dtype)


def held(keep, *arrays):
    if not keep:
        return arrays
    return [pltpu.with_memory_space_constraint(x, pltpu.VMEM) for x in arrays]


def dot(a, b, contract=((1,), (0,))):
    return lax.dot_general(a, b, (contract, ((), ())), preferred_element_type=F32)


def whole(shape):
    return pl.BlockSpec(shape, lambda i, *unused: (0,) * len(shape))


def collect_kernel(counts_ref, lists_ref, x_ref, out_ref):
    dests, slots = lists_ref.shape
    step = BIG // slots
    lane = lax.broadcasted_iota(jnp.int32, (slots, x_ref.shape[0]), 1)
    slot = lax.broadcasted_iota(jnp.int32, (slots, 1), 0)
    turned = lists_ref[...].T
    for first in range(0, dests, step):
        parts = []
        for d in range(first, first + step):
            named = jnp.where(slot < counts_ref[0, d], turned[:, d : d + 1], -1)
            parts.append(jnp.where(named == lane, 1.0, 0.0).astype(BF16))
        pick = jnp.concatenate(parts, axis=0)
        out_ref[first * slots : (first + step) * slots, :] = dot(pick, x_ref[...]).astype(BF16)


def collect(counts, lists, x):
    dests, slots = lists.shape
    return pl.pallas_call(
        collect_kernel,
        in_specs=[SMEM, VMEM, VMEM],
        out_shape=jax.ShapeDtypeStruct((dests * slots, x.shape[1]), BF16),
        compiler_params=params(60),
        name="collect",
    )(counts, lists, x)


def build_kernel(rows_ref, cols_ref, tiles_ref, x_ref, adj_ref, far_ref, own_ref, total, order, starts, cursor):
    num_tiles, edge = tiles_ref.shape[0], tiles_ref.shape[1]
    per = ROWS // edge
    blocks = pl.num_programs(0)
    i = pl.program_id(0)

    @pl.when(i == 0)
    def _():
        def clear(b, unused):
            starts[b] = 0
            return unused

        lax.fori_loop(0, blocks + 1, clear, 0)

        def count(t, unused):
            k = rows_ref[t] // per + 1
            starts[k] = starts[k] + 1
            return unused

        lax.fori_loop(0, num_tiles, count, 0, unroll=4)

        def add(b, running):
            running = running + starts[b]
            starts[b] = running
            cursor[b] = running
            return running

        lax.fori_loop(0, blocks + 1, add, 0)

        def place(t, unused):
            k = rows_ref[t] // per
            at = cursor[k]
            cursor[k] = at + 1
            order[at] = t
            return unused

        lax.fori_loop(0, num_tiles, place, 0, unroll=4)

    total[...] = jnp.zeros_like(total)

    def one(j, unused):
        t = order[j]
        r = pl.multiple_of((rows_ref[t] % per) * edge, edge)
        c = pl.multiple_of(cols_ref[t] * edge, edge)
        at = (pl.ds(r, edge), pl.ds(c, edge))
        total[at] = total[at] + tiles_ref[t].astype(F32)
        return unused

    lax.fori_loop(starts[i], starts[i + 1], one, 0)
    owned = x_ref.shape[0]
    adj_ref[...] = total[:, :owned].astype(BF16)
    own_ref[...] = dot(adj_ref[...], x_ref[...])
    far_ref[...] = total[:, owned:].astype(BF16)


def build(tile_rows, tile_cols, tile_vals, x, remote):
    owned, width = x.shape
    num_tiles = tile_vals.shape[0]
    blocks = owned // ROWS
    return pl.pallas_call(
        build_kernel,
        grid_spec=pltpu.PrefetchScalarGridSpec(
            num_scalar_prefetch=2,
            grid=(blocks,),
            in_specs=[whole(tile_vals.shape), whole(x.shape)],
            out_specs=[
                pl.BlockSpec((ROWS, owned), lambda i, *unused: (i, 0)),
                pl.BlockSpec((ROWS, remote), lambda i, *unused: (i, 0)),
                pl.BlockSpec((ROWS, width), lambda i, *unused: (i, 0)),
            ],
            scratch_shapes=[
                pltpu.VMEM((ROWS, owned + remote), F32),
                pltpu.SMEM((num_tiles,), jnp.int32),
                pltpu.SMEM((blocks + 1,), jnp.int32),
                pltpu.SMEM((blocks + 1,), jnp.int32),
            ],
        ),
        out_shape=[
            jax.ShapeDtypeStruct((owned, owned), BF16),
            jax.ShapeDtypeStruct((owned, remote), BF16),
            jax.ShapeDtypeStruct((owned, width), F32),
        ],
        compiler_params=params(48),
        cost_estimate=pl.CostEstimate(
            flops=2 * owned * owned * width, bytes_accessed=40 * 1024 * 1024, transcendentals=0
        ),
        name="build",
    )(tile_rows, tile_cols, tile_vals, x)


def layer_kernel(
    me_ref, far_hbm, own_hbm, cot_hbm, w_ref, got_ref,
    act_hbm, far_ref, slope_ref, mine_ref, other_ref,
    own, cot, hid, act, sems, sent,
):
    blocks = sems.shape[1]
    views = [pl.ds(n * BIG, BIG) for n in range(blocks)]

    def fetch(n):
        pairs = ((far_hbm, far_ref), (own_hbm, own), (cot_hbm, cot))
        copies = [pltpu.make_async_copy(a.at[views[n]], b.at[views[n]], sems.at[k, n]) for k, (a, b) in enumerate(pairs)]
        for copy in copies:
            copy.start()
        return copies

    coming = fetch(0)
    sending = []
    for n, at in enumerate(views):
        copies = coming
        for copy in copies[:2]:
            copy.wait()
        if n + 1 < blocks:
            coming = fetch(n + 1)
        hidden = (own[at, :] + dot(far_ref[at, :], got_ref[...])).astype(BF16)
        hid[at, :] = hidden
        preact = dot(hidden, w_ref[...])
        copies[2].wait()
        gate = 0.5 + 0.5 * jnp.tanh(0.5 * preact)
        act[at, :] = (preact * gate).astype(BF16)
        sending.append(pltpu.make_async_copy(act.at[at], act_hbm.at[at], sent.at[n]))
        sending[n].start()
        slope = cot[at, :].astype(F32) * gate * (1.0 + preact * (1.0 - gate))
        slope_ref[at, :] = slope.astype(BF16)
    half = mine_ref.shape[0]
    core = me_ref[0] % 2
    for out_ref, first in ((other_ref, (1 - core) * half), (mine_ref, core * half)):
        columns = hid[:, pl.ds(pl.multiple_of(first, half), half)]
        out_ref[...] = dot(columns, slope_ref[...], ((0,), (0,))).astype(out_ref.dtype)
    for copy in sending:
        copy.wait()


def layer(keep, me, far, own, got, cotangent, weight):
    owned, width = own.shape
    half = (width // 2, width)
    blocks = owned // BIG
    weight, got = held(keep, weight, got)
    return pl.pallas_call(
        layer_kernel,
        in_specs=[SMEM, HBM, HBM, HBM, VMEM, VMEM],
        out_specs=[HBM, VMEM, VMEM, VMEM, VMEM],
        out_shape=[
            jax.ShapeDtypeStruct((owned, width), BF16),
            made(keep, far.shape, BF16),
            made(keep, (owned, width), BF16),
            made(keep, half, F32),
            made(keep, half, BF16),
        ],
        scratch_shapes=[
            pltpu.VMEM((owned, width), F32),
            pltpu.VMEM((owned, width), BF16),
            pltpu.VMEM((owned, width), BF16),
            pltpu.VMEM((owned, width), BF16),
            pltpu.SemaphoreType.DMA((3, blocks)),
            pltpu.SemaphoreType.DMA((blocks,)),
        ],
        compiler_params=params(28 if keep else 60),
        name="layer",
    )(me, far, own, cotangent, weight, got)


def grad_kernel(slope_ref, w_ref, grad_ref, grad_hbm, sems):
    copies = []
    for n in range(sems.shape[0]):
        at = pl.ds(n * BIG, BIG)
        grad_ref[at, :] = dot(slope_ref[at, :], w_ref[...], ((1,), (1,))).astype(BF16)
        copies.append(pltpu.make_async_copy(grad_ref.at[at], grad_hbm.at[at], sems.at[n]))
        copies[n].start()
    for copy in copies:
        copy.wait()


def hidden_grad(keep, slope, weight):
    return pl.pallas_call(
        grad_kernel,
        in_specs=[VMEM] * 2,
        out_specs=[VMEM, HBM],
        out_shape=[made(keep, slope.shape, BF16), jax.ShapeDtypeStruct(slope.shape, BF16)],
        scratch_shapes=[pltpu.SemaphoreType.DMA((slope.shape[0] // BIG,))],
        compiler_params=params(12 if keep else 40),
        name="hidden_grad",
    )(*held(keep, slope, weight))


def back_kernel(far_ref, grad_ref, after_ref, out_hbm, out, sems):
    copies = []
    for n in range(sems.shape[0]):
        at = pl.ds(n * BIG, BIG)
        out[at, :] = dot(far_ref[:, at], grad_ref[...], ((0,), (0,))).astype(BF16)
        copies.append(pltpu.make_async_copy(out.at[at], out_hbm.at[at], sems.at[n]))
        copies[n].start()
    for copy in copies:
        copy.wait()


def back_rows(keep, far, grad, after):
    shape = (far.shape[1], grad.shape[1])
    return pl.pallas_call(
        back_kernel,
        in_specs=[VMEM, VMEM, HBM],
        out_specs=HBM,
        out_shape=jax.ShapeDtypeStruct(shape, BF16),
        scratch_shapes=[pltpu.VMEM(shape, BF16), pltpu.SemaphoreType.DMA((shape[0] // BIG,))],
        compiler_params=params(16 if keep else 60),
        name="back_rows",
    )(*held(keep, far, grad), after)


def spread_kernel(adj_ref, grad_ref, out_ref):
    out_ref[...] = dot(adj_ref[...], grad_ref[...], ((0,), (0,)))


def spread(adjacency, grad):
    owned, width = grad.shape
    return pl.pallas_call(
        spread_kernel,
        grid=(owned // BIG,),
        in_specs=[pl.BlockSpec((owned, BIG), lambda i: (0, i)), whole(grad.shape)],
        out_specs=pl.BlockSpec((BIG, width), lambda i: (i, 0)),
        out_shape=jax.ShapeDtypeStruct((owned, width), F32),
        compiler_params=params(60),
        cost_estimate=pl.CostEstimate(
            flops=2 * owned * owned * width, bytes_accessed=16 * 1024 * 1024, transcendentals=0
        ),
        name="spread",
    )(adjacency, grad)


def return_kernel(index_ref, owned_hbm, got_ref, out_hbm, owned, out, sems, sent):
    blocks = sems.shape[0]
    views = [pl.ds(n * BIG, BIG) for n in range(blocks)]
    coming = [pltpu.make_async_copy(owned_hbm.at[at], owned.at[at], sems.at[n]) for n, at in enumerate(views)]
    for copy in coming:
        copy.start()

    def pick(n):
        row = lax.broadcasted_iota(jnp.int32, (BIG, index_ref.shape[1]), 0) + n * BIG
        return jnp.where(row == index_ref[...], 1.0, 0.0).astype(BF16)

    sending = []
    for n, at in enumerate(views):
        added = dot(pick(n), got_ref[...])
        coming[n].wait()
        out[at, :] = (owned[at, :] + added).astype(BF16)
        sending.append(pltpu.make_async_copy(out.at[at], out_hbm.at[at], sent.at[n]))
        sending[n].start()
    for copy in sending:
        copy.wait()


def give_back(keep, index, owned, got):
    rows, width = owned.shape
    (got,) = held(keep, got)
    return pl.pallas_call(
        return_kernel,
        in_specs=[VMEM, HBM, VMEM],
        out_specs=HBM,
        out_shape=jax.ShapeDtypeStruct((rows, width), BF16),
        scratch_shapes=[
            pltpu.VMEM((rows, width), F32),
            pltpu.VMEM((rows, width), BF16),
            pltpu.SemaphoreType.DMA((rows // BIG,)),
            pltpu.SemaphoreType.DMA((rows // BIG,)),
        ],
        compiler_params=params(28 if keep else 60),
        name="give_back",
    )(index, owned, got)


def exchange(x, axes):
    return lax.all_to_all(x, axes, split_axis=0, concat_axis=0, tiled=True)


def cut_kernel(me_ref, mine_ref, got_ref, *out_refs):
    height = mine_ref.shape[0] // len(out_refs)
    for k, out_ref in enumerate(out_refs):
        at = pl.ds(pl.multiple_of(((me_ref[0] // 2) ^ k) * height, height), height)
        out_ref[...] = (mine_ref[at, :] + got_ref[at, :].astype(F32)).astype(out_ref.dtype)


def cut(me, mine, got, chips):
    height, width = got.shape[0] // chips, got.shape[1]
    return pl.pallas_call(
        cut_kernel,
        in_specs=[SMEM, VMEM, VMEM],
        out_shape=[jax.ShapeDtypeStruct((height, width), F32 if k == 0 else BF16) for k in range(chips)],
        compiler_params=params(8),
        name="cut",
    )(me, mine, got)


def join_kernel(me_ref, *refs):
    in_refs, out_ref = refs[:-1], refs[-1]
    height, half = in_refs[0].shape[0], out_ref.shape[0] // 2
    for k, in_ref in enumerate(in_refs):
        owner = me_ref[0] ^ k
        at = pl.multiple_of((owner % 2) * half + (owner // 2) * height, height)
        out_ref[pl.ds(at, height), :] = in_ref[...].astype(F32)


def join(me, parts):
    height, width = parts[0].shape
    return pl.pallas_call(
        join_kernel,
        in_specs=[SMEM] + [VMEM] * len(parts),
        out_shape=jax.ShapeDtypeStruct((height * len(parts), width), F32),
        compiler_params=params(8),
        name="join",
    )(me, *parts)


def add_kernel(after_ref, *refs):
    parts = [ref[...].astype(F32) for ref in refs[:-1]]
    while len(parts) > 1:
        parts = [parts[k] + parts[k + 1] for k in range(0, len(parts), 2)]
    refs[-1][...] = parts[0].astype(BF16)


def add(after, parts):
    return pl.pallas_call(
        add_kernel,
        in_specs=[HBM] + [VMEM] * len(parts),
        out_shape=jax.ShapeDtypeStruct(parts[0].shape, BF16),
        compiler_params=params(8),
        name="add",
    )(after, *parts)


def swap(x, axis, size, k):
    return lax.ppermute(x, axis, [(i, i ^ k) for i in range(size)])


def per_device(groups, locals_, features, weight, cotangent, tile_vals, tile_rows, tile_cols, send_rows, counts):
    rows_own, width = features.shape
    lists = send_rows[0]
    peers, slots = lists.shape
    remote = peers * slots
    keep = remote <= rows_own
    me = lax.axis_index("local").astype(jnp.int32).reshape(1)
    outgoing = collect(counts, lists, features)
    arrived = exchange(outgoing.reshape(peers, slots, width), AXES).reshape(remote, width)
    adjacency, far, own = build(tile_rows, tile_cols, tile_vals, features, remote)
    activated, far, slope, mine, other = layer(keep, me, far, own, arrived, cotangent, weight)
    chips = locals_ // 2
    pieces = cut(me, mine, swap(other, "local", locals_, 1), chips)
    grad, grad_out = hidden_grad(keep, slope, weight)
    back = back_rows(keep, far, grad, pieces[-1])
    returned = exchange(back.reshape(peers, slots, width), AXES).reshape(remote, width)
    owned = spread(adjacency, grad_out)
    piece = add(owned, [pieces[0]] + [swap(pieces[k], "local", locals_, 2 * k) for k in range(1, chips)])
    piece = add(me, [piece] + [swap(piece, "group", groups, k) for k in range(1, groups)])
    weight_grad = join(me, [piece] + [swap(piece, "local", locals_, k) for k in range(1, locals_)])
    live = jnp.arange(slots)[None, :] < counts[0][:, None]
    feature_grad = give_back(keep, jnp.where(live, lists, -1).reshape(1, remote), owned, returned)
    return activated, feature_grad, weight_grad


def solution(mesh):
    return jax.shard_map(
        functools.partial(per_device, mesh.shape["group"], mesh.shape["local"]),
        mesh=mesh,
        in_specs=(
            P(AXES, None),
            P(),
            P(AXES, None),
            P(AXES, None, None),
            P(AXES),
            P(AXES),
            P(AXES, None, None),
            P(AXES, None),
        ),
        out_specs=(P(AXES, None), P(AXES, None), P()),
        check_vma=False,
    )
```

time: 139 us -> 113 us (0.81)
  blocking collectives: 36.3 us -> 0 us
  starting transfers between devices: 9.94 us -> 25.9 us
  local copies, waits for them, and re-layouts: 3.04 us -> 13.4 us
  Pallas kernels: 61.7 us -> 52.1 us
  matrix products: 3.49 us -> 0 us
  other arithmetic: 3.14 us -> 0.08 us
    all_to_all x3 -> x0, blocking collectives: 36.3 us -> none  [exchange(): return lax.all_to_all(x, axes, split_axis=0, concat_axis=0, tiled=True)]
    ppermute x0 -> x14, waiting for transfers between devices: none -> 15.2 us  [swap(): return lax.ppermute(x, axis, [(i, i ^ k) for i in range(size)])]
    ppermute x0 -> x14, starting transfers between devices: none -> 14.7 us  [swap(): return lax.ppermute(x, axis, [(i, i ^ k) for i in range(size)])]
    all_to_all x2, waiting for transfers between devices: 19.5 us -> 5.05 us  [exchange(): return lax.all_to_all(x, axes, split_axis=0, concat_axis=0, tiled=True)]
    unnamed x9 -> x24, local copies, waits for them, and re-layouts: 2.73 us -> 13.3 us
    pallas_call x4 -> x10, Pallas kernels: 42 us -> 32.6 us  [the longest x1 9.21 us: spread(): pl.pallas_call(spread_kernel, grid=(owned // BIG,), in_specs=[pl.BlockSpe...]
    dot_general x1 -> x0, matrix products: 3.49 us -> none  [dot(): lax.dot_general(a, b, (contract, ((), ())), preferred_element_type=F32)]
  transfers between devices with their start and end apart: 2 -> 16, of which waited for: 2 -> 8; matrix products, arithmetic and copies ran while one was open for 1% -> 0% of each run, Pallas kernels for 22% -> 28%
where the time goes in v1:
time: 113 us
  Pallas kernels  52.1 us (46%)
  starting transfers between devices  25.9 us (23%)
  waiting for transfers between devices  20.2 us (18%)
  local copies, waits for them, and re-layouts  13.4 us (12%)
    pallas_call x1, Pallas kernels, build(): pl.pallas_call(build_kernel, grid_spec=pltpu.PrefetchScalarGridSpec(num_s...  19.6 us
    ppermute x14, waiting for transfers between devices, swap(): return lax.ppermute(x, axis, [(i, i ^ k) for i in range(size)])  15.2 us
    ppermute x14, starting transfers between devices, swap(): return lax.ppermute(x, axis, [(i, i ^ k) for i in range(size)])  14.7 us
    unnamed x24, local copies, waits for them, and re-layouts  13.3 us
    all_to_all x2, starting transfers between devices, exchange(): return lax.all_to_all(x, axes, split_axis=0, concat_axis=0, tiled=True)  11.2 us
    pallas_call x1, Pallas kernels, spread(): pl.pallas_call(spread_kernel, grid=(owned // BIG,), in_specs=[pl.BlockSpe...  9.21 us
    pallas_call x1, Pallas kernels, layer(): pl.pallas_call(layer_kernel, in_specs=[SMEM, HBM, HBM, HBM, VMEM, VMEM],...  7.65 us
    all_to_all x2, waiting for transfers between devices, exchange(): return lax.all_to_all(x, axes, split_axis=0, concat_axis=0, tiled=True)  5.05 us
  transfers between devices with their start and end apart: 16, of which 8 were waited for; matrix products, arithmetic and copies ran while one was open for 0% of the time, Pallas kernels for 28%

profile of v1, /device:TPU:0, one launch (start us, length us, event | category | flops | bytes accessed | tf_op | source)
XLA Modules:
  0.0 112.7 jit_solution(14917322958066524993)
XLA Ops:
  0.7 5.0 %collect.1 = bf16[1024,512]{1,0:T(8,128)(2,1)} custom-call(s32[1,32]{1,0:T(1,128)} %counts_ref.1, s32[32,32]{1,0:T(8,128)} %bitcast.10, bf16[2048,512]{1,0:T(8,128)(2,1)} %x_ref.3), custom_call_target="tpu_custom_call" | custom-call | tf_op jit(solution)/shard_map/collect/pallas_call | solution.py:62
  5.7 7.3 %all-to-all-start = ((bf16[32,32,512]{2,1,0:T(8,128)(2,1)}), bf16[32,32,512]{2,1,0:T(8,128)(2,1)S(1)}, u32[]{:S(2)}, u32[]{:S(2)}) async-start(bf16[32,32,512]{2,1,0:T(8,128)(2,1)} %bitcast.9), calls=%async_computation | async-start | bytes 2097152 | tf_op jit(solution)/shard_map/all_to_all | solution.py:341
  13.0 1.6 %copy-done.5 = bf16[2048,512]{1,0:T(8,128)(2,1)S(1)} copy-done((bf16[2048,512]{1,0:T(8,128)(2,1)S(1)}, bf16[2048,512]{1,0:T(8,128)(2,1)}, u32[]{:S(2)}) %copy-start.5) | copy-done | bytes 2097176
  14.6 19.6 %build.1 = (bf16[2048,2048]{1,0:T(8,128)(2,1)}, bf16[2048,1024]{1,0:T(8,128)(2,1)}, f32[2048,512]{1,0:T(8,128)}) custom-call(s32[256]{0:T(256)S(1)} %copy-done.8, s32[256]{0:T(256)S(1)} %copy-done.9, bf16[256,128,128]{2,1,0:T(8,128)(2,1)} %tiles_ref.1, bf16[2048,512]{1,0:T(8,128)(2,1)S(1)} %copy-done.5), custom_call_target="tpu_custom_call" | custom-call | flops 4294967296 | bytes 41943040 | tf_op jit(solution)/shard_map/build/pallas_call | solution.py:130
  34.2 5.0 %all-to-all-done = bf16[32,32,512]{2,1,0:T(8,128)(2,1)S(1)} async-done(((bf16[32,32,512]{2,1,0:T(8,128)(2,1)}), bf16[32,32,512]{2,1,0:T(8,128)(2,1)S(1)}, u32[]{:S(2)}, u32[]{:S(2)}) %all-to-all-start) | async-done | bytes 1048608 | tf_op jit(solution)/shard_map/all_to_all | solution.py:341
  39.2 2.2 %copy-done.2 = bf16[2048,1024]{1,0:T(8,128)(2,1)S(1)} copy-done((bf16[2048,1024]{1,0:T(8,128)(2,1)S(1)}, bf16[2048,1024]{1,0:T(8,128)(2,1)}, u32[]{:S(2)}) %copy-start.2) | copy-done | bytes 4194328
  41.4 2.2 %copy-done.3 = f32[2048,512]{1,0:T(8,128)S(1)} copy-done((f32[2048,512]{1,0:T(8,128)S(1)}, f32[2048,512]{1,0:T(8,128)}, u32[]{:S(2)}) %copy-start.3) | copy-done | bytes 4194328
  43.6 1.6 %copy-done.6 = bf16[2048,512]{1,0:T(8,128)(2,1)S(1)} copy-done((bf16[2048,512]{1,0:T(8,128)(2,1)S(1)}, bf16[2048,512]{1,0:T(8,128)(2,1)}, u32[]{:S(2)}) %copy-start.6) | copy-done | bytes 2097176
  45.2 7.6 %layer.1 = (bf16[2048,512]{1,0:T(8,128)(2,1)}, bf16[2048,1024]{1,0:T(8,128)(2,1)S(1)}, bf16[2048,512]{1,0:T(8,128)(2,1)S(1)}, f32[256,512]{1,0:T(8,128)S(1)}, bf16[256,512]{1,0:T(8,128)(2,1)S(1)}) custom-call(s32[1]{0:T(128)} %bitcast.me_ref.after_ref, bf16[2048,1024]{1,0:T(8,128)(2,1)S(1)} %copy-done.2, f32[2048,512]{1,0:T(8,128)S(1)} %copy-done.3, ...), custom_call_target="tpu_custom_call" | custom-call | tf_op jit(solution)/shard_map/layer/pallas_call | solution.py:208
  52.9 2.1 %hidden_grad.1 = (bf16[2048,512]{1,0:T(8,128)(2,1)S(1)}, bf16[2048,512]{1,0:T(8,128)(2,1)S(1)}) custom-call(bf16[2048,512]{1,0:T(8,128)(2,1)S(1)} %get-tuple-element.21.slope_ref, bf16[512,512]{1,0:T(8,128)(2,1)S(1)} %copy-done.4), custom_call_target="tpu_custom_call" | custom-call | tf_op jit(solution)/shard_map/hidden_grad/pallas_call | solution.py:244
  55.0 1.3 %copy-done.7 = bf16[2048,512]{1,0:T(8,128)(2,1)} copy-done((bf16[2048,512]{1,0:T(8,128)(2,1)}, bf16[2048,512]{1,0:T(8,128)(2,1)S(1)}, u32[]{:S(2)}) %copy-start.7) | copy-done | bytes 2097176
  56.4 3.2 %back_rows.1 = bf16[1024,512]{1,0:T(8,128)(2,1)} custom-call(bf16[2048,1024]{1,0:T(8,128)(2,1)S(1)} %get-tuple-element.23.far_ref, bf16[2048,512]{1,0:T(8,128)(2,1)S(1)} %get-tuple-element.24.grad_ref, bf16[64,512]{1,0:T(8,128)(2,1)S(1)} %get-tuple-element.27.after_ref), custom_call_target="tpu_custom_call" | custom-call | tf_op jit(solution)/shard_map/back_rows/pallas_call | solution.py:268
  59.6 3.9 %all-to-all-start.1 = ((bf16[32,32,512]{2,1,0:T(8,128)(2,1)}), bf16[32,32,512]{2,1,0:T(8,128)(2,1)S(1)}, u32[]{:S(2)}, u32[]{:S(2)}) async-start(bf16[32,32,512]{2,1,0:T(8,128)(2,1)} %bitcast.5), calls=%async_computation.1 | async-start | bytes 2097152 | tf_op jit(solution)/shard_map/all_to_all | solution.py:341
  63.5 2.6 %collective-permute-start.3 = (bf16[64,512]{1,0:T(8,128)(2,1)S(1)}, bf16[64,512]{1,0:T(8,128)(2,1)S(1)}, u32[]{:S(2)}, u32[]{:S(2)}) collective-permute-start(bf16[64,512]{1,0:T(8,128)(2,1)S(1)} %get-tuple-element.27.after_ref), channel_id=1, source_target_pairs={{0,6},{1,7},{2,4},{3,5},{4,2},{5,3},{6,0},{7,1},{8,14},{9,15},{10,... | collective-permute-start | bytes 196616 | tf_op jit(solution)/shard_map/ppermute | solution.py:400
  66.0 0.6 collective-permute-start.1
  67.0 9.2 %spread.1.owned_hbm.after_ref = f32[2048,512]{1,0:T(8,128)} custom-call(bf16[2048,2048]{1,0:T(8,128)(2,1)} %get-tuple-element.20.adj_ref, bf16[2048,512]{1,0:T(8,128)(2,1)} %copy-done.7), custom_call_target="tpu_custom_call" | custom-call | flops 4294967296 | bytes 16777216 | tf_op jit(solution)/shard_map/spread/pallas_call | solution.py:285
  76.2 0.6 collective-permute-done.1.refs_1_
  76.8 2.2 %copy-done = f32[2048,512]{1,0:T(8,128)S(1)} copy-done((f32[2048,512]{1,0:T(8,128)S(1)}, f32[2048,512]{1,0:T(8,128)}, u32[]{:S(2)}) %copy-start) | copy-done | bytes 4194328
  79.0 1.1 collective-permute-start.4
  80.2 3.4 %collective-permute-start.5 = (bf16[64,512]{1,0:T(8,128)(2,1)S(1)}, bf16[64,512]{1,0:T(8,128)(2,1)S(1)}, u32[]{:S(2)}, u32[]{:S(2)}) collective-permute-start(bf16[64,512]{1,0:T(8,128)(2,1)S(1)} %add.2.refs_0_), channel_id=1, source_target_pairs={{0,16},{8,24},{16,0},{24,8},{1,17},{9,25},{17,1},{25,9},{2,18},{10... | collective-permute-start | bytes 196616 | tf_op jit(solution)/shard_map/ppermute | solution.py:400
  83.6 1.0 collective-permute-done.4.refs_1_
  84.6 9.6 %collective-permute-done.5.refs_2_ = bf16[64,512]{1,0:T(8,128)(2,1)S(1)} collective-permute-done((bf16[64,512]{1,0:T(8,128)(2,1)S(1)}, bf16[64,512]{1,0:T(8,128)(2,1)S(1)}, u32[]{:S(2)}, u32[]{:S(2)}) %collective-permute-start.5) | collective-permute-done | bytes 65568 | tf_op jit(solution)/shard_map/ppermute | solution.py:400
  94.3 1.5 %collective-permute-start.10 = (bf16[64,512]{1,0:T(8,128)(2,1)S(1)}, bf16[64,512]{1,0:T(8,128)(2,1)S(1)}, u32[]{:S(2)}, u32[]{:S(2)}) collective-permute-start(bf16[64,512]{1,0:T(8,128)(2,1)S(1)} %add.3.refs_0_), channel_id=1, source_target_pairs={{0,4},{1,5},{2,6},{3,7},{4,0},{5,1},{6,2},{7,3},{8,12},{9,13},{10,... | collective-permute-start | bytes 196616 | tf_op jit(solution)/shard_map/ppermute | solution.py:400
  96.1 1.5 %collective-permute-start.12 = (bf16[64,512]{1,0:T(8,128)(2,1)S(1)}, bf16[64,512]{1,0:T(8,128)(2,1)S(1)}, u32[]{:S(2)}, u32[]{:S(2)}) collective-permute-start(bf16[64,512]{1,0:T(8,128)(2,1)S(1)} %add.3.refs_0_), channel_id=1, source_target_pairs={{0,6},{1,7},{2,4},{3,5},{4,2},{5,3},{6,0},{7,1},{8,14},{9,15},{10,... | collective-permute-start | bytes 196616 | tf_op jit(solution)/shard_map/ppermute | solution.py:400
  97.5 1.5 %collective-permute-start.13 = (bf16[64,512]{1,0:T(8,128)(2,1)S(1)}, bf16[64,512]{1,0:T(8,128)(2,1)S(1)}, u32[]{:S(2)}, u32[]{:S(2)}) collective-permute-start(bf16[64,512]{1,0:T(8,128)(2,1)S(1)} %add.3.refs_0_), channel_id=1, source_target_pairs={{0,7},{1,6},{2,5},{3,4},{4,3},{5,2},{6,1},{7,0},{8,15},{9,14},{10,... | collective-permute-start | bytes 196616 | tf_op jit(solution)/shard_map/ppermute | solution.py:400
  99.1 1.5 %collective-permute-start.8 = (bf16[64,512]{1,0:T(8,128)(2,1)S(1)}, bf16[64,512]{1,0:T(8,128)(2,1)S(1)}, u32[]{:S(2)}, u32[]{:S(2)}) collective-permute-start(bf16[64,512]{1,0:T(8,128)(2,1)S(1)} %add.3.refs_0_), channel_id=1, source_target_pairs={{0,2},{1,3},{2,0},{3,1},{4,6},{5,7},{6,4},{7,5},{8,10},{9,11},{10,... | collective-permute-start | bytes 196616 | tf_op jit(solution)/shard_map/ppermute | solution.py:400
  101.0 0.8 collective-permute-done.12.refs_6_
  101.9 0.5 collective-permute-done.13.refs_7_
  102.3 2.4 %collective-permute-done.8.refs_2_ = bf16[64,512]{1,0:T(8,128)(2,1)S(1)} collective-permute-done((bf16[64,512]{1,0:T(8,128)(2,1)S(1)}, bf16[64,512]{1,0:T(8,128)(2,1)S(1)}, u32[]{:S(2)}, u32[]{:S(2)}) %collective-permute-start.8) | collective-permute-done | bytes 65568 | tf_op jit(solution)/shard_map/ppermute | solution.py:400
  105.0 1.0 join.1
  106.1 2.2 %copy-done.1 = f32[2048,512]{1,0:T(8,128)S(1)} copy-done((f32[2048,512]{1,0:T(8,128)S(1)}, f32[2048,512]{1,0:T(8,128)}, u32[]{:S(2)}) %copy-start.1) | copy-done | bytes 4194328
  108.3 4.3 %give_back.1 = bf16[2048,512]{1,0:T(8,128)(2,1)} custom-call(s32[1,1024]{1,0:T(1,128)S(1)} %broadcast_select_fusion.index_ref, f32[2048,512]{1,0:T(8,128)S(1)} %copy-done.1, bf16[1024,512]{1,0:T(8,128)(2,1)S(1)} %bitcast.7), custom_call_target="tpu_custom_call" | custom-call | tf_op jit(solution)/shard_map/give_back/pallas_call | solution.py:324
  (39 shorter events, 1.7 us)
Async XLA Ops:
  0.6 12.4 %copy-start.8 = (s32[256]{0:T(256)S(1)}, s32[256]{0:T(256)}, u32[]{:S(2)}) copy-start(s32[256]{0:T(256)} %rows_ref.1) | copy-start | bytes 3076
  0.6 12.4 %copy-start.9 = (s32[256]{0:T(256)S(1)}, s32[256]{0:T(256)}, u32[]{:S(2)}) copy-start(s32[256]{0:T(256)} %cols_ref.1) | copy-start | bytes 3076
  5.7 33.5 %all-to-all-start = ((bf16[32,32,512]{2,1,0:T(8,128)(2,1)}), bf16[32,32,512]{2,1,0:T(8,128)(2,1)S(1)}, u32[]{:S(2)}, u32[]{:S(2)}) async-start(bf16[32,32,512]{2,1,0:T(8,128)(2,1)} %bitcast.9), calls=%async_computation | async-start | bytes 2097152 | tf_op jit(solution)/shard_map/all_to_all | solution.py:341
  13.0 1.6 %copy-start.5 = (bf16[2048,512]{1,0:T(8,128)(2,1)S(1)}, bf16[2048,512]{1,0:T(8,128)(2,1)}, u32[]{:S(2)}) copy-start(bf16[2048,512]{1,0:T(8,128)(2,1)} %x_ref.3) | copy-start | bytes 6291460
  14.6 24.6 %copy-start.4 = (bf16[512,512]{1,0:T(8,128)(2,1)S(1)}, bf16[512,512]{1,0:T(8,128)(2,1)}, u32[]{:S(2)}) copy-start(bf16[512,512]{1,0:T(8,128)(2,1)} %w_ref.3) | copy-start | bytes 1572868
  39.2 2.2 %copy-start.2 = (bf16[2048,1024]{1,0:T(8,128)(2,1)S(1)}, bf16[2048,1024]{1,0:T(8,128)(2,1)}, u32[]{:S(2)}) copy-start(bf16[2048,1024]{1,0:T(8,128)(2,1)} %get-tuple-element.17.far_hbm) | copy-start | bytes 12582916
  41.4 2.2 %copy-start.3 = (f32[2048,512]{1,0:T(8,128)S(1)}, f32[2048,512]{1,0:T(8,128)}, u32[]{:S(2)}) copy-start(f32[2048,512]{1,0:T(8,128)} %get-tuple-element.18.own_hbm) | copy-start | bytes 12582916
  43.6 1.6 %copy-start.6 = (bf16[2048,512]{1,0:T(8,128)(2,1)S(1)}, bf16[2048,512]{1,0:T(8,128)(2,1)}, u32[]{:S(2)}) copy-start(bf16[2048,512]{1,0:T(8,128)(2,1)} %cot_hbm.1) | copy-start | bytes 6291460
  52.9 3.5 %collective-permute-start = (bf16[256,512]{1,0:T(8,128)(2,1)S(1)}, bf16[256,512]{1,0:T(8,128)(2,1)S(1)}, u32[]{:S(2)}, u32[]{:S(2)}) collective-permute-start(bf16[256,512]{1,0:T(8,128)(2,1)S(1)} %get-tuple-element.26), channel_id=1, source_target_pairs={{0,1},{1,0},{2,3},{3,2},{4,5},{5,4},{6,7},{7,6},{8,9},{9,8},{10,11... | collective-permute-start | bytes 786440 | tf_op jit(solution)/shard_map/ppermute | solution.py:400
  55.0 1.3 %copy-start.7 = (bf16[2048,512]{1,0:T(8,128)(2,1)}, bf16[2048,512]{1,0:T(8,128)(2,1)S(1)}, u32[]{:S(2)}) copy-start(bf16[2048,512]{1,0:T(8,128)(2,1)S(1)} %get-tuple-element.22.grad_ref) | copy-start | bytes 6291460
  59.6 46.5 %all-to-all-start.1 = ((bf16[32,32,512]{2,1,0:T(8,128)(2,1)}), bf16[32,32,512]{2,1,0:T(8,128)(2,1)S(1)}, u32[]{:S(2)}, u32[]{:S(2)}) async-start(bf16[32,32,512]{2,1,0:T(8,128)(2,1)} %bitcast.5), calls=%async_computation.1 | async-start | bytes 2097152 | tf_op jit(solution)/shard_map/all_to_all | solution.py:341
  63.5 12.8 %collective-permute-start.3 = (bf16[64,512]{1,0:T(8,128)(2,1)S(1)}, bf16[64,512]{1,0:T(8,128)(2,1)S(1)}, u32[]{:S(2)}, u32[]{:S(2)}) collective-permute-start(bf16[64,512]{1,0:T(8,128)(2,1)S(1)} %get-tuple-element.27.after_ref), channel_id=1, source_target_pairs={{0,6},{1,7},{2,4},{3,5},{4,2},{5,3},{6,0},{7,1},{8,14},{9,15},{10,... | collective-permute-start | bytes 196616 | tf_op jit(solution)/shard_map/ppermute | solution.py:400
  66.0 10.8 %collective-permute-start.1 = (bf16[64,512]{1,0:T(8,128)(2,1)S(1)}, bf16[64,512]{1,0:T(8,128)(2,1)S(1)}, u32[]{:S(2)}, u32[]{:S(2)}) collective-permute-start(bf16[64,512]{1,0:T(8,128)(2,1)S(1)} %get-tuple-element.29), channel_id=1, source_target_pairs={{0,2},{1,3},{2,0},{3,1},{4,6},{5,7},{6,4},{7,5},{8,10},{9,11},{10,... | collective-permute-start | bytes 196616 | tf_op jit(solution)/shard_map/ppermute | solution.py:400
  66.6 10.2 %collective-permute-start.2 = (bf16[64,512]{1,0:T(8,128)(2,1)S(1)}, bf16[64,512]{1,0:T(8,128)(2,1)S(1)}, u32[]{:S(2)}, u32[]{:S(2)}) collective-permute-start(bf16[64,512]{1,0:T(8,128)(2,1)S(1)} %get-tuple-element.30), channel_id=1, source_target_pairs={{0,4},{1,5},{2,6},{3,7},{4,0},{5,1},{6,2},{7,3},{8,12},{9,13},{10,... | collective-permute-start | bytes 196616 | tf_op jit(solution)/shard_map/ppermute | solution.py:400
  76.8 2.2 %copy-start = (f32[2048,512]{1,0:T(8,128)S(1)}, f32[2048,512]{1,0:T(8,128)}, u32[]{:S(2)}) copy-start(f32[2048,512]{1,0:T(8,128)} %spread.1.owned_hbm.after_ref) | copy-start | bytes 12582916
  79.0 16.8 %copy-start.11 = (s32[1,32]{1,0:T(1,128)S(1)}, s32[1,32]{1,0:T(1,128)}, u32[]{:S(2)}) copy-start(s32[1,32]{1,0:T(1,128)} %counts_ref.1) | copy-start | bytes 388
  79.0 16.9 %copy-start.10 = (s32[1,32,32]{2,1,0:T(8,128)S(1)}, s32[1,32,32]{2,1,0:T(8,128)}, u32[]{:S(2)}) copy-start(s32[1,32,32]{2,1,0:T(8,128)} %param.14) | copy-start | bytes 12292
  79.0 5.6 %collective-permute-start.4 = (bf16[64,512]{1,0:T(8,128)(2,1)S(1)}, bf16[64,512]{1,0:T(8,128)(2,1)S(1)}, u32[]{:S(2)}, u32[]{:S(2)}) collective-permute-start(bf16[64,512]{1,0:T(8,128)(2,1)S(1)} %add.2.refs_0_), channel_id=1, source_target_pairs={{0,8},{8,0},{16,24},{24,16},{1,9},{9,1},{17,25},{25,17},{2,10},{10... | collective-permute-start | bytes 196616 | tf_op jit(solution)/shard_map/ppermute | solution.py:400
  80.2 14.1 %collective-permute-start.5 = (bf16[64,512]{1,0:T(8,128)(2,1)S(1)}, bf16[64,512]{1,0:T(8,128)(2,1)S(1)}, u32[]{:S(2)}, u32[]{:S(2)}) collective-permute-start(bf16[64,512]{1,0:T(8,128)(2,1)S(1)} %add.2.refs_0_), channel_id=1, source_target_pairs={{0,16},{8,24},{16,0},{24,8},{1,17},{9,25},{17,1},{25,9},{2,18},{10... | collective-permute-start | bytes 196616 | tf_op jit(solution)/shard_map/ppermute | solution.py:400
  83.6 10.6 %collective-permute-start.6 = (bf16[64,512]{1,0:T(8,128)(2,1)S(1)}, bf16[64,512]{1,0:T(8,128)(2,1)S(1)}, u32[]{:S(2)}, u32[]{:S(2)}) collective-permute-start(bf16[64,512]{1,0:T(8,128)(2,1)S(1)} %add.2.refs_0_), channel_id=1, source_target_pairs={{0,24},{8,16},{16,8},{24,0},{1,25},{9,17},{17,9},{25,1},{2,26},{10... | collective-permute-start | bytes 196616 | tf_op jit(solution)/shard_map/ppermute | solution.py:400
  94.3 4.8 %collective-permute-start.10 = (bf16[64,512]{1,0:T(8,128)(2,1)S(1)}, bf16[64,512]{1,0:T(8,128)(2,1)S(1)}, u32[]{:S(2)}, u32[]{:S(2)}) collective-permute-start(bf16[64,512]{1,0:T(8,128)(2,1)S(1)} %add.3.refs_0_), channel_id=1, source_target_pairs={{0,4},{1,5},{2,6},{3,7},{4,0},{5,1},{6,2},{7,3},{8,12},{9,13},{10,... | collective-permute-start | bytes 196616 | tf_op jit(solution)/shard_map/ppermute | solution.py:400
  95.8 4.8 %collective-permute-start.11 = (bf16[64,512]{1,0:T(8,128)(2,1)S(1)}, bf16[64,512]{1,0:T(8,128)(2,1)S(1)}, u32[]{:S(2)}, u32[]{:S(2)}) collective-permute-start(bf16[64,512]{1,0:T(8,128)(2,1)S(1)} %add.3.refs_0_), channel_id=1, source_target_pairs={{0,5},{1,4},{2,7},{3,6},{4,1},{5,0},{6,3},{7,2},{8,13},{9,12},{10,... | collective-permute-start | bytes 196616 | tf_op jit(solution)/shard_map/ppermute | solution.py:400
  96.1 5.8 %collective-permute-start.12 = (bf16[64,512]{1,0:T(8,128)(2,1)S(1)}, bf16[64,512]{1,0:T(8,128)(2,1)S(1)}, u32[]{:S(2)}, u32[]{:S(2)}) collective-permute-start(bf16[64,512]{1,0:T(8,128)(2,1)S(1)} %add.3.refs_0_), channel_id=1, source_target_pairs={{0,6},{1,7},{2,4},{3,5},{4,2},{5,3},{6,0},{7,1},{8,14},{9,15},{10,... | collective-permute-start | bytes 196616 | tf_op jit(solution)/shard_map/ppermute | solution.py:400
  97.5 4.8 %collective-permute-start.13 = (bf16[64,512]{1,0:T(8,128)(2,1)S(1)}, bf16[64,512]{1,0:T(8,128)(2,1)S(1)}, u32[]{:S(2)}, u32[]{:S(2)}) collective-permute-start(bf16[64,512]{1,0:T(8,128)(2,1)S(1)} %add.3.refs_0_), channel_id=1, source_target_pairs={{0,7},{1,6},{2,5},{3,4},{4,3},{5,2},{6,1},{7,0},{8,15},{9,14},{10,... | collective-permute-start | bytes 196616 | tf_op jit(solution)/shard_map/ppermute | solution.py:400
  99.0 3.3 %collective-permute-start.7 = (bf16[64,512]{1,0:T(8,128)(2,1)S(1)}, bf16[64,512]{1,0:T(8,128)(2,1)S(1)}, u32[]{:S(2)}, u32[]{:S(2)}) collective-permute-start(bf16[64,512]{1,0:T(8,128)(2,1)S(1)} %add.3.refs_0_), channel_id=1, source_target_pairs={{0,1},{1,0},{2,3},{3,2},{4,5},{5,4},{6,7},{7,6},{8,9},{9,8},{10,11... | collective-permute-start | bytes 196616 | tf_op jit(solution)/shard_map/ppermute | solution.py:400
  99.1 5.6 %collective-permute-start.8 = (bf16[64,512]{1,0:T(8,128)(2,1)S(1)}, bf16[64,512]{1,0:T(8,128)(2,1)S(1)}, u32[]{:S(2)}, u32[]{:S(2)}) collective-permute-start(bf16[64,512]{1,0:T(8,128)(2,1)S(1)} %add.3.refs_0_), channel_id=1, source_target_pairs={{0,2},{1,3},{2,0},{3,1},{4,6},{5,7},{6,4},{7,5},{8,10},{9,11},{10,... | collective-permute-start | bytes 196616 | tf_op jit(solution)/shard_map/ppermute | solution.py:400
  100.6 4.4 %collective-permute-start.9 = (bf16[64,512]{1,0:T(8,128)(2,1)S(1)}, bf16[64,512]{1,0:T(8,128)(2,1)S(1)}, u32[]{:S(2)}, u32[]{:S(2)}) collective-permute-start(bf16[64,512]{1,0:T(8,128)(2,1)S(1)} %add.3.refs_0_), channel_id=1, source_target_pairs={{0,3},{1,2},{2,1},{3,0},{4,7},{5,6},{6,5},{7,4},{8,11},{9,10},{10,... | collective-permute-start | bytes 196616 | tf_op jit(solution)/shard_map/ppermute | solution.py:400
  106.1 2.2 %copy-start.1 = (f32[2048,512]{1,0:T(8,128)S(1)}, f32[2048,512]{1,0:T(8,128)}, u32[]{:S(2)}) copy-start(f32[2048,512]{1,0:T(8,128)} %spread.1.owned_hbm.after_ref) | copy-start | bytes 12582916

commit v2 on v1

--- a/solution.py
+++ b/solution.py
@@ -21,7 +21,8 @@
 
 VMEM = pl.BlockSpec(memory_space=pltpu.VMEM)
 SMEM = pl.BlockSpec(memory_space=pltpu.SMEM)
-HBM = pl.BlockSpec(memory_space=pl.ANY)
+ANY = pl.BlockSpec(memory_space=pl.ANY)
+HBM = pl.BlockSpec(memory_space=pltpu.MemorySpace.HBM)
 
 
 def made(keep, shape, dtype):
@@ -32,6 +33,14 @@
     if not keep:
         return arrays
     return [pltpu.with_memory_space_constraint(x, pltpu.VMEM) for x in arrays]
+
+
+def stored(*arrays):
+    return [pltpu.with_memory_space_constraint(x, pltpu.MemorySpace.HBM) for x in arrays]
+
+
+def far_made(shape, dtype):
+    return pltpu.MemorySpace.HBM(shape, dtype)
 
 
 def dot(a, b, contract=((1,), (0,))):
@@ -146,9 +155,9 @@
             ],
         ),
         out_shape=[
-            jax.ShapeDtypeStruct((owned, owned), BF16),
-            jax.ShapeDtypeStruct((owned, remote), BF16),
-            jax.ShapeDtypeStruct((owned, width), F32),
+            far_made((owned, owned), BF16),
+            far_made((owned, remote), BF16),
+            far_made((owned, width), F32),
         ],
         compiler_params=params(48),
         cost_estimate=pl.CostEstimate(
@@ -210,7 +219,7 @@
         in_specs=[SMEM, HBM, HBM, HBM, VMEM, VMEM],
         out_specs=[HBM, VMEM, VMEM, VMEM, VMEM],
         out_shape=[
-            jax.ShapeDtypeStruct((owned, width), BF16),
+            far_made((owned, width), BF16),
             made(keep, far.shape, BF16),
             made(keep, (owned, width), BF16),
             made(keep, half, F32),
@@ -226,7 +235,7 @@
         ],
         compiler_params=params(28 if keep else 60),
         name="layer",
-    )(me, far, own, cotangent, weight, got)
+    )(me, *stored(far, own, cotangent), weight, got)
 
 
 def grad_kernel(slope_ref, w_ref, grad_ref, grad_hbm, sems):
@@ -245,7 +254,7 @@
         grad_kernel,
         in_specs=[VMEM] * 2,
         out_specs=[VMEM, HBM],
-        out_shape=[made(keep, slope.shape, BF16), jax.ShapeDtypeStruct(slope.shape, BF16)],
+        out_shape=[made(keep, slope.shape, BF16), far_made(slope.shape, BF16)],
         scratch_shapes=[pltpu.SemaphoreType.DMA((slope.shape[0] // BIG,))],
         compiler_params=params(12 if keep else 40),
         name="hidden_grad",
@@ -267,9 +276,9 @@
     shape = (far.shape[1], grad.shape[1])
     return pl.pallas_call(
         back_kernel,
-        in_specs=[VMEM, VMEM, HBM],
+        in_specs=[VMEM, VMEM, ANY],
         out_specs=HBM,
-        out_shape=jax.ShapeDtypeStruct(shape, BF16),
+        out_shape=far_made(shape, BF16),
         scratch_shapes=[pltpu.VMEM(shape, BF16), pltpu.SemaphoreType.DMA((shape[0] // BIG,))],
         compiler_params=params(16 if keep else 60),
         name="back_rows",
@@ -287,13 +296,13 @@
         grid=(owned // BIG,),
         in_specs=[pl.BlockSpec((owned, BIG), lambda i: (0, i)), whole(grad.shape)],
         out_specs=pl.BlockSpec((BIG, width), lambda i: (i, 0)),
-        out_shape=jax.ShapeDtypeStruct((owned, width), F32),
+        out_shape=far_made((owned, width), F32),
         compiler_params=params(60),
         cost_estimate=pl.CostEstimate(
             flops=2 * owned * owned * width, bytes_accessed=16 * 1024 * 1024, transcendentals=0
         ),
         name="spread",
-    )(adjacency, grad)
+    )(*stored(adjacency, grad))
 
 
 def return_kernel(index_ref, owned_hbm, got_ref, out_hbm, owned, out, sems, sent):
@@ -325,7 +334,7 @@
         return_kernel,
         in_specs=[VMEM, HBM, VMEM],
         out_specs=HBM,
-        out_shape=jax.ShapeDtypeStruct((rows, width), BF16),
+        out_shape=far_made((rows, width), BF16),
         scratch_shapes=[
             pltpu.VMEM((rows, width), F32),
             pltpu.VMEM((rows, width), BF16),
@@ -334,7 +343,7 @@
         ],
         compiler_params=params(28 if keep else 60),
         name="give_back",
-    )(index, owned, got)
+    )(index, *stored(owned), got)
 
 
 def exchange(x, axes):
@@ -359,7 +368,7 @@
     )(me, mine, got)
 
 
-def join_kernel(me_ref, *refs):
+def join_kernel(me_ref, after_ref, *refs):
     in_refs, out_ref = refs[:-1], refs[-1]
     height, half = in_refs[0].shape[0], out_ref.shape[0] // 2
     for k, in_ref in enumerate(in_refs):
@@ -368,15 +377,15 @@
         out_ref[pl.ds(at, height), :] = in_ref[...].astype(F32)
 
 
-def join(me, parts):
+def join(me, after, parts):
     height, width = parts[0].shape
     return pl.pallas_call(
         join_kernel,
-        in_specs=[SMEM] + [VMEM] * len(parts),
+        in_specs=[SMEM, ANY] + [VMEM] * len(parts),
         out_shape=jax.ShapeDtypeStruct((height * len(parts), width), F32),
         compiler_params=params(8),
         name="join",
-    )(me, *parts)
+    )(me, after, *parts)
 
 
 def add_kernel(after_ref, *refs):
@@ -389,7 +398,7 @@
 def add(after, parts):
     return pl.pallas_call(
         add_kernel,
-        in_specs=[HBM] + [VMEM] * len(parts),
+        in_specs=[ANY] + [VMEM] * len(parts),
         out_shape=jax.ShapeDtypeStruct(parts[0].shape, BF16),
         compiler_params=params(8),
         name="add",
@@ -418,11 +427,17 @@
     returned = exchange(back.reshape(peers, slots, width), AXES).reshape(remote, width)
     owned = spread(adjacency, grad_out)
     piece = add(owned, [pieces[0]] + [swap(pieces[k], "local", locals_, 2 * k) for k in range(1, chips)])
-    piece = add(me, [piece] + [swap(piece, "group", groups, k) for k in range(1, groups)])
-    weight_grad = join(me, [piece] + [swap(piece, "local", locals_, k) for k in range(1, locals_)])
+    step = 1
+    while step < groups:
+        piece = add(me, [piece, swap(piece, "group", groups, step)])
+        step *= 2
+    gathered = []
+    for k in range(chips):
+        mine = swap(piece, "local", locals_, 2 * k) if k else piece
+        gathered += [mine, swap(mine, "local", locals_, 1)]
     live = jnp.arange(slots)[None, :] < counts[0][:, None]
     feature_grad = give_back(keep, jnp.where(live, lists, -1).reshape(1, remote), owned, returned)
-    return activated, feature_grad, weight_grad
+    return activated, feature_grad, join(me, feature_grad, gathered)
 
 
 def solution(mesh):

time: 113 us -> 102 us (0.903)
  local copies, waits for them, and re-layouts: 13.4 us -> 5.55 us
  starting transfers between devices: 25.9 us -> 22.1 us
  Pallas kernels: 52.1 us -> 53.8 us
  waiting for transfers between devices: 20.2 us -> 19 us
    unnamed x24 -> x16, local copies, waits for them, and re-layouts: 13.3 us -> 5.38 us
    ppermute x14 -> x13, starting transfers between devices: 14.7 us -> 10.9 us  [swap(): return lax.ppermute(x, axis, [(i, i ^ k) for i in range(size)])]
    pallas_call x1, Pallas kernels: 7.65 us -> 8.98 us  [layer(): pl.pallas_call(layer_kernel, in_specs=[SMEM, HBM, HBM, HBM, VMEM, VMEM],...]
    ppermute x14 -> x13, waiting for transfers between devices: 15.2 us -> 13.9 us  [swap(): return lax.ppermute(x, axis, [(i, i ^ k) for i in range(size)])]
    pallas_call x4 -> x5, Pallas kernels: 4.28 us -> 4.29 us  [the longest x1 3.18 us: back_rows(): pl.pallas_call(back_kernel, in_specs=[VMEM, VMEM, ANY], out_specs=HBM, ou...]
  transfers between devices with their start and end apart: 16 -> 15, of which waited for: 8 -> 7; matrix products, arithmetic and copies ran while one was open for 0% -> 0% of each run, Pallas kernels for 28% -> 35%
where the time goes in v2:
time: 102 us; the launch traced here: 101 us
  Pallas kernels  53.8 us (53%)
  starting transfers between devices  22.1 us (22%)
  waiting for transfers between devices  19 us (19%)
  local copies, waits for them, and re-layouts  5.55 us (5%)
    pallas_call x1, Pallas kernels, build(): pl.pallas_call(build_kernel, grid_spec=pltpu.PrefetchScalarGridSpec(num_s...  19.5 us
    ppermute x13, waiting for transfers between devices, swap(): return lax.ppermute(x, axis, [(i, i ^ k) for i in range(size)])  13.9 us
    all_to_all x2, starting transfers between devices, exchange(): return lax.all_to_all(x, axes, split_axis=0, concat_axis=0, tiled=True)  11.2 us
    ppermute x13, starting transfers between devices, swap(): return lax.ppermute(x, axis, [(i, i ^ k) for i in range(size)])  10.9 us
    pallas_call x1, Pallas kernels, spread(): pl.pallas_call(spread_kernel, grid=(owned // BIG,), in_specs=[pl.BlockSpe...  9.21 us
    pallas_call x1, Pallas kernels, layer(): pl.pallas_call(layer_kernel, in_specs=[SMEM, HBM, HBM, HBM, VMEM, VMEM],...  8.98 us
    unnamed x16, local copies, waits for them, and re-layouts  5.38 us
    all_to_all x2, waiting for transfers between devices, exchange(): return lax.all_to_all(x, axes, split_axis=0, concat_axis=0, tiled=True)  5.09 us
  transfers between devices with their start and end apart: 15, of which 7 were waited for; matrix products, arithmetic and copies ran while one was open for 0% of the time, Pallas kernels for 35%

profile of v2, /device:TPU:0, one launch (start us, length us, event | category | flops | bytes accessed | tf_op | source)
XLA Modules:
  0.0 101.2 jit_solution(15674017361340445022)
XLA Ops:
  0.7 5.0 %collect.1 = bf16[1024,512]{1,0:T(8,128)(2,1)} custom-call(s32[1,32]{1,0:T(1,128)} %counts_ref.1, s32[32,32]{1,0:T(8,128)} %bitcast.11, bf16[2048,512]{1,0:T(8,128)(2,1)} %x_ref.3), custom_call_target="tpu_custom_call" | custom-call | tf_op jit(solution)/shard_map/collect/pallas_call | solution.py:71
  5.7 7.3 %all-to-all-start = ((bf16[32,32,512]{2,1,0:T(8,128)(2,1)}), bf16[32,32,512]{2,1,0:T(8,128)(2,1)S(1)}, u32[]{:S(2)}, u32[]{:S(2)}) async-start(bf16[32,32,512]{2,1,0:T(8,128)(2,1)} %bitcast.10), calls=%async_computation | async-start | bytes 2097152 | tf_op jit(solution)/shard_map/all_to_all | solution.py:350
  13.0 1.6 %copy-done.3 = bf16[2048,512]{1,0:T(8,128)(2,1)S(1)} copy-done((bf16[2048,512]{1,0:T(8,128)(2,1)S(1)}, bf16[2048,512]{1,0:T(8,128)(2,1)}, u32[]{:S(2)}) %copy-start.3) | copy-done | bytes 2097176
  14.6 19.5 %build.1 = (bf16[2048,2048]{1,0:T(8,128)(2,1)}, bf16[2048,1024]{1,0:T(8,128)(2,1)}, f32[2048,512]{1,0:T(8,128)}) custom-call(s32[256]{0:T(256)S(1)} %copy-done.4, s32[256]{0:T(256)S(1)} %copy-done.5, bf16[256,128,128]{2,1,0:T(8,128)(2,1)} %tiles_ref.1, bf16[2048,512]{1,0:T(8,128)(2,1)S(1)} %copy-done.3), custom_call_target="tpu_custom_call" | custom-call | flops 4294967296 | bytes 41943040 | tf_op jit(solution)/shard_map/build/pallas_call | solution.py:139
  34.1 5.1 %all-to-all-done = bf16[32,32,512]{2,1,0:T(8,128)(2,1)S(1)} async-done(((bf16[32,32,512]{2,1,0:T(8,128)(2,1)}), bf16[32,32,512]{2,1,0:T(8,128)(2,1)S(1)}, u32[]{:S(2)}, u32[]{:S(2)}) %all-to-all-start) | async-done | bytes 1048608 | tf_op jit(solution)/shard_map/all_to_all | solution.py:350
  39.2 9.0 %layer.1 = (bf16[2048,512]{1,0:T(8,128)(2,1)}, bf16[2048,1024]{1,0:T(8,128)(2,1)S(1)}, bf16[2048,512]{1,0:T(8,128)(2,1)S(1)}, f32[256,512]{1,0:T(8,128)S(1)}, bf16[256,512]{1,0:T(8,128)(2,1)S(1)}) custom-call(s32[1]{0:T(128)} %bitcast.me_ref.after_ref, bf16[2048,1024]{1,0:T(8,128)(2,1)} %get-tuple-element.17.far_hbm, f32[2048,512]{1,0:T(8,128)} %get-tuple-element.18.own_hbm, ...), custom_call_target="tpu_custom_call" | custom-call | tf_op jit(solution)/shard_map/layer/pallas_call | solution.py:217
  48.3 2.1 %hidden_grad.1 = (bf16[2048,512]{1,0:T(8,128)(2,1)S(1)}, bf16[2048,512]{1,0:T(8,128)(2,1)}) custom-call(bf16[2048,512]{1,0:T(8,128)(2,1)S(1)} %get-tuple-element.21.slope_ref, bf16[512,512]{1,0:T(8,128)(2,1)S(1)} %copy-done.2), custom_call_target="tpu_custom_call" | custom-call | tf_op jit(solution)/shard_map/hidden_grad/pallas_call | solution.py:253
  50.5 3.2 %back_rows.1 = bf16[1024,512]{1,0:T(8,128)(2,1)} custom-call(bf16[2048,1024]{1,0:T(8,128)(2,1)S(1)} %get-tuple-element.23.far_ref, bf16[2048,512]{1,0:T(8,128)(2,1)S(1)} %get-tuple-element.24.grad_ref, bf16[64,512]{1,0:T(8,128)(2,1)S(1)} %get-tuple-element.27.after_ref), custom_call_target="tpu_custom_call" | custom-call | tf_op jit(solution)/shard_map/back_rows/pallas_call | solution.py:277
  53.7 3.9 %all-to-all-start.1 = ((bf16[32,32,512]{2,1,0:T(8,128)(2,1)}), bf16[32,32,512]{2,1,0:T(8,128)(2,1)S(1)}, u32[]{:S(2)}, u32[]{:S(2)}) async-start(bf16[32,32,512]{2,1,0:T(8,128)(2,1)} %bitcast.9), calls=%async_computation.1 | async-start | bytes 2097152 | tf_op jit(solution)/shard_map/all_to_all | solution.py:350
  57.6 2.6 %collective-permute-start.3 = (bf16[64,512]{1,0:T(8,128)(2,1)S(1)}, bf16[64,512]{1,0:T(8,128)(2,1)S(1)}, u32[]{:S(2)}, u32[]{:S(2)}) collective-permute-start(bf16[64,512]{1,0:T(8,128)(2,1)S(1)} %get-tuple-element.27.after_ref), channel_id=1, source_target_pairs={{0,6},{1,7},{2,4},{3,5},{4,2},{5,3},{6,0},{7,1},{8,14},{9,15},{10,... | collective-permute-start | bytes 196616 | tf_op jit(solution)/shard_map/ppermute | solution.py:409
  60.2 0.6 collective-permute-start.1
  60.7 0.4 collective-permute-start.2
  61.2 9.2 %spread.1.owned_hbm.after_ref = f32[2048,512]{1,0:T(8,128)} custom-call(bf16[2048,2048]{1,0:T(8,128)(2,1)} %get-tuple-element.20.adj_ref, bf16[2048,512]{1,0:T(8,128)(2,1)} %get-tuple-element.22.grad_ref), custom_call_target="tpu_custom_call" | custom-call | flops 4294967296 | bytes 16777216 | tf_op jit(solution)/shard_map/spread/pallas_call | solution.py:294
  70.4 0.6 collective-permute-done.1.refs_1_
  70.9 2.2 %copy-done = f32[2048,512]{1,0:T(8,128)S(1)} copy-done((f32[2048,512]{1,0:T(8,128)S(1)}, f32[2048,512]{1,0:T(8,128)}, u32[]{:S(2)}) %copy-start) | copy-done | bytes 4194328
  73.2 1.1 %collective-permute-start.4 = (bf16[64,512]{1,0:T(8,128)(2,1)S(1)}, bf16[64,512]{1,0:T(8,128)(2,1)S(1)}, u32[]{:S(2)}, u32[]{:S(2)}) collective-permute-start(bf16[64,512]{1,0:T(8,128)(2,1)S(1)} %add.3.refs_0_), channel_id=1, source_target_pairs={{0,8},{8,0},{16,24},{24,16},{1,9},{9,1},{17,25},{25,17},{2,10},{10... | collective-permute-start | bytes 196616 | tf_op jit(solution)/shard_map/ppermute | solution.py:409
  74.3 4.4 %collective-permute-done.4.refs_1_ = bf16[64,512]{1,0:T(8,128)(2,1)S(1)} collective-permute-done((bf16[64,512]{1,0:T(8,128)(2,1)S(1)}, bf16[64,512]{1,0:T(8,128)(2,1)S(1)}, u32[]{:S(2)}, u32[]{:S(2)}) %collective-permute-start.4) | collective-permute-done | bytes 65568 | tf_op jit(solution)/shard_map/ppermute | solution.py:409
  78.7 2.3 %collective-permute-start.5 = (bf16[64,512]{1,0:T(8,128)(2,1)S(1)}, bf16[64,512]{1,0:T(8,128)(2,1)S(1)}, u32[]{:S(2)}, u32[]{:S(2)}) collective-permute-start(bf16[64,512]{1,0:T(8,128)(2,1)S(1)} %add.4.refs_0_), channel_id=1, source_target_pairs={{0,16},{8,24},{16,0},{24,8},{1,17},{9,25},{17,1},{25,9},{2,18},{10... | collective-permute-start | bytes 196616 | tf_op jit(solution)/shard_map/ppermute | solution.py:409
  81.0 5.4 %collective-permute-done.5.refs_1_ = bf16[64,512]{1,0:T(8,128)(2,1)S(1)} collective-permute-done((bf16[64,512]{1,0:T(8,128)(2,1)S(1)}, bf16[64,512]{1,0:T(8,128)(2,1)S(1)}, u32[]{:S(2)}, u32[]{:S(2)}) %collective-permute-start.5) | collective-permute-done | bytes 65568 | tf_op jit(solution)/shard_map/ppermute | solution.py:409
  86.5 1.5 %collective-permute-start.9 = (bf16[64,512]{1,0:T(8,128)(2,1)S(1)}, bf16[64,512]{1,0:T(8,128)(2,1)S(1)}, u32[]{:S(2)}, u32[]{:S(2)}) collective-permute-start(bf16[64,512]{1,0:T(8,128)(2,1)S(1)} %add.5.refs_0_), channel_id=1, source_target_pairs={{0,4},{1,5},{2,6},{3,7},{4,0},{5,1},{6,2},{7,3},{8,12},{9,13},{10,... | collective-permute-start | bytes 196616 | tf_op jit(solution)/shard_map/ppermute | solution.py:409
  88.0 1.5 %collective-permute-start.11 = (bf16[64,512]{1,0:T(8,128)(2,1)S(1)}, bf16[64,512]{1,0:T(8,128)(2,1)S(1)}, u32[]{:S(2)}, u32[]{:S(2)}) collective-permute-start(bf16[64,512]{1,0:T(8,128)(2,1)S(1)} %add.5.refs_0_), channel_id=1, source_target_pairs={{0,6},{1,7},{2,4},{3,5},{4,2},{5,3},{6,0},{7,1},{8,14},{9,15},{10,... | collective-permute-start | bytes 196616 | tf_op jit(solution)/shard_map/ppermute | solution.py:409
  89.5 0.6 collective-permute-start.7
  90.0 0.1 iota_compare_fusion
  90.1 0.1 squeeze.6
  90.2 0.1 lt.29
  90.3 0.5 collective-permute-done.9.refs_4_
  90.8 2.7 %collective-permute-done.11.refs_6_ = bf16[64,512]{1,0:T(8,128)(2,1)S(1)} collective-permute-done((bf16[64,512]{1,0:T(8,128)(2,1)S(1)}, bf16[64,512]{1,0:T(8,128)(2,1)S(1)}, u32[]{:S(2)}, u32[]{:S(2)}) %collective-permute-start.11) | collective-permute-done | bytes 65568 | tf_op jit(solution)/shard_map/ppermute | solution.py:409
  93.5 0.3 collective-permute-done.7.refs_2_
  93.7 0.3 collective-permute-start.8
  94.0 4.5 %give_back.1.after_ref = bf16[2048,512]{1,0:T(8,128)(2,1)} custom-call(s32[1,1024]{1,0:T(1,128)S(1)} %broadcast_select_fusion.index_ref, f32[2048,512]{1,0:T(8,128)} %spread.1.owned_hbm.after_ref, bf16[1024,512]{1,0:T(8,128)(2,1)S(1)} %bitcast.7), custom_call_target="tpu_custom_call" | custom-call | tf_op jit(solution)/shard_map/give_back/pallas_call | solution.py:333
  98.6 1.6 %copy-done.1 = bf16[2048,512]{1,0:T(8,128)(2,1)S(1)} copy-done((bf16[2048,512]{1,0:T(8,128)(2,1)S(1)}, bf16[2048,512]{1,0:T(8,128)(2,1)}, u32[]{:S(2)}) %copy-start.1) | copy-done | bytes 2097176
  100.2 1.0 %join.1 = f32[512,512]{1,0:T(8,128)} custom-call(s32[1]{0:T(128)} %bitcast.me_ref.after_ref, bf16[2048,512]{1,0:T(8,128)(2,1)S(1)} %copy-done.1, bf16[64,512]{1,0:T(8,128)(2,1)S(1)} %add.5.refs_0_, bf16[64,512]{1,0:T(8,128)(2,1)S(1)} %collective-permute-done.6.refs_1_, bf16[64,512]{1,0:T(8,128)(2,1)S(1)} %collective-permute-done.7.refs_2_, ...), custom_call_target="tpu_custom_call" | custom-call | tf_op jit(solution)/shard_map/join/pallas_call | solution.py:382
  (30 shorter events, 0.3 us)
Async XLA Ops:
  0.6 12.4 %copy-start.4 = (s32[256]{0:T(256)S(1)}, s32[256]{0:T(256)}, u32[]{:S(2)}) copy-start(s32[256]{0:T(256)} %rows_ref.1) | copy-start | bytes 3076
  0.6 12.4 %copy-start.5 = (s32[256]{0:T(256)S(1)}, s32[256]{0:T(256)}, u32[]{:S(2)}) copy-start(s32[256]{0:T(256)} %cols_ref.1) | copy-start | bytes 3076
  5.7 33.5 %all-to-all-start = ((bf16[32,32,512]{2,1,0:T(8,128)(2,1)}), bf16[32,32,512]{2,1,0:T(8,128)(2,1)S(1)}, u32[]{:S(2)}, u32[]{:S(2)}) async-start(bf16[32,32,512]{2,1,0:T(8,128)(2,1)} %bitcast.10), calls=%async_computation | async-start | bytes 2097152 | tf_op jit(solution)/shard_map/all_to_all | solution.py:350
  13.0 1.6 %copy-start.3 = (bf16[2048,512]{1,0:T(8,128)(2,1)S(1)}, bf16[2048,512]{1,0:T(8,128)(2,1)}, u32[]{:S(2)}) copy-start(bf16[2048,512]{1,0:T(8,128)(2,1)} %x_ref.3) | copy-start | bytes 6291460
  14.6 24.6 %copy-start.2 = (bf16[512,512]{1,0:T(8,128)(2,1)S(1)}, bf16[512,512]{1,0:T(8,128)(2,1)}, u32[]{:S(2)}) copy-start(bf16[512,512]{1,0:T(8,128)(2,1)} %w_ref.3) | copy-start | bytes 1572868
  48.2 2.2 %collective-permute-start = (bf16[256,512]{1,0:T(8,128)(2,1)S(1)}, bf16[256,512]{1,0:T(8,128)(2,1)S(1)}, u32[]{:S(2)}, u32[]{:S(2)}) collective-permute-start(bf16[256,512]{1,0:T(8,128)(2,1)S(1)} %get-tuple-element.26), channel_id=1, source_target_pairs={{0,1},{1,0},{2,3},{3,2},{4,5},{5,4},{6,7},{7,6},{8,9},{9,8},{10,11... | collective-permute-start | bytes 786440 | tf_op jit(solution)/shard_map/ppermute | solution.py:409
  53.7 40.3 %all-to-all-start.1 = ((bf16[32,32,512]{2,1,0:T(8,128)(2,1)}), bf16[32,32,512]{2,1,0:T(8,128)(2,1)S(1)}, u32[]{:S(2)}, u32[]{:S(2)}) async-start(bf16[32,32,512]{2,1,0:T(8,128)(2,1)} %bitcast.9), calls=%async_computation.1 | async-start | bytes 2097152 | tf_op jit(solution)/shard_map/all_to_all | solution.py:350
  57.6 12.8 %collective-permute-start.3 = (bf16[64,512]{1,0:T(8,128)(2,1)S(1)}, bf16[64,512]{1,0:T(8,128)(2,1)S(1)}, u32[]{:S(2)}, u32[]{:S(2)}) collective-permute-start(bf16[64,512]{1,0:T(8,128)(2,1)S(1)} %get-tuple-element.27.after_ref), channel_id=1, source_target_pairs={{0,6},{1,7},{2,4},{3,5},{4,2},{5,3},{6,0},{7,1},{8,14},{9,15},{10,... | collective-permute-start | bytes 196616 | tf_op jit(solution)/shard_map/ppermute | solution.py:409
  60.2 10.8 %collective-permute-start.1 = (bf16[64,512]{1,0:T(8,128)(2,1)S(1)}, bf16[64,512]{1,0:T(8,128)(2,1)S(1)}, u32[]{:S(2)}, u32[]{:S(2)}) collective-permute-start(bf16[64,512]{1,0:T(8,128)(2,1)S(1)} %get-tuple-element.29), channel_id=1, source_target_pairs={{0,2},{1,3},{2,0},{3,1},{4,6},{5,7},{6,4},{7,5},{8,10},{9,11},{10,... | collective-permute-start | bytes 196616 | tf_op jit(solution)/shard_map/ppermute | solution.py:409
  60.7 10.2 %collective-permute-start.2 = (bf16[64,512]{1,0:T(8,128)(2,1)S(1)}, bf16[64,512]{1,0:T(8,128)(2,1)S(1)}, u32[]{:S(2)}, u32[]{:S(2)}) collective-permute-start(bf16[64,512]{1,0:T(8,128)(2,1)S(1)} %get-tuple-element.30), channel_id=1, source_target_pairs={{0,4},{1,5},{2,6},{3,7},{4,0},{5,1},{6,2},{7,3},{8,12},{9,13},{10,... | collective-permute-start | bytes 196616 | tf_op jit(solution)/shard_map/ppermute | solution.py:409
  70.9 2.2 %copy-start = (f32[2048,512]{1,0:T(8,128)S(1)}, f32[2048,512]{1,0:T(8,128)}, u32[]{:S(2)}) copy-start(f32[2048,512]{1,0:T(8,128)} %spread.1.owned_hbm.after_ref) | copy-start | bytes 12582916
  73.1 16.9 %copy-start.7 = (s32[1,32]{1,0:T(1,128)S(1)}, s32[1,32]{1,0:T(1,128)}, u32[]{:S(2)}) copy-start(s32[1,32]{1,0:T(1,128)} %counts_ref.1) | copy-start | bytes 388
  73.1 17.0 %copy-start.6 = (s32[1,32,32]{2,1,0:T(8,128)S(1)}, s32[1,32,32]{2,1,0:T(8,128)}, u32[]{:S(2)}) copy-start(s32[1,32,32]{2,1,0:T(8,128)} %param.14) | copy-start | bytes 12292
  73.2 5.6 %collective-permute-start.4 = (bf16[64,512]{1,0:T(8,128)(2,1)S(1)}, bf16[64,512]{1,0:T(8,128)(2,1)S(1)}, u32[]{:S(2)}, u32[]{:S(2)}) collective-permute-start(bf16[64,512]{1,0:T(8,128)(2,1)S(1)} %add.3.refs_0_), channel_id=1, source_target_pairs={{0,8},{8,0},{16,24},{24,16},{1,9},{9,1},{17,25},{25,17},{2,10},{10... | collective-permute-start | bytes 196616 | tf_op jit(solution)/shard_map/ppermute | solution.py:409
  78.7 7.7 %collective-permute-start.5 = (bf16[64,512]{1,0:T(8,128)(2,1)S(1)}, bf16[64,512]{1,0:T(8,128)(2,1)S(1)}, u32[]{:S(2)}, u32[]{:S(2)}) collective-permute-start(bf16[64,512]{1,0:T(8,128)(2,1)S(1)} %add.4.refs_0_), channel_id=1, source_target_pairs={{0,16},{8,24},{16,0},{24,8},{1,17},{9,25},{17,1},{25,9},{2,18},{10... | collective-permute-start | bytes 196616 | tf_op jit(solution)/shard_map/ppermute | solution.py:409
  86.5 4.3 %collective-permute-start.9 = (bf16[64,512]{1,0:T(8,128)(2,1)S(1)}, bf16[64,512]{1,0:T(8,128)(2,1)S(1)}, u32[]{:S(2)}, u32[]{:S(2)}) collective-permute-start(bf16[64,512]{1,0:T(8,128)(2,1)S(1)} %add.5.refs_0_), channel_id=1, source_target_pairs={{0,4},{1,5},{2,6},{3,7},{4,0},{5,1},{6,2},{7,3},{8,12},{9,13},{10,... | collective-permute-start | bytes 196616 | tf_op jit(solution)/shard_map/ppermute | solution.py:409
  88.0 5.5 %collective-permute-start.11 = (bf16[64,512]{1,0:T(8,128)(2,1)S(1)}, bf16[64,512]{1,0:T(8,128)(2,1)S(1)}, u32[]{:S(2)}, u32[]{:S(2)}) collective-permute-start(bf16[64,512]{1,0:T(8,128)(2,1)S(1)} %add.5.refs_0_), channel_id=1, source_target_pairs={{0,6},{1,7},{2,4},{3,5},{4,2},{5,3},{6,0},{7,1},{8,14},{9,15},{10,... | collective-permute-start | bytes 196616 | tf_op jit(solution)/shard_map/ppermute | solution.py:409
  89.5 4.3 %collective-permute-start.7 = (bf16[64,512]{1,0:T(8,128)(2,1)S(1)}, bf16[64,512]{1,0:T(8,128)(2,1)S(1)}, u32[]{:S(2)}, u32[]{:S(2)}) collective-permute-start(bf16[64,512]{1,0:T(8,128)(2,1)S(1)} %add.5.refs_0_), channel_id=1, source_target_pairs={{0,2},{1,3},{2,0},{3,1},{4,6},{5,7},{6,4},{7,5},{8,10},{9,11},{10,... | collective-permute-start | bytes 196616 | tf_op jit(solution)/shard_map/ppermute | solution.py:409
  90.3 8.3 %collective-permute-start.6 = (bf16[64,512]{1,0:T(8,128)(2,1)S(1)}, bf16[64,512]{1,0:T(8,128)(2,1)S(1)}, u32[]{:S(2)}, u32[]{:S(2)}) collective-permute-start(bf16[64,512]{1,0:T(8,128)(2,1)S(1)} %add.5.refs_0_), channel_id=1, source_target_pairs={{0,1},{1,0},{2,3},{3,2},{4,5},{5,4},{6,7},{7,6},{8,9},{9,8},{10,11... | collective-permute-start | bytes 196616 | tf_op jit(solution)/shard_map/ppermute | solution.py:409
  90.8 7.7 %collective-permute-start.10 = (bf16[64,512]{1,0:T(8,128)(2,1)S(1)}, bf16[64,512]{1,0:T(8,128)(2,1)S(1)}, u32[]{:S(2)}, u32[]{:S(2)}) collective-permute-start(bf16[64,512]{1,0:T(8,128)(2,1)S(1)} %collective-permute-done.9.refs_4_), channel_id=1, source_target_pairs={{0,1},{1,0},{2,3},{3,2},{4,5},{5,4},{6,7},{7,6},{8,9},{9,8},{10,11... | collective-permute-start | bytes 196616 | tf_op jit(solution)/shard_map/ppermute | solution.py:409
  93.5 5.1 %collective-permute-start.12 = (bf16[64,512]{1,0:T(8,128)(2,1)S(1)}, bf16[64,512]{1,0:T(8,128)(2,1)S(1)}, u32[]{:S(2)}, u32[]{:S(2)}) collective-permute-start(bf16[64,512]{1,0:T(8,128)(2,1)S(1)} %collective-permute-done.11.refs_6_), channel_id=1, source_target_pairs={{0,1},{1,0},{2,3},{3,2},{4,5},{5,4},{6,7},{7,6},{8,9},{9,8},{10,11... | collective-permute-start | bytes 196616 | tf_op jit(solution)/shard_map/ppermute | solution.py:409
  93.7 4.8 %collective-permute-start.8 = (bf16[64,512]{1,0:T(8,128)(2,1)S(1)}, bf16[64,512]{1,0:T(8,128)(2,1)S(1)}, u32[]{:S(2)}, u32[]{:S(2)}) collective-permute-start(bf16[64,512]{1,0:T(8,128)(2,1)S(1)} %collective-permute-done.7.refs_2_), channel_id=1, source_target_pairs={{0,1},{1,0},{2,3},{3,2},{4,5},{5,4},{6,7},{7,6},{8,9},{9,8},{10,11... | collective-permute-start | bytes 196616 | tf_op jit(solution)/shard_map/ppermute | solution.py:409
  98.6 1.6 %copy-start.1 = (bf16[2048,512]{1,0:T(8,128)(2,1)S(1)}, bf16[2048,512]{1,0:T(8,128)(2,1)}, u32[]{:S(2)}) copy-start(bf16[2048,512]{1,0:T(8,128)(2,1)} %give_back.1.after_ref) | copy-start | bytes 6291460

commit v3 on v2

--- a/solution.py
+++ b/solution.py
@@ -21,7 +21,6 @@
 
 VMEM = pl.BlockSpec(memory_space=pltpu.VMEM)
 SMEM = pl.BlockSpec(memory_space=pltpu.SMEM)
-ANY = pl.BlockSpec(memory_space=pl.ANY)
 HBM = pl.BlockSpec(memory_space=pltpu.MemorySpace.HBM)
 
 
@@ -168,135 +167,128 @@
 
 
 def layer_kernel(
-    me_ref, far_hbm, own_hbm, cot_hbm, w_ref, got_ref,
-    act_hbm, far_ref, slope_ref, mine_ref, other_ref,
-    own, cot, hid, act, sems, sent,
+    far_hbm, own_hbm, cot_hbm, w_ref, got_ref,
+    act_hbm, hid_hbm, slope_hbm, grad_hbm, back_hbm,
+    far, own, cot, act, hid, slope, grad, back, sems, sent,
 ):
     blocks = sems.shape[1]
     views = [pl.ds(n * BIG, BIG) for n in range(blocks)]
 
     def fetch(n):
-        pairs = ((far_hbm, far_ref), (own_hbm, own), (cot_hbm, cot))
+        pairs = ((far_hbm, far), (own_hbm, own), (cot_hbm, cot))
         copies = [pltpu.make_async_copy(a.at[views[n]], b.at[views[n]], sems.at[k, n]) for k, (a, b) in enumerate(pairs)]
         for copy in copies:
             copy.start()
         return copies
 
+    sending = []
+
+    def send(k, n, a, b, at):
+        sending.append(pltpu.make_async_copy(a.at[at], b.at[at], sent.at[k, n]))
+        sending[-1].start()
+
     coming = fetch(0)
-    sending = []
     for n, at in enumerate(views):
         copies = coming
         for copy in copies[:2]:
             copy.wait()
         if n + 1 < blocks:
             coming = fetch(n + 1)
-        hidden = (own[at, :] + dot(far_ref[at, :], got_ref[...])).astype(BF16)
-        hid[at, :] = hidden
-        preact = dot(hidden, w_ref[...])
+        hid[at, :] = (own[at, :] + dot(far[at, :], got_ref[...])).astype(BF16)
+        send(0, n, hid, hid_hbm, at)
+        preact = dot(hid[at, :], w_ref[...])
         copies[2].wait()
         gate = 0.5 + 0.5 * jnp.tanh(0.5 * preact)
         act[at, :] = (preact * gate).astype(BF16)
-        sending.append(pltpu.make_async_copy(act.at[at], act_hbm.at[at], sent.at[n]))
-        sending[n].start()
-        slope = cot[at, :].astype(F32) * gate * (1.0 + preact * (1.0 - gate))
-        slope_ref[at, :] = slope.astype(BF16)
+        send(1, n, act, act_hbm, at)
+        slope[at, :] = (cot[at, :].astype(F32) * gate * (1.0 + preact * (1.0 - gate))).astype(BF16)
+        send(2, n, slope, slope_hbm, at)
+        grad[at, :] = dot(slope[at, :], w_ref[...], ((1,), (1,))).astype(BF16)
+        send(3, n, grad, grad_hbm, at)
+    for n in range(back.shape[0] // BIG):
+        at = pl.ds(n * BIG, BIG)
+        back[at, :] = dot(far[:, at], grad[...], ((0,), (0,))).astype(BF16)
+        send(4, n, back, back_hbm, at)
+    for copy in sending:
+        copy.wait()
+
+
+def layer(keep, far, own, got, cotangent, weight):
+    owned, width = own.shape
+    remote = got.shape[0]
+    blocks = owned // BIG
+    weight, got = held(keep, weight, got)
+    rows = (owned, width)
+    return pl.pallas_call(
+        layer_kernel,
+        in_specs=[HBM, HBM, HBM, VMEM, VMEM],
+        out_specs=[HBM] * 5,
+        out_shape=[far_made(rows, BF16)] * 4 + [far_made(got.shape, BF16)],
+        scratch_shapes=[pltpu.VMEM(far.shape, BF16), pltpu.VMEM(rows, F32)]
+        + [pltpu.VMEM(rows, BF16)] * 5
+        + [
+            pltpu.VMEM(got.shape, BF16),
+            pltpu.SemaphoreType.DMA((3, blocks)),
+            pltpu.SemaphoreType.DMA((5, max(blocks, remote // BIG))),
+        ],
+        compiler_params=params(40 if keep else 60),
+        name="layer",
+    )(*stored(far, own, cotangent), weight, got)
+
+
+def partial_kernel(me_ref, hid_hbm, slope_hbm, mine_ref, other_ref, hid, slope, total, sems):
+    blocks = sems.shape[1]
+    views = [pl.ds(n * BIG, BIG) for n in range(blocks)]
+    coming = [
+        [pltpu.make_async_copy(a.at[at], b.at[at], sems.at[k, n]) for k, (a, b) in enumerate(((hid_hbm, hid), (slope_hbm, slope)))]
+        for n, at in enumerate(views)
+    ]
+    for copies in coming:
+        for copy in copies:
+            copy.start()
+    for n, at in enumerate(views):
+        for copy in coming[n]:
+            copy.wait()
+        part = dot(hid[at, :], slope[at, :], ((0,), (0,)))
+        total[...] = part if n == 0 else total[...] + part
     half = mine_ref.shape[0]
     core = me_ref[0] % 2
     for out_ref, first in ((other_ref, (1 - core) * half), (mine_ref, core * half)):
-        columns = hid[:, pl.ds(pl.multiple_of(first, half), half)]
-        out_ref[...] = dot(columns, slope_ref[...], ((0,), (0,))).astype(out_ref.dtype)
-    for copy in sending:
-        copy.wait()
-
-
-def layer(keep, me, far, own, got, cotangent, weight):
-    owned, width = own.shape
+        out_ref[...] = total[pl.ds(pl.multiple_of(first, half), half), :].astype(out_ref.dtype)
+
+
+def partial_grad(keep, me, hidden, slope):
+    owned, width = hidden.shape
     half = (width // 2, width)
-    blocks = owned // BIG
-    weight, got = held(keep, weight, got)
-    return pl.pallas_call(
-        layer_kernel,
-        in_specs=[SMEM, HBM, HBM, HBM, VMEM, VMEM],
-        out_specs=[HBM, VMEM, VMEM, VMEM, VMEM],
-        out_shape=[
-            far_made((owned, width), BF16),
-            made(keep, far.shape, BF16),
-            made(keep, (owned, width), BF16),
-            made(keep, half, F32),
-            made(keep, half, BF16),
-        ],
+    return pl.pallas_call(
+        partial_kernel,
+        in_specs=[SMEM, HBM, HBM],
+        out_specs=[VMEM, VMEM],
+        out_shape=[made(keep, half, F32), made(keep, half, BF16)],
         scratch_shapes=[
-            pltpu.VMEM((owned, width), F32),
             pltpu.VMEM((owned, width), BF16),
             pltpu.VMEM((owned, width), BF16),
-            pltpu.VMEM((owned, width), BF16),
-            pltpu.SemaphoreType.DMA((3, blocks)),
-            pltpu.SemaphoreType.DMA((blocks,)),
+            pltpu.VMEM((width, width), F32),
+            pltpu.SemaphoreType.DMA((2, owned // BIG)),
         ],
-        compiler_params=params(28 if keep else 60),
-        name="layer",
-    )(me, *stored(far, own, cotangent), weight, got)
-
-
-def grad_kernel(slope_ref, w_ref, grad_ref, grad_hbm, sems):
-    copies = []
-    for n in range(sems.shape[0]):
-        at = pl.ds(n * BIG, BIG)
-        grad_ref[at, :] = dot(slope_ref[at, :], w_ref[...], ((1,), (1,))).astype(BF16)
-        copies.append(pltpu.make_async_copy(grad_ref.at[at], grad_hbm.at[at], sems.at[n]))
-        copies[n].start()
-    for copy in copies:
-        copy.wait()
-
-
-def hidden_grad(keep, slope, weight):
-    return pl.pallas_call(
-        grad_kernel,
-        in_specs=[VMEM] * 2,
-        out_specs=[VMEM, HBM],
-        out_shape=[made(keep, slope.shape, BF16), far_made(slope.shape, BF16)],
-        scratch_shapes=[pltpu.SemaphoreType.DMA((slope.shape[0] // BIG,))],
-        compiler_params=params(12 if keep else 40),
-        name="hidden_grad",
-    )(*held(keep, slope, weight))
-
-
-def back_kernel(far_ref, grad_ref, after_ref, out_hbm, out, sems):
-    copies = []
-    for n in range(sems.shape[0]):
-        at = pl.ds(n * BIG, BIG)
-        out[at, :] = dot(far_ref[:, at], grad_ref[...], ((0,), (0,))).astype(BF16)
-        copies.append(pltpu.make_async_copy(out.at[at], out_hbm.at[at], sems.at[n]))
-        copies[n].start()
-    for copy in copies:
-        copy.wait()
-
-
-def back_rows(keep, far, grad, after):
-    shape = (far.shape[1], grad.shape[1])
-    return pl.pallas_call(
-        back_kernel,
-        in_specs=[VMEM, VMEM, ANY],
-        out_specs=HBM,
-        out_shape=far_made(shape, BF16),
-        scratch_shapes=[pltpu.VMEM(shape, BF16), pltpu.SemaphoreType.DMA((shape[0] // BIG,))],
-        compiler_params=params(16 if keep else 60),
-        name="back_rows",
-    )(*held(keep, far, grad), after)
+        compiler_params=params(20),
+        name="partial_grad",
+    )(me, *stored(hidden, slope))
 
 
 def spread_kernel(adj_ref, grad_ref, out_ref):
     out_ref[...] = dot(adj_ref[...], grad_ref[...], ((0,), (0,)))
 
 
-def spread(adjacency, grad):
+def spread(adjacency, grad, part, parts):
     owned, width = grad.shape
+    blocks = owned // BIG // parts
     return pl.pallas_call(
         spread_kernel,
-        grid=(owned // BIG,),
-        in_specs=[pl.BlockSpec((owned, BIG), lambda i: (0, i)), whole(grad.shape)],
+        grid=(blocks,),
+        in_specs=[pl.BlockSpec((owned, BIG), lambda i: (0, i + part * blocks)), whole(grad.shape)],
         out_specs=pl.BlockSpec((BIG, width), lambda i: (i, 0)),
-        out_shape=far_made((owned, width), F32),
+        out_shape=far_made((owned // parts, width), F32),
         compiler_params=params(60),
         cost_estimate=pl.CostEstimate(
             flops=2 * owned * owned * width, bytes_accessed=16 * 1024 * 1024, transcendentals=0
@@ -305,10 +297,13 @@
     )(*stored(adjacency, grad))
 
 
-def return_kernel(index_ref, owned_hbm, got_ref, out_hbm, owned, out, sems, sent):
+def return_kernel(index_ref, first_hbm, second_hbm, got_ref, out_hbm, owned, out, sems, sent):
     blocks = sems.shape[0]
     views = [pl.ds(n * BIG, BIG) for n in range(blocks)]
-    coming = [pltpu.make_async_copy(owned_hbm.at[at], owned.at[at], sems.at[n]) for n, at in enumerate(views)]
+    coming = []
+    for n, at in enumerate(views):
+        half_hbm = (first_hbm, second_hbm)[2 * n // blocks]
+        coming.append(pltpu.make_async_copy(half_hbm.at[views[n % (blocks // 2)]], owned.at[at], sems.at[n]))
     for copy in coming:
         copy.start()
 
@@ -327,12 +322,12 @@
         copy.wait()
 
 
-def give_back(keep, index, owned, got):
-    rows, width = owned.shape
+def give_back(keep, index, first, second, got):
+    rows, width = 2 * first.shape[0], first.shape[1]
     (got,) = held(keep, got)
     return pl.pallas_call(
         return_kernel,
-        in_specs=[VMEM, HBM, VMEM],
+        in_specs=[VMEM, HBM, HBM, VMEM],
         out_specs=HBM,
         out_shape=far_made((rows, width), BF16),
         scratch_shapes=[
@@ -343,7 +338,7 @@
         ],
         compiler_params=params(28 if keep else 60),
         name="give_back",
-    )(index, *stored(owned), got)
+    )(index, *stored(first, second), got)
 
 
 def exchange(x, axes):
@@ -368,7 +363,7 @@
     )(me, mine, got)
 
 
-def join_kernel(me_ref, after_ref, *refs):
+def join_kernel(me_ref, *refs):
     in_refs, out_ref = refs[:-1], refs[-1]
     height, half = in_refs[0].shape[0], out_ref.shape[0] // 2
     for k, in_ref in enumerate(in_refs):
@@ -377,15 +372,15 @@
         out_ref[pl.ds(at, height), :] = in_ref[...].astype(F32)
 
 
-def join(me, after, parts):
+def join(me, parts):
     height, width = parts[0].shape
     return pl.pallas_call(
         join_kernel,
-        in_specs=[SMEM, ANY] + [VMEM] * len(parts),
+        in_specs=[SMEM] + [VMEM] * len(parts),
         out_shape=jax.ShapeDtypeStruct((height * len(parts), width), F32),
         compiler_params=params(8),
         name="join",
-    )(me, after, *parts)
+    )(me, *parts)
 
 
 def add_kernel(after_ref, *refs):
@@ -398,11 +393,11 @@
 def add(after, parts):
     return pl.pallas_call(
         add_kernel,
-        in_specs=[ANY] + [VMEM] * len(parts),
+        in_specs=[HBM] + [VMEM] * len(parts),
         out_shape=jax.ShapeDtypeStruct(parts[0].shape, BF16),
         compiler_params=params(8),
         name="add",
-    )(after, *parts)
+    )(*stored(after), *parts)
 
 
 def swap(x, axis, size, k):
@@ -419,25 +414,25 @@
     outgoing = collect(counts, lists, features)
     arrived = exchange(outgoing.reshape(peers, slots, width), AXES).reshape(remote, width)
     adjacency, far, own = build(tile_rows, tile_cols, tile_vals, features, remote)
-    activated, far, slope, mine, other = layer(keep, me, far, own, arrived, cotangent, weight)
+    activated, hidden, slope, grad, back = layer(keep, far, own, arrived, cotangent, weight)
+    returned = exchange(back.reshape(peers, slots, width), AXES).reshape(remote, width)
+    first = spread(adjacency, grad, 0, 2)
+    second = spread(adjacency, grad, 1, 2)
+    live = jnp.arange(slots)[None, :] < counts[0][:, None]
+    feature_grad = give_back(keep, jnp.where(live, lists, -1).reshape(1, remote), first, second, returned)
     chips = locals_ // 2
+    mine, other = partial_grad(keep, me, hidden, slope)
     pieces = cut(me, mine, swap(other, "local", locals_, 1), chips)
-    grad, grad_out = hidden_grad(keep, slope, weight)
-    back = back_rows(keep, far, grad, pieces[-1])
-    returned = exchange(back.reshape(peers, slots, width), AXES).reshape(remote, width)
-    owned = spread(adjacency, grad_out)
-    piece = add(owned, [pieces[0]] + [swap(pieces[k], "local", locals_, 2 * k) for k in range(1, chips)])
-    step = 1
-    while step < groups:
-        piece = add(me, [piece, swap(piece, "group", groups, step)])
-        step *= 2
+    piece = add(first, [pieces[0]] + [swap(pieces[k], "local", locals_, 2 * k) for k in range(1, chips)])
+    step, after = groups // 2, second
+    while step:
+        piece = add(after, [piece, swap(piece, "group", groups, step)])
+        step, after = step // 2, feature_grad
     gathered = []
     for k in range(chips):
         mine = swap(piece, "local", locals_, 2 * k) if k else piece
         gathered += [mine, swap(mine, "local", locals_, 1)]
-    live = jnp.arange(slots)[None, :] < counts[0][:, None]
-    feature_grad = give_back(keep, jnp.where(live, lists, -1).reshape(1, remote), owned, returned)
-    return activated, feature_grad, join(me, feature_grad, gathered)
+    return activated, feature_grad, join(me, gathered)
 
 
 def solution(mesh):

time: 102 us -> 99.6 us (0.976)
  local copies, waits for them, and re-layouts: 5.55 us -> 1.24 us
  Pallas kernels: 53.8 us -> 56.6 us
    unnamed x16 -> x12, local copies, waits for them, and re-layouts: 5.38 us -> 1.07 us
    pallas_call x9, Pallas kernels: 29.1 us -> 31.9 us  [the longest x1 11.8 us: layer(): pl.pallas_call(layer_kernel, in_specs=[HBM, HBM, HBM, VMEM, VMEM], out_sp...]
    all_to_all x2, waiting for transfers between devices: 5.09 us -> 6.68 us  [exchange(): return lax.all_to_all(x, axes, split_axis=0, concat_axis=0, tiled=True)]
    ppermute x13, waiting for transfers between devices: 13.9 us -> 12.4 us  [swap(): return lax.ppermute(x, axis, [(i, i ^ k) for i in range(size)])]
  transfers between devices with their start and end apart: 15 -> 15, of which waited for: 7 -> 9; matrix products, arithmetic and copies ran while one was open for 0% -> 0% of each run, Pallas kernels for 35% -> 39%
where the time goes in v3:
time: 99.6 us; the launch traced here: 99.1 us
  Pallas kernels  56.6 us (57%)
  starting transfers between devices  21.3 us (21%)
  waiting for transfers between devices  19 us (19%)
  local copies, waits for them, and re-layouts  1.24 us (1%)
    pallas_call x1, Pallas kernels, build(): pl.pallas_call(build_kernel, grid_spec=pltpu.PrefetchScalarGridSpec(num_s...  19.5 us
    ppermute x13, waiting for transfers between devices, swap(): return lax.ppermute(x, axis, [(i, i ^ k) for i in range(size)])  12.4 us
    pallas_call x1, Pallas kernels, layer(): pl.pallas_call(layer_kernel, in_specs=[HBM, HBM, HBM, VMEM, VMEM], out_sp...  11.8 us
    pallas_call x2, Pallas kernels, spread(): pl.pallas_call(spread_kernel, grid=(blocks,), in_specs=[pl.BlockSpec((own...  11.6 us
    all_to_all x2, starting transfers between devices, exchange(): return lax.all_to_all(x, axes, split_axis=0, concat_axis=0, tiled=True)  11.1 us
    ppermute x13, starting transfers between devices, swap(): return lax.ppermute(x, axis, [(i, i ^ k) for i in range(size)])  10.2 us
    all_to_all x2, waiting for transfers between devices, exchange(): return lax.all_to_all(x, axes, split_axis=0, concat_axis=0, tiled=True)  6.68 us
    pallas_call x1, Pallas kernels, collect(): pl.pallas_call(collect_kernel, in_specs=[SMEM, VMEM, VMEM], out_shape=jax...  5.17 us
  transfers between devices with their start and end apart: 15, of which 9 were waited for; matrix products, arithmetic and copies ran while one was open for 0% of the time, Pallas kernels for 39%

profile of v3, /device:TPU:0, one launch (start us, length us, event | category | flops | bytes accessed | tf_op | source)
XLA Modules:
  0.0 99.1 jit_solution(4249473349622666597)
XLA Ops:
  0.7 5.2 %collect.1 = bf16[1024,512]{1,0:T(8,128)(2,1)} custom-call(s32[1,32]{1,0:T(1,128)} %counts_ref.1, s32[32,32]{1,0:T(8,128)} %bitcast.11, bf16[2048,512]{1,0:T(8,128)(2,1)} %x_ref.3), custom_call_target="tpu_custom_call" | custom-call | tf_op jit(solution)/shard_map/collect/pallas_call | solution.py:70
  5.8 7.3 %all-to-all-start = ((bf16[32,32,512]{2,1,0:T(8,128)(2,1)}), bf16[32,32,512]{2,1,0:T(8,128)(2,1)S(1)}, u32[]{:S(2)}, u32[]{:S(2)}) async-start(bf16[32,32,512]{2,1,0:T(8,128)(2,1)} %bitcast.9), calls=%async_computation | async-start | bytes 2097152 | tf_op jit(solution)/shard_map/all_to_all | solution.py:345
  13.2 19.5 %build.1 = (bf16[2048,2048]{1,0:T(8,128)(2,1)}, bf16[2048,1024]{1,0:T(8,128)(2,1)}, f32[2048,512]{1,0:T(8,128)}) custom-call(s32[256]{0:T(256)S(1)} %copy-done.2, s32[256]{0:T(256)S(1)} %copy-done.3, bf16[256,128,128]{2,1,0:T(8,128)(2,1)} %tiles_ref.1, bf16[2048,512]{1,0:T(8,128)(2,1)S(1)} %copy-done), custom_call_target="tpu_custom_call" | custom-call | flops 4294967296 | bytes 41943040 | tf_op jit(solution)/shard_map/build/pallas_call | solution.py:138
  32.7 6.7 %all-to-all-done = bf16[32,32,512]{2,1,0:T(8,128)(2,1)S(1)} async-done(((bf16[32,32,512]{2,1,0:T(8,128)(2,1)}), bf16[32,32,512]{2,1,0:T(8,128)(2,1)S(1)}, u32[]{:S(2)}, u32[]{:S(2)}) %all-to-all-start) | async-done | bytes 1048608 | tf_op jit(solution)/shard_map/all_to_all | solution.py:345
  39.4 1.0 %copy-done.1 = bf16[512,512]{1,0:T(8,128)(2,1)S(1)} copy-done((bf16[512,512]{1,0:T(8,128)(2,1)S(1)}, bf16[512,512]{1,0:T(8,128)(2,1)}, u32[]{:S(2)}) %copy-start.1) | copy-done | bytes 524312
  40.4 11.8 %layer.1 = (bf16[2048,512]{1,0:T(8,128)(2,1)}, bf16[2048,512]{1,0:T(8,128)(2,1)}, bf16[2048,512]{1,0:T(8,128)(2,1)}, bf16[2048,512]{1,0:T(8,128)(2,1)}, bf16[1024,512]{1,0:T(8,128)(2,1)}) custom-call(bf16[2048,1024]{1,0:T(8,128)(2,1)} %get-tuple-element.17.far_hbm, f32[2048,512]{1,0:T(8,128)} %get-tuple-element.18.own_hbm, bf16[2048,512]{1,0:T(8,128)(2,1)} %cot_hbm.1, ...), custom_call_target="tpu_custom_call" | custom-call | tf_op jit(solution)/shard_map/layer/pallas_call | solution.py:222
  52.2 3.8 %all-to-all-start.1 = ((bf16[32,32,512]{2,1,0:T(8,128)(2,1)}), bf16[32,32,512]{2,1,0:T(8,128)(2,1)S(1)}, u32[]{:S(2)}, u32[]{:S(2)}) async-start(bf16[32,32,512]{2,1,0:T(8,128)(2,1)} %bitcast.10), calls=%async_computation.1 | async-start | bytes 2097152 | tf_op jit(solution)/shard_map/all_to_all | solution.py:345
  56.0 2.9 %partial_grad.1 = (f32[256,512]{1,0:T(8,128)S(1)}, bf16[256,512]{1,0:T(8,128)(2,1)S(1)}) custom-call(s32[1]{0:T(128)} %bitcast.6.me_ref, bf16[2048,512]{1,0:T(8,128)(2,1)} %get-tuple-element.23.hid_hbm, bf16[2048,512]{1,0:T(8,128)(2,1)} %get-tuple-element.24.slope_hbm), custom_call_target="tpu_custom_call" | custom-call | tf_op jit(solution)/shard_map/partial_grad/pallas_call | solution.py:263
  58.9 0.1 collective-permute-start
  59.1 0.1 squeeze.6
  59.1 0.1 iota_compare_fusion
  59.2 0.1 lt.29
  59.3 1.2 %collective-permute-done.got_ref = bf16[256,512]{1,0:T(8,128)(2,1)S(1)} collective-permute-done((bf16[256,512]{1,0:T(8,128)(2,1)S(1)}, bf16[256,512]{1,0:T(8,128)(2,1)S(1)}, u32[]{:S(2)}, u32[]{:S(2)}) %collective-permute-start) | collective-permute-done | bytes 262176 | tf_op jit(solution)/shard_map/ppermute | solution.py:404
  60.6 1.7 %collective-permute-start.1 = (bf16[64,512]{1,0:T(8,128)(2,1)S(1)}, bf16[64,512]{1,0:T(8,128)(2,1)S(1)}, u32[]{:S(2)}, u32[]{:S(2)}) collective-permute-start(bf16[64,512]{1,0:T(8,128)(2,1)S(1)} %get-tuple-element.28), channel_id=1, source_target_pairs={{0,2},{1,3},{2,0},{3,1},{4,6},{5,7},{6,4},{7,5},{8,10},{9,11},{10,... | collective-permute-start | bytes 196616 | tf_op jit(solution)/shard_map/ppermute | solution.py:404
  62.2 1.5 %collective-permute-start.2 = (bf16[64,512]{1,0:T(8,128)(2,1)S(1)}, bf16[64,512]{1,0:T(8,128)(2,1)S(1)}, u32[]{:S(2)}, u32[]{:S(2)}) collective-permute-start(bf16[64,512]{1,0:T(8,128)(2,1)S(1)} %get-tuple-element.29), channel_id=1, source_target_pairs={{0,4},{1,5},{2,6},{3,7},{4,0},{5,1},{6,2},{7,3},{8,12},{9,13},{10,... | collective-permute-start | bytes 196616 | tf_op jit(solution)/shard_map/ppermute | solution.py:404
  63.7 0.4 collective-permute-start.3
  64.1 5.8 %spread.2.first_hbm.after_ref = f32[1024,512]{1,0:T(8,128)} custom-call(bf16[2048,2048]{1,0:T(8,128)(2,1)} %get-tuple-element.20.adj_ref, bf16[2048,512]{1,0:T(8,128)(2,1)} %get-tuple-element.21.grad_ref), custom_call_target="tpu_custom_call" | custom-call | flops 4294967296 | bytes 16777216 | tf_op jit(solution)/shard_map/spread/pallas_call | solution.py:286
  69.9 0.9 collective-permute-done.3.refs_3_
  70.9 2.6 %collective-permute-start.4 = (bf16[64,512]{1,0:T(8,128)(2,1)S(1)}, bf16[64,512]{1,0:T(8,128)(2,1)S(1)}, u32[]{:S(2)}, u32[]{:S(2)}) collective-permute-start(bf16[64,512]{1,0:T(8,128)(2,1)S(1)} %add.3.refs_0_), channel_id=1, source_target_pairs={{0,16},{8,24},{16,0},{24,8},{1,17},{9,25},{17,1},{25,9},{2,18},{10... | collective-permute-start | bytes 196616 | tf_op jit(solution)/shard_map/ppermute | solution.py:404
  73.5 5.8 %spread.3.second_hbm.after_ref = f32[1024,512]{1,0:T(8,128)} custom-call(bf16[2048,2048]{1,0:T(8,128)(2,1)} %get-tuple-element.20.adj_ref, bf16[2048,512]{1,0:T(8,128)(2,1)} %get-tuple-element.21.grad_ref), custom_call_target="tpu_custom_call" | custom-call | flops 4294967296 | bytes 16777216 | tf_op jit(solution)/shard_map/spread/pallas_call | solution.py:286
  79.3 5.5 %collective-permute-done.4.refs_1_ = bf16[64,512]{1,0:T(8,128)(2,1)S(1)} collective-permute-done((bf16[64,512]{1,0:T(8,128)(2,1)S(1)}, bf16[64,512]{1,0:T(8,128)(2,1)S(1)}, u32[]{:S(2)}, u32[]{:S(2)}) %collective-permute-start.4) | collective-permute-done | bytes 65568 | tf_op jit(solution)/shard_map/ppermute | solution.py:404
  85.0 4.5 %give_back.1.after_ref = bf16[2048,512]{1,0:T(8,128)(2,1)} custom-call(s32[1,1024]{1,0:T(1,128)S(1)} %broadcast_select_fusion.index_ref, f32[1024,512]{1,0:T(8,128)} %spread.2.first_hbm.after_ref, f32[1024,512]{1,0:T(8,128)} %spread.3.second_hbm.after_ref, bf16[1024,512]{1,0:T(8,128)(2,1)S(1)} %bitcast.7), custom_call_target="tpu_custom_call" | custom-call | tf_op jit(solution)/shard_map/give_back/pallas_call | solution.py:328
  89.6 1.5 %collective-permute-start.9 = (bf16[64,512]{1,0:T(8,128)(2,1)S(1)}, bf16[64,512]{1,0:T(8,128)(2,1)S(1)}, u32[]{:S(2)}, u32[]{:S(2)}) collective-permute-start(bf16[64,512]{1,0:T(8,128)(2,1)S(1)} %add.5.refs_0_), channel_id=1, source_target_pairs={{0,4},{1,5},{2,6},{3,7},{4,0},{5,1},{6,2},{7,3},{8,12},{9,13},{10,... | collective-permute-start | bytes 196616 | tf_op jit(solution)/shard_map/ppermute | solution.py:404
  91.1 1.4 %collective-permute-start.11 = (bf16[64,512]{1,0:T(8,128)(2,1)S(1)}, bf16[64,512]{1,0:T(8,128)(2,1)S(1)}, u32[]{:S(2)}, u32[]{:S(2)}) collective-permute-start(bf16[64,512]{1,0:T(8,128)(2,1)S(1)} %add.5.refs_0_), channel_id=1, source_target_pairs={{0,6},{1,7},{2,4},{3,5},{4,2},{5,3},{6,0},{7,1},{8,14},{9,15},{10,... | collective-permute-start | bytes 196616 | tf_op jit(solution)/shard_map/ppermute | solution.py:404
  92.5 0.6 collective-permute-start.7
  93.1 0.8 collective-permute-done.9.refs_4_
  93.9 2.7 %collective-permute-done.11.refs_6_ = bf16[64,512]{1,0:T(8,128)(2,1)S(1)} collective-permute-done((bf16[64,512]{1,0:T(8,128)(2,1)S(1)}, bf16[64,512]{1,0:T(8,128)(2,1)S(1)}, u32[]{:S(2)}, u32[]{:S(2)}) %collective-permute-start.11) | collective-permute-done | bytes 65568 | tf_op jit(solution)/shard_map/ppermute | solution.py:404
  96.6 0.3 collective-permute-done.7.refs_2_
  96.8 0.3 collective-permute-start.8
  97.1 0.7 collective-permute-done.12.refs_7_
  97.8 0.3 collective-permute-done.8.refs_3_
  98.1 1.0 %join.1 = f32[512,512]{1,0:T(8,128)} custom-call(s32[1]{0:T(128)} %bitcast.6.me_ref, bf16[64,512]{1,0:T(8,128)(2,1)S(1)} %add.5.refs_0_, bf16[64,512]{1,0:T(8,128)(2,1)S(1)} %collective-permute-done.6.refs_1_, bf16[64,512]{1,0:T(8,128)(2,1)S(1)} %collective-permute-done.7.refs_2_, bf16[64,512]{1,0:T(8,128)(2,1)S(1)} %collective-permute-done.8.refs_3_, ...), custom_call_target="tpu_custom_call" | custom-call | tf_op jit(solution)/shard_map/join/pallas_call | solution.py:377
  (26 shorter events, 0.2 us)
Async XLA Ops:
  0.6 12.5 %copy-start = (bf16[2048,512]{1,0:T(8,128)(2,1)S(1)}, bf16[2048,512]{1,0:T(8,128)(2,1)}, u32[]{:S(2)}) copy-start(bf16[2048,512]{1,0:T(8,128)(2,1)} %x_ref.3) | copy-start | bytes 6291460
  0.6 12.5 %copy-start.2 = (s32[256]{0:T(256)S(1)}, s32[256]{0:T(256)}, u32[]{:S(2)}) copy-start(s32[256]{0:T(256)} %rows_ref.1) | copy-start | bytes 3076
  0.7 12.5 %copy-start.3 = (s32[256]{0:T(256)S(1)}, s32[256]{0:T(256)}, u32[]{:S(2)}) copy-start(s32[256]{0:T(256)} %cols_ref.1) | copy-start | bytes 3076
  5.8 33.5 %all-to-all-start = ((bf16[32,32,512]{2,1,0:T(8,128)(2,1)}), bf16[32,32,512]{2,1,0:T(8,128)(2,1)S(1)}, u32[]{:S(2)}, u32[]{:S(2)}) async-start(bf16[32,32,512]{2,1,0:T(8,128)(2,1)} %bitcast.9), calls=%async_computation | async-start | bytes 2097152 | tf_op jit(solution)/shard_map/all_to_all | solution.py:345
  39.4 1.0 %copy-start.1 = (bf16[512,512]{1,0:T(8,128)(2,1)S(1)}, bf16[512,512]{1,0:T(8,128)(2,1)}, u32[]{:S(2)}) copy-start(bf16[512,512]{1,0:T(8,128)(2,1)} %w_ref.1) | copy-start | bytes 1572868
  52.2 32.8 %all-to-all-start.1 = ((bf16[32,32,512]{2,1,0:T(8,128)(2,1)}), bf16[32,32,512]{2,1,0:T(8,128)(2,1)S(1)}, u32[]{:S(2)}, u32[]{:S(2)}) async-start(bf16[32,32,512]{2,1,0:T(8,128)(2,1)} %bitcast.10), calls=%async_computation.1 | async-start | bytes 2097152 | tf_op jit(solution)/shard_map/all_to_all | solution.py:345
  56.0 3.1 %copy-start.4 = (s32[1,32,32]{2,1,0:T(8,128)S(1)}, s32[1,32,32]{2,1,0:T(8,128)}, u32[]{:S(2)}) copy-start(s32[1,32,32]{2,1,0:T(8,128)} %param.14) | copy-start | bytes 12292
  56.0 3.1 %copy-start.5 = (s32[1,32]{1,0:T(1,128)S(1)}, s32[1,32]{1,0:T(1,128)}, u32[]{:S(2)}) copy-start(s32[1,32]{1,0:T(1,128)} %counts_ref.1) | copy-start | bytes 388
  58.9 1.6 %collective-permute-start = (bf16[256,512]{1,0:T(8,128)(2,1)S(1)}, bf16[256,512]{1,0:T(8,128)(2,1)S(1)}, u32[]{:S(2)}, u32[]{:S(2)}) collective-permute-start(bf16[256,512]{1,0:T(8,128)(2,1)S(1)} %get-tuple-element.26), channel_id=1, source_target_pairs={{0,1},{1,0},{2,3},{3,2},{4,5},{5,4},{6,7},{7,6},{8,9},{9,8},{10,11... | collective-permute-start | bytes 786440 | tf_op jit(solution)/shard_map/ppermute | solution.py:404
  60.6 9.4 %collective-permute-start.1 = (bf16[64,512]{1,0:T(8,128)(2,1)S(1)}, bf16[64,512]{1,0:T(8,128)(2,1)S(1)}, u32[]{:S(2)}, u32[]{:S(2)}) collective-permute-start(bf16[64,512]{1,0:T(8,128)(2,1)S(1)} %get-tuple-element.28), channel_id=1, source_target_pairs={{0,2},{1,3},{2,0},{3,1},{4,6},{5,7},{6,4},{7,5},{8,10},{9,11},{10,... | collective-permute-start | bytes 196616 | tf_op jit(solution)/shard_map/ppermute | solution.py:404
  62.2 7.7 %collective-permute-start.2 = (bf16[64,512]{1,0:T(8,128)(2,1)S(1)}, bf16[64,512]{1,0:T(8,128)(2,1)S(1)}, u32[]{:S(2)}, u32[]{:S(2)}) collective-permute-start(bf16[64,512]{1,0:T(8,128)(2,1)S(1)} %get-tuple-element.29), channel_id=1, source_target_pairs={{0,4},{1,5},{2,6},{3,7},{4,0},{5,1},{6,2},{7,3},{8,12},{9,13},{10,... | collective-permute-start | bytes 196616 | tf_op jit(solution)/shard_map/ppermute | solution.py:404
  63.7 7.1 %collective-permute-start.3 = (bf16[64,512]{1,0:T(8,128)(2,1)S(1)}, bf16[64,512]{1,0:T(8,128)(2,1)S(1)}, u32[]{:S(2)}, u32[]{:S(2)}) collective-permute-start(bf16[64,512]{1,0:T(8,128)(2,1)S(1)} %get-tuple-element.30), channel_id=1, source_target_pairs={{0,6},{1,7},{2,4},{3,5},{4,2},{5,3},{6,0},{7,1},{8,14},{9,15},{10,... | collective-permute-start | bytes 196616 | tf_op jit(solution)/shard_map/ppermute | solution.py:404
  70.9 14.0 %collective-permute-start.4 = (bf16[64,512]{1,0:T(8,128)(2,1)S(1)}, bf16[64,512]{1,0:T(8,128)(2,1)S(1)}, u32[]{:S(2)}, u32[]{:S(2)}) collective-permute-start(bf16[64,512]{1,0:T(8,128)(2,1)S(1)} %add.3.refs_0_), channel_id=1, source_target_pairs={{0,16},{8,24},{16,0},{24,8},{1,17},{9,25},{17,1},{25,9},{2,18},{10... | collective-permute-start | bytes 196616 | tf_op jit(solution)/shard_map/ppermute | solution.py:404
  84.9 4.6 %collective-permute-start.5 = (bf16[64,512]{1,0:T(8,128)(2,1)S(1)}, bf16[64,512]{1,0:T(8,128)(2,1)S(1)}, u32[]{:S(2)}, u32[]{:S(2)}) collective-permute-start(bf16[64,512]{1,0:T(8,128)(2,1)S(1)} %add.4.refs_0_), channel_id=1, source_target_pairs={{0,8},{8,0},{16,24},{24,16},{1,9},{9,1},{17,25},{25,17},{2,10},{10... | collective-permute-start | bytes 196616 | tf_op jit(solution)/shard_map/ppermute | solution.py:404
  89.6 4.3 %collective-permute-start.9 = (bf16[64,512]{1,0:T(8,128)(2,1)S(1)}, bf16[64,512]{1,0:T(8,128)(2,1)S(1)}, u32[]{:S(2)}, u32[]{:S(2)}) collective-permute-start(bf16[64,512]{1,0:T(8,128)(2,1)S(1)} %add.5.refs_0_), channel_id=1, source_target_pairs={{0,4},{1,5},{2,6},{3,7},{4,0},{5,1},{6,2},{7,3},{8,12},{9,13},{10,... | collective-permute-start | bytes 196616 | tf_op jit(solution)/shard_map/ppermute | solution.py:404
  91.1 5.5 %collective-permute-start.11 = (bf16[64,512]{1,0:T(8,128)(2,1)S(1)}, bf16[64,512]{1,0:T(8,128)(2,1)S(1)}, u32[]{:S(2)}, u32[]{:S(2)}) collective-permute-start(bf16[64,512]{1,0:T(8,128)(2,1)S(1)} %add.5.refs_0_), channel_id=1, source_target_pairs={{0,6},{1,7},{2,4},{3,5},{4,2},{5,3},{6,0},{7,1},{8,14},{9,15},{10,... | collective-permute-start | bytes 196616 | tf_op jit(solution)/shard_map/ppermute | solution.py:404
  92.5 4.3 %collective-permute-start.7 = (bf16[64,512]{1,0:T(8,128)(2,1)S(1)}, bf16[64,512]{1,0:T(8,128)(2,1)S(1)}, u32[]{:S(2)}, u32[]{:S(2)}) collective-permute-start(bf16[64,512]{1,0:T(8,128)(2,1)S(1)} %add.5.refs_0_), channel_id=1, source_target_pairs={{0,2},{1,3},{2,0},{3,1},{4,6},{5,7},{6,4},{7,5},{8,10},{9,11},{10,... | collective-permute-start | bytes 196616 | tf_op jit(solution)/shard_map/ppermute | solution.py:404
  93.1 4.0 %collective-permute-start.6 = (bf16[64,512]{1,0:T(8,128)(2,1)S(1)}, bf16[64,512]{1,0:T(8,128)(2,1)S(1)}, u32[]{:S(2)}, u32[]{:S(2)}) collective-permute-start(bf16[64,512]{1,0:T(8,128)(2,1)S(1)} %add.5.refs_0_), channel_id=1, source_target_pairs={{0,1},{1,0},{2,3},{3,2},{4,5},{5,4},{6,7},{7,6},{8,9},{9,8},{10,11... | collective-permute-start | bytes 196616 | tf_op jit(solution)/shard_map/ppermute | solution.py:404
  93.9 3.2 %collective-permute-start.10 = (bf16[64,512]{1,0:T(8,128)(2,1)S(1)}, bf16[64,512]{1,0:T(8,128)(2,1)S(1)}, u32[]{:S(2)}, u32[]{:S(2)}) collective-permute-start(bf16[64,512]{1,0:T(8,128)(2,1)S(1)} %collective-permute-done.9.refs_4_), channel_id=1, source_target_pairs={{0,1},{1,0},{2,3},{3,2},{4,5},{5,4},{6,7},{7,6},{8,9},{9,8},{10,11... | collective-permute-start | bytes 196616 | tf_op jit(solution)/shard_map/ppermute | solution.py:404
  96.6 1.3 %collective-permute-start.12 = (bf16[64,512]{1,0:T(8,128)(2,1)S(1)}, bf16[64,512]{1,0:T(8,128)(2,1)S(1)}, u32[]{:S(2)}, u32[]{:S(2)}) collective-permute-start(bf16[64,512]{1,0:T(8,128)(2,1)S(1)} %collective-permute-done.11.refs_6_), channel_id=1, source_target_pairs={{0,1},{1,0},{2,3},{3,2},{4,5},{5,4},{6,7},{7,6},{8,9},{9,8},{10,11... | collective-permute-start | bytes 196616 | tf_op jit(solution)/shard_map/ppermute | solution.py:404
  96.8 1.3 %collective-permute-start.8 = (bf16[64,512]{1,0:T(8,128)(2,1)S(1)}, bf16[64,512]{1,0:T(8,128)(2,1)S(1)}, u32[]{:S(2)}, u32[]{:S(2)}) collective-permute-start(bf16[64,512]{1,0:T(8,128)(2,1)S(1)} %collective-permute-done.7.refs_2_), channel_id=1, source_target_pairs={{0,1},{1,0},{2,3},{3,2},{4,5},{5,4},{6,7},{7,6},{8,9},{9,8},{10,11... | collective-permute-start | bytes 196616 | tf_op jit(solution)/shard_map/ppermute | solution.py:404

commit v4 on v3

--- a/solution.py
+++ b/solution.py
@@ -167,9 +167,9 @@
 
 
 def layer_kernel(
-    far_hbm, own_hbm, cot_hbm, w_ref, got_ref,
+    far_hbm, own_hbm, cot_hbm, w_hbm, got_ref,
     act_hbm, hid_hbm, slope_hbm, grad_hbm, back_hbm,
-    far, own, cot, act, hid, slope, grad, back, sems, sent,
+    far, own, cot, act, hid, slope, grad, w, back, sems, sent, w_sem,
 ):
     blocks = sems.shape[1]
     views = [pl.ds(n * BIG, BIG) for n in range(blocks)]
@@ -188,6 +188,8 @@
         sending[-1].start()
 
     coming = fetch(0)
+    weight = pltpu.make_async_copy(w_hbm, w, w_sem)
+    weight.start()
     for n, at in enumerate(views):
         copies = coming
         for copy in copies[:2]:
@@ -196,14 +198,16 @@
             coming = fetch(n + 1)
         hid[at, :] = (own[at, :] + dot(far[at, :], got_ref[...])).astype(BF16)
         send(0, n, hid, hid_hbm, at)
-        preact = dot(hid[at, :], w_ref[...])
         copies[2].wait()
+        if n == 0:
+            weight.wait()
+        preact = dot(hid[at, :], w[...])
         gate = 0.5 + 0.5 * jnp.tanh(0.5 * preact)
         act[at, :] = (preact * gate).astype(BF16)
         send(1, n, act, act_hbm, at)
         slope[at, :] = (cot[at, :].astype(F32) * gate * (1.0 + preact * (1.0 - gate))).astype(BF16)
         send(2, n, slope, slope_hbm, at)
-        grad[at, :] = dot(slope[at, :], w_ref[...], ((1,), (1,))).astype(BF16)
+        grad[at, :] = dot(slope[at, :], w[...], ((1,), (1,))).astype(BF16)
         send(3, n, grad, grad_hbm, at)
     for n in range(back.shape[0] // BIG):
         at = pl.ds(n * BIG, BIG)
@@ -217,23 +221,25 @@
     owned, width = own.shape
     remote = got.shape[0]
     blocks = owned // BIG
-    weight, got = held(keep, weight, got)
+    (got,) = held(keep, got)
     rows = (owned, width)
     return pl.pallas_call(
         layer_kernel,
-        in_specs=[HBM, HBM, HBM, VMEM, VMEM],
+        in_specs=[HBM] * 4 + [VMEM],
         out_specs=[HBM] * 5,
         out_shape=[far_made(rows, BF16)] * 4 + [far_made(got.shape, BF16)],
         scratch_shapes=[pltpu.VMEM(far.shape, BF16), pltpu.VMEM(rows, F32)]
         + [pltpu.VMEM(rows, BF16)] * 5
         + [
+            pltpu.VMEM(weight.shape, BF16),
             pltpu.VMEM(got.shape, BF16),
             pltpu.SemaphoreType.DMA((3, blocks)),
             pltpu.SemaphoreType.DMA((5, max(blocks, remote // BIG))),
+            pltpu.SemaphoreType.DMA,
         ],
         compiler_params=params(40 if keep else 60),
         name="layer",
-    )(*stored(far, own, cotangent), weight, got)
+    )(*stored(far, own, cotangent, weight), got)
 
 
 def partial_kernel(me_ref, hid_hbm, slope_hbm, mine_ref, other_ref, hid, slope, total, sems):
@@ -363,24 +369,42 @@
     )(me, mine, got)
 
 
-def join_kernel(me_ref, *refs):
-    in_refs, out_ref = refs[:-1], refs[-1]
-    height, half = in_refs[0].shape[0], out_ref.shape[0] // 2
-    for k, in_ref in enumerate(in_refs):
-        owner = me_ref[0] ^ k
-        at = pl.multiple_of((owner % 2) * half + (owner // 2) * height, height)
-        out_ref[pl.ds(at, height), :] = in_ref[...].astype(F32)
-
-
-def join(me, parts):
-    height, width = parts[0].shape
-    return pl.pallas_call(
-        join_kernel,
-        in_specs=[SMEM] + [VMEM] * len(parts),
-        out_shape=jax.ShapeDtypeStruct((height * len(parts), width), F32),
+def relay_kernel(after_ref, *refs):
+    height = refs[0].shape[0]
+    for k, ref in enumerate(refs[:-1]):
+        refs[-1][k * height : (k + 1) * height, :] = ref[...]
+
+
+def relay(after, pieces):
+    height, width = pieces[0].shape
+    return pl.pallas_call(
+        relay_kernel,
+        in_specs=[HBM] + [VMEM] * len(pieces),
+        out_shape=jax.ShapeDtypeStruct((height * len(pieces), width), BF16),
+        compiler_params=params(8),
+        name="relay",
+    )(*stored(after), *pieces)
+
+
+def join_kernel(chips, me_ref, mine_ref, other_ref, out_ref):
+    half = mine_ref.shape[0]
+    height = half // chips
+    core, chip = me_ref[0] % 2, me_ref[0] // 2
+    for owner, ref in ((core, mine_ref), (1 - core, other_ref)):
+        for k in range(chips):
+            at = pl.multiple_of(owner * half + (chip ^ k) * height, height)
+            out_ref[pl.ds(at, height), :] = ref[k * height : (k + 1) * height, :].astype(F32)
+
+
+def join(me, mine, other, chips):
+    half, width = mine.shape
+    return pl.pallas_call(
+        functools.partial(join_kernel, chips),
+        in_specs=[SMEM, VMEM, VMEM],
+        out_shape=jax.ShapeDtypeStruct((2 * half, width), F32),
         compiler_params=params(8),
         name="join",
-    )(me, *parts)
+    )(me, mine, other)
 
 
 def add_kernel(after_ref, *refs):
@@ -424,15 +448,14 @@
     mine, other = partial_grad(keep, me, hidden, slope)
     pieces = cut(me, mine, swap(other, "local", locals_, 1), chips)
     piece = add(first, [pieces[0]] + [swap(pieces[k], "local", locals_, 2 * k) for k in range(1, chips)])
-    step, after = groups // 2, second
-    while step:
+    step, after = 1, second
+    while step < groups:
         piece = add(after, [piece, swap(piece, "group", groups, step)])
-        step, after = step // 2, feature_grad
-    gathered = []
-    for k in range(chips):
-        mine = swap(piece, "local", locals_, 2 * k) if k else piece
-        gathered += [mine, swap(mine, "local", locals_, 1)]
-    return activated, feature_grad, join(me, gathered)
+        step, after = 2 * step, second
+    pieces = [piece] + [swap(piece, "local", locals_, 2 * k) for k in range(1, chips)]
+    half = relay(feature_grad, pieces)
+    weight_grad = join(me, half, swap(half, "local", locals_, 1), chips)
+    return activated, feature_grad, weight_grad
 
 
 def solution(mesh):

time: 99.6 us -> 95.3 us (0.957)
  waiting for transfers between devices: 19 us -> 14.4 us
  starting transfers between devices: 21.3 us -> 22.6 us
  local copies, waits for them, and re-layouts: 1.24 us -> 0.19 us
    ppermute x13 -> x10, waiting for transfers between devices: 12.4 us -> 7.75 us  [swap(): return lax.ppermute(x, axis, [(i, i ^ k) for i in range(size)])]
    ppermute x13 -> x10, starting transfers between devices: 10.2 us -> 11.5 us  [swap(): return lax.ppermute(x, axis, [(i, i ^ k) for i in range(size)])]
    unnamed x12 -> x10, local copies, waits for them, and re-layouts: 1.07 us -> 0.02 us
    pallas_call x2 -> x3, Pallas kernels: 12.8 us -> 13.1 us  [the longest x1 12 us: layer(): pl.pallas_call(layer_kernel, in_specs=[HBM] * 4 + [VMEM], out_specs=[HBM]...]
  transfers between devices with their start and end apart: 15 -> 12, of which waited for: 9 -> 6; matrix products, arithmetic and copies ran while one was open for 0% -> 0% of each run, Pallas kernels for 39% -> 41%
where the time goes in v4:
time: 95.3 us; the launch traced here: 95 us
  Pallas kernels  56.9 us (60%)
  starting transfers between devices  22.6 us (24%)
  waiting for transfers between devices  14.4 us (15%)
    pallas_call x1, Pallas kernels, build(): pl.pallas_call(build_kernel, grid_spec=pltpu.PrefetchScalarGridSpec(num_s...  19.5 us
    pallas_call x1, Pallas kernels, layer(): pl.pallas_call(layer_kernel, in_specs=[HBM] * 4 + [VMEM], out_specs=[HBM]...  12 us
    pallas_call x2, Pallas kernels, spread(): pl.pallas_call(spread_kernel, grid=(blocks,), in_specs=[pl.BlockSpec((own...  11.6 us
    ppermute x10, starting transfers between devices, swap(): return lax.ppermute(x, axis, [(i, i ^ k) for i in range(size)])  11.5 us
    all_to_all x2, starting transfers between devices, exchange(): return lax.all_to_all(x, axes, split_axis=0, concat_axis=0, tiled=True)  11.1 us
    ppermute x10, waiting for transfers between devices, swap(): return lax.ppermute(x, axis, [(i, i ^ k) for i in range(size)])  7.75 us
    all_to_all x2, waiting for transfers between devices, exchange(): return lax.all_to_all(x, axes, split_axis=0, concat_axis=0, tiled=True)  6.67 us
    pallas_call x1, Pallas kernels, collect(): pl.pallas_call(collect_kernel, in_specs=[SMEM, VMEM, VMEM], out_shape=jax...  5.17 us
  transfers between devices with their start and end apart: 12, of which 6 were waited for; matrix products, arithmetic and copies ran while one was open for 0% of the time, Pallas kernels for 41%

profile of v4, /device:TPU:0, one launch (start us, length us, event | category | flops | bytes accessed | tf_op | source)
XLA Modules:
  0.0 95.0 jit_solution(4151485954484453677)
XLA Ops:
  0.7 5.2 %collect.1 = bf16[1024,512]{1,0:T(8,128)(2,1)} custom-call(s32[1,32]{1,0:T(1,128)} %counts_ref.1, s32[32,32]{1,0:T(8,128)} %bitcast.11, bf16[2048,512]{1,0:T(8,128)(2,1)} %x_ref.3), custom_call_target="tpu_custom_call" | custom-call | tf_op jit(solution)/shard_map/collect/pallas_call | solution.py:70
  5.8 7.3 %all-to-all-start = ((bf16[32,32,512]{2,1,0:T(8,128)(2,1)}), bf16[32,32,512]{2,1,0:T(8,128)(2,1)S(1)}, u32[]{:S(2)}, u32[]{:S(2)}) async-start(bf16[32,32,512]{2,1,0:T(8,128)(2,1)} %bitcast.9), calls=%async_computation | async-start | bytes 2097152 | tf_op jit(solution)/shard_map/all_to_all | solution.py:351
  13.2 19.5 %build.1 = (bf16[2048,2048]{1,0:T(8,128)(2,1)}, bf16[2048,1024]{1,0:T(8,128)(2,1)}, f32[2048,512]{1,0:T(8,128)}) custom-call(s32[256]{0:T(256)S(1)} %copy-done.1, s32[256]{0:T(256)S(1)} %copy-done.2, bf16[256,128,128]{2,1,0:T(8,128)(2,1)} %tiles_ref.1, bf16[2048,512]{1,0:T(8,128)(2,1)S(1)} %copy-done), custom_call_target="tpu_custom_call" | custom-call | flops 4294967296 | bytes 41943040 | tf_op jit(solution)/shard_map/build/pallas_call | solution.py:138
  32.7 6.7 %all-to-all-done = bf16[32,32,512]{2,1,0:T(8,128)(2,1)S(1)} async-done(((bf16[32,32,512]{2,1,0:T(8,128)(2,1)}), bf16[32,32,512]{2,1,0:T(8,128)(2,1)S(1)}, u32[]{:S(2)}, u32[]{:S(2)}) %all-to-all-start) | async-done | bytes 1048608 | tf_op jit(solution)/shard_map/all_to_all | solution.py:351
  39.4 12.0 %layer.1 = (bf16[2048,512]{1,0:T(8,128)(2,1)}, bf16[2048,512]{1,0:T(8,128)(2,1)}, bf16[2048,512]{1,0:T(8,128)(2,1)}, bf16[2048,512]{1,0:T(8,128)(2,1)}, bf16[1024,512]{1,0:T(8,128)(2,1)}) custom-call(bf16[2048,1024]{1,0:T(8,128)(2,1)} %get-tuple-element.17.far_hbm, f32[2048,512]{1,0:T(8,128)} %get-tuple-element.18.own_hbm, bf16[2048,512]{1,0:T(8,128)(2,1)} %cot_hbm.1, ...), custom_call_target="tpu_custom_call" | custom-call | tf_op jit(solution)/shard_map/layer/pallas_call | solution.py:226
  51.4 3.8 %all-to-all-start.1 = ((bf16[32,32,512]{2,1,0:T(8,128)(2,1)}), bf16[32,32,512]{2,1,0:T(8,128)(2,1)S(1)}, u32[]{:S(2)}, u32[]{:S(2)}) async-start(bf16[32,32,512]{2,1,0:T(8,128)(2,1)} %bitcast.10), calls=%async_computation.1 | async-start | bytes 2097152 | tf_op jit(solution)/shard_map/all_to_all | solution.py:351
  55.2 2.9 %partial_grad.1 = (f32[256,512]{1,0:T(8,128)S(1)}, bf16[256,512]{1,0:T(8,128)(2,1)S(1)}) custom-call(s32[1]{0:T(128)} %bitcast.6.me_ref, bf16[2048,512]{1,0:T(8,128)(2,1)} %get-tuple-element.23.hid_hbm, bf16[2048,512]{1,0:T(8,128)(2,1)} %get-tuple-element.24.slope_hbm), custom_call_target="tpu_custom_call" | custom-call | tf_op jit(solution)/shard_map/partial_grad/pallas_call | solution.py:269
  58.1 0.1 collective-permute-start
  58.2 1.5 %collective-permute-done.got_ref = bf16[256,512]{1,0:T(8,128)(2,1)S(1)} collective-permute-done((bf16[256,512]{1,0:T(8,128)(2,1)S(1)}, bf16[256,512]{1,0:T(8,128)(2,1)S(1)}, u32[]{:S(2)}, u32[]{:S(2)}) %collective-permute-start) | collective-permute-done | bytes 262176 | tf_op jit(solution)/shard_map/ppermute | solution.py:428
  59.8 1.7 %collective-permute-start.1 = (bf16[64,512]{1,0:T(8,128)(2,1)S(1)}, bf16[64,512]{1,0:T(8,128)(2,1)S(1)}, u32[]{:S(2)}, u32[]{:S(2)}) collective-permute-start(bf16[64,512]{1,0:T(8,128)(2,1)S(1)} %get-tuple-element.28), channel_id=1, source_target_pairs={{0,2},{1,3},{2,0},{3,1},{4,6},{5,7},{6,4},{7,5},{8,10},{9,11},{10,... | collective-permute-start | bytes 196616 | tf_op jit(solution)/shard_map/ppermute | solution.py:428
  61.4 1.5 %collective-permute-start.2 = (bf16[64,512]{1,0:T(8,128)(2,1)S(1)}, bf16[64,512]{1,0:T(8,128)(2,1)S(1)}, u32[]{:S(2)}, u32[]{:S(2)}) collective-permute-start(bf16[64,512]{1,0:T(8,128)(2,1)S(1)} %get-tuple-element.29), channel_id=1, source_target_pairs={{0,4},{1,5},{2,6},{3,7},{4,0},{5,1},{6,2},{7,3},{8,12},{9,13},{10,... | collective-permute-start | bytes 196616 | tf_op jit(solution)/shard_map/ppermute | solution.py:428
  62.9 0.4 collective-permute-start.3
  63.3 5.8 %spread.2.first_hbm.after_ref = f32[1024,512]{1,0:T(8,128)} custom-call(bf16[2048,2048]{1,0:T(8,128)(2,1)} %get-tuple-element.20.adj_ref, bf16[2048,512]{1,0:T(8,128)(2,1)} %get-tuple-element.21.grad_ref), custom_call_target="tpu_custom_call" | custom-call | flops 4294967296 | bytes 16777216 | tf_op jit(solution)/shard_map/spread/pallas_call | solution.py:292
  69.1 0.0 collective-permute-done.1.refs_1_
  69.1 1.0 %collective-permute-done.3.refs_3_ = bf16[64,512]{1,0:T(8,128)(2,1)S(1)} collective-permute-done((bf16[64,512]{1,0:T(8,128)(2,1)S(1)}, bf16[64,512]{1,0:T(8,128)(2,1)S(1)}, u32[]{:S(2)}, u32[]{:S(2)}) %collective-permute-start.3) | collective-permute-done | bytes 65568 | tf_op jit(solution)/shard_map/ppermute | solution.py:428
  70.1 1.1 %collective-permute-start.4 = (bf16[64,512]{1,0:T(8,128)(2,1)S(1)}, bf16[64,512]{1,0:T(8,128)(2,1)S(1)}, u32[]{:S(2)}, u32[]{:S(2)}) collective-permute-start(bf16[64,512]{1,0:T(8,128)(2,1)S(1)} %add.3.refs_0_), channel_id=1, source_target_pairs={{0,8},{8,0},{16,24},{24,16},{1,9},{9,1},{17,25},{25,17},{2,10},{10... | collective-permute-start | bytes 196616 | tf_op jit(solution)/shard_map/ppermute | solution.py:428
  71.2 5.8 %spread.3.second_hbm.after_ref = f32[1024,512]{1,0:T(8,128)} custom-call(bf16[2048,2048]{1,0:T(8,128)(2,1)} %get-tuple-element.20.adj_ref, bf16[2048,512]{1,0:T(8,128)(2,1)} %get-tuple-element.21.grad_ref), custom_call_target="tpu_custom_call" | custom-call | flops 4294967296 | bytes 16777216 | tf_op jit(solution)/shard_map/spread/pallas_call | solution.py:292
  77.0 0.0 collective-permute-done.4.refs_1_
  77.0 3.1 %collective-permute-start.5 = (bf16[64,512]{1,0:T(8,128)(2,1)S(1)}, bf16[64,512]{1,0:T(8,128)(2,1)S(1)}, u32[]{:S(2)}, u32[]{:S(2)}) collective-permute-start(bf16[64,512]{1,0:T(8,128)(2,1)S(1)} %add.4.refs_0_), channel_id=1, source_target_pairs={{0,16},{8,24},{16,0},{24,8},{1,17},{9,25},{17,1},{25,9},{2,18},{10... | collective-permute-start | bytes 196616 | tf_op jit(solution)/shard_map/ppermute | solution.py:428
  80.1 0.1 iota_compare_fusion
  80.2 0.1 squeeze.6
  80.2 0.1 lt.29
  80.3 3.7 %collective-permute-done.5.refs_1_ = bf16[64,512]{1,0:T(8,128)(2,1)S(1)} collective-permute-done((bf16[64,512]{1,0:T(8,128)(2,1)S(1)}, bf16[64,512]{1,0:T(8,128)(2,1)S(1)}, u32[]{:S(2)}, u32[]{:S(2)}) %collective-permute-start.5) | collective-permute-done | bytes 65568 | tf_op jit(solution)/shard_map/ppermute | solution.py:428
  84.1 1.5 %collective-permute-start.6 = (bf16[64,512]{1,0:T(8,128)(2,1)S(1)}, bf16[64,512]{1,0:T(8,128)(2,1)S(1)}, u32[]{:S(2)}, u32[]{:S(2)}) collective-permute-start(bf16[64,512]{1,0:T(8,128)(2,1)S(1)} %add.5.refs_0_), channel_id=1, source_target_pairs={{0,2},{1,3},{2,0},{3,1},{4,6},{5,7},{6,4},{7,5},{8,10},{9,11},{10,... | collective-permute-start | bytes 196616 | tf_op jit(solution)/shard_map/ppermute | solution.py:428
  85.6 1.5 %collective-permute-start.7 = (bf16[64,512]{1,0:T(8,128)(2,1)S(1)}, bf16[64,512]{1,0:T(8,128)(2,1)S(1)}, u32[]{:S(2)}, u32[]{:S(2)}) collective-permute-start(bf16[64,512]{1,0:T(8,128)(2,1)S(1)} %add.5.refs_0_), channel_id=1, source_target_pairs={{0,4},{1,5},{2,6},{3,7},{4,0},{5,1},{6,2},{7,3},{8,12},{9,13},{10,... | collective-permute-start | bytes 196616 | tf_op jit(solution)/shard_map/ppermute | solution.py:428
  87.1 0.5 collective-permute-start.8
  87.7 4.5 %give_back.1.after_ref = bf16[2048,512]{1,0:T(8,128)(2,1)} custom-call(s32[1,1024]{1,0:T(1,128)S(1)} %broadcast_select_fusion.index_ref, f32[1024,512]{1,0:T(8,128)} %spread.2.first_hbm.after_ref, f32[1024,512]{1,0:T(8,128)} %spread.3.second_hbm.after_ref, bf16[1024,512]{1,0:T(8,128)(2,1)S(1)} %bitcast.7), custom_call_target="tpu_custom_call" | custom-call | tf_op jit(solution)/shard_map/give_back/pallas_call | solution.py:334
  92.2 0.0 collective-permute-done.6.refs_1_
  92.2 0.1 collective-permute-done.8.refs_3_
  92.3 0.1 collective-permute-start.9
  92.4 1.5 %collective-permute-done.9.other_ref = bf16[256,512]{1,0:T(8,128)(2,1)S(1)} collective-permute-done((bf16[256,512]{1,0:T(8,128)(2,1)S(1)}, bf16[256,512]{1,0:T(8,128)(2,1)S(1)}, u32[]{:S(2)}, u32[]{:S(2)}) %collective-permute-start.9) | collective-permute-done | bytes 262176 | tf_op jit(solution)/shard_map/ppermute | solution.py:428
  93.9 1.0 %join.1 = f32[512,512]{1,0:T(8,128)} custom-call(s32[1]{0:T(128)} %bitcast.6.me_ref, bf16[256,512]{1,0:T(8,128)(2,1)S(1)} %relay.1.mine_ref, bf16[256,512]{1,0:T(8,128)(2,1)S(1)} %collective-permute-done.9.other_ref), custom_call_target="tpu_custom_call" | custom-call | tf_op jit(solution)/shard_map/join/pallas_call | solution.py:401
  (19 shorter events, 0.2 us)
Async XLA Ops:
  0.6 12.5 %copy-start = (bf16[2048,512]{1,0:T(8,128)(2,1)S(1)}, bf16[2048,512]{1,0:T(8,128)(2,1)}, u32[]{:S(2)}) copy-start(bf16[2048,512]{1,0:T(8,128)(2,1)} %x_ref.3) | copy-start | bytes 6291460
  0.6 12.5 %copy-start.1 = (s32[256]{0:T(256)S(1)}, s32[256]{0:T(256)}, u32[]{:S(2)}) copy-start(s32[256]{0:T(256)} %rows_ref.1) | copy-start | bytes 3076
  0.7 12.5 %copy-start.2 = (s32[256]{0:T(256)S(1)}, s32[256]{0:T(256)}, u32[]{:S(2)}) copy-start(s32[256]{0:T(256)} %cols_ref.1) | copy-start | bytes 3076
  5.8 33.5 %all-to-all-start = ((bf16[32,32,512]{2,1,0:T(8,128)(2,1)}), bf16[32,32,512]{2,1,0:T(8,128)(2,1)S(1)}, u32[]{:S(2)}, u32[]{:S(2)}) async-start(bf16[32,32,512]{2,1,0:T(8,128)(2,1)} %bitcast.9), calls=%async_computation | async-start | bytes 2097152 | tf_op jit(solution)/shard_map/all_to_all | solution.py:351
  51.4 36.3 %all-to-all-start.1 = ((bf16[32,32,512]{2,1,0:T(8,128)(2,1)}), bf16[32,32,512]{2,1,0:T(8,128)(2,1)S(1)}, u32[]{:S(2)}, u32[]{:S(2)}) async-start(bf16[32,32,512]{2,1,0:T(8,128)(2,1)} %bitcast.10), calls=%async_computation.1 | async-start | bytes 2097152 | tf_op jit(solution)/shard_map/all_to_all | solution.py:351
  58.1 1.6 %collective-permute-start = (bf16[256,512]{1,0:T(8,128)(2,1)S(1)}, bf16[256,512]{1,0:T(8,128)(2,1)S(1)}, u32[]{:S(2)}, u32[]{:S(2)}) collective-permute-start(bf16[256,512]{1,0:T(8,128)(2,1)S(1)} %get-tuple-element.26), channel_id=1, source_target_pairs={{0,1},{1,0},{2,3},{3,2},{4,5},{5,4},{6,7},{7,6},{8,9},{9,8},{10,11... | collective-permute-start | bytes 786440 | tf_op jit(solution)/shard_map/ppermute | solution.py:428
  59.8 9.3 %collective-permute-start.1 = (bf16[64,512]{1,0:T(8,128)(2,1)S(1)}, bf16[64,512]{1,0:T(8,128)(2,1)S(1)}, u32[]{:S(2)}, u32[]{:S(2)}) collective-permute-start(bf16[64,512]{1,0:T(8,128)(2,1)S(1)} %get-tuple-element.28), channel_id=1, source_target_pairs={{0,2},{1,3},{2,0},{3,1},{4,6},{5,7},{6,4},{7,5},{8,10},{9,11},{10,... | collective-permute-start | bytes 196616 | tf_op jit(solution)/shard_map/ppermute | solution.py:428
  61.4 7.7 %collective-permute-start.2 = (bf16[64,512]{1,0:T(8,128)(2,1)S(1)}, bf16[64,512]{1,0:T(8,128)(2,1)S(1)}, u32[]{:S(2)}, u32[]{:S(2)}) collective-permute-start(bf16[64,512]{1,0:T(8,128)(2,1)S(1)} %get-tuple-element.29), channel_id=1, source_target_pairs={{0,4},{1,5},{2,6},{3,7},{4,0},{5,1},{6,2},{7,3},{8,12},{9,13},{10,... | collective-permute-start | bytes 196616 | tf_op jit(solution)/shard_map/ppermute | solution.py:428
  62.9 7.2 %collective-permute-start.3 = (bf16[64,512]{1,0:T(8,128)(2,1)S(1)}, bf16[64,512]{1,0:T(8,128)(2,1)S(1)}, u32[]{:S(2)}, u32[]{:S(2)}) collective-permute-start(bf16[64,512]{1,0:T(8,128)(2,1)S(1)} %get-tuple-element.30), channel_id=1, source_target_pairs={{0,6},{1,7},{2,4},{3,5},{4,2},{5,3},{6,0},{7,1},{8,14},{9,15},{10,... | collective-permute-start | bytes 196616 | tf_op jit(solution)/shard_map/ppermute | solution.py:428
  70.1 6.9 %collective-permute-start.4 = (bf16[64,512]{1,0:T(8,128)(2,1)S(1)}, bf16[64,512]{1,0:T(8,128)(2,1)S(1)}, u32[]{:S(2)}, u32[]{:S(2)}) collective-permute-start(bf16[64,512]{1,0:T(8,128)(2,1)S(1)} %add.3.refs_0_), channel_id=1, source_target_pairs={{0,8},{8,0},{16,24},{24,16},{1,9},{9,1},{17,25},{25,17},{2,10},{10... | collective-permute-start | bytes 196616 | tf_op jit(solution)/shard_map/ppermute | solution.py:428
  77.0 3.1 %copy-start.4 = (s32[1,32]{1,0:T(1,128)S(1)}, s32[1,32]{1,0:T(1,128)}, u32[]{:S(2)}) copy-start(s32[1,32]{1,0:T(1,128)} %counts_ref.1) | copy-start | bytes 388
  77.0 3.2 %copy-start.3 = (s32[1,32,32]{2,1,0:T(8,128)S(1)}, s32[1,32,32]{2,1,0:T(8,128)}, u32[]{:S(2)}) copy-start(s32[1,32,32]{2,1,0:T(8,128)} %param.14) | copy-start | bytes 12292
  77.0 7.1 %collective-permute-start.5 = (bf16[64,512]{1,0:T(8,128)(2,1)S(1)}, bf16[64,512]{1,0:T(8,128)(2,1)S(1)}, u32[]{:S(2)}, u32[]{:S(2)}) collective-permute-start(bf16[64,512]{1,0:T(8,128)(2,1)S(1)} %add.4.refs_0_), channel_id=1, source_target_pairs={{0,16},{8,24},{16,0},{24,8},{1,17},{9,25},{17,1},{25,9},{2,18},{10... | collective-permute-start | bytes 196616 | tf_op jit(solution)/shard_map/ppermute | solution.py:428
  84.1 8.1 %collective-permute-start.6 = (bf16[64,512]{1,0:T(8,128)(2,1)S(1)}, bf16[64,512]{1,0:T(8,128)(2,1)S(1)}, u32[]{:S(2)}, u32[]{:S(2)}) collective-permute-start(bf16[64,512]{1,0:T(8,128)(2,1)S(1)} %add.5.refs_0_), channel_id=1, source_target_pairs={{0,2},{1,3},{2,0},{3,1},{4,6},{5,7},{6,4},{7,5},{8,10},{9,11},{10,... | collective-permute-start | bytes 196616 | tf_op jit(solution)/shard_map/ppermute | solution.py:428
  85.6 6.6 %collective-permute-start.7 = (bf16[64,512]{1,0:T(8,128)(2,1)S(1)}, bf16[64,512]{1,0:T(8,128)(2,1)S(1)}, u32[]{:S(2)}, u32[]{:S(2)}) collective-permute-start(bf16[64,512]{1,0:T(8,128)(2,1)S(1)} %add.5.refs_0_), channel_id=1, source_target_pairs={{0,4},{1,5},{2,6},{3,7},{4,0},{5,1},{6,2},{7,3},{8,12},{9,13},{10,... | collective-permute-start | bytes 196616 | tf_op jit(solution)/shard_map/ppermute | solution.py:428
  87.1 5.2 %collective-permute-start.8 = (bf16[64,512]{1,0:T(8,128)(2,1)S(1)}, bf16[64,512]{1,0:T(8,128)(2,1)S(1)}, u32[]{:S(2)}, u32[]{:S(2)}) collective-permute-start(bf16[64,512]{1,0:T(8,128)(2,1)S(1)} %add.5.refs_0_), channel_id=1, source_target_pairs={{0,6},{1,7},{2,4},{3,5},{4,2},{5,3},{6,0},{7,1},{8,14},{9,15},{10,... | collective-permute-start | bytes 196616 | tf_op jit(solution)/shard_map/ppermute | solution.py:428
  92.3 1.6 %collective-permute-start.9 = (bf16[256,512]{1,0:T(8,128)(2,1)S(1)}, bf16[256,512]{1,0:T(8,128)(2,1)S(1)}, u32[]{:S(2)}, u32[]{:S(2)}) collective-permute-start(bf16[256,512]{1,0:T(8,128)(2,1)S(1)} %relay.1.mine_ref), channel_id=1, source_target_pairs={{0,1},{1,0},{2,3},{3,2},{4,5},{5,4},{6,7},{7,6},{8,9},{9,8},{10,11... | collective-permute-start | bytes 786440 | tf_op jit(solution)/shard_map/ppermute | solution.py:428

commit v5 on v4

--- a/solution.py
+++ b/solution.py
@@ -50,30 +50,57 @@
     return pl.BlockSpec(shape, lambda i, *unused: (0,) * len(shape))
 
 
-def collect_kernel(counts_ref, lists_ref, x_ref, out_ref):
+def collect_kernel(counts_ref, lists_ref, x_hbm, out_hbm, x, total, out, came, sent):
     dests, slots = lists_ref.shape
     step = BIG // slots
-    lane = lax.broadcasted_iota(jnp.int32, (slots, x_ref.shape[0]), 1)
+    chunks, rounds = came.shape[0], sent.shape[0]
+    deep = x.shape[0] // chunks
+    fetch = []
+    for k in range(chunks):
+        at = pl.ds(k * deep, deep)
+        fetch.append(pltpu.make_async_copy(x_hbm.at[at], x.at[at], came.at[k]))
+        fetch[k].start()
+    lane = lax.broadcasted_iota(jnp.int32, (slots, deep), 1)
     slot = lax.broadcasted_iota(jnp.int32, (slots, 1), 0)
     turned = lists_ref[...].T
-    for first in range(0, dests, step):
-        parts = []
-        for d in range(first, first + step):
-            named = jnp.where(slot < counts_ref[0, d], turned[:, d : d + 1], -1)
-            parts.append(jnp.where(named == lane, 1.0, 0.0).astype(BF16))
-        pick = jnp.concatenate(parts, axis=0)
-        out_ref[first * slots : (first + step) * slots, :] = dot(pick, x_ref[...]).astype(BF16)
+    named = [jnp.where(slot < counts_ref[0, d], turned[:, d : d + 1], -1) for d in range(dests)]
+    sending = []
+    for k in range(chunks):
+        fetch[k].wait()
+        for n in range(rounds):
+            at = pl.ds(n * BIG, BIG)
+            picks = [jnp.where(named[d] - k * deep == lane, 1.0, 0.0).astype(BF16) for d in range(n * step, (n + 1) * step)]
+            found = dot(jnp.concatenate(picks, axis=0), x[k * deep : (k + 1) * deep, :])
+            if k > 0:
+                found = total[at, :] + found
+            if k + 1 < chunks:
+                total[at, :] = found
+            else:
+                out[at, :] = found.astype(BF16)
+                sending.append(pltpu.make_async_copy(out.at[at], out_hbm.at[at], sent.at[n]))
+                sending[n].start()
+    for copy in sending:
+        copy.wait()
 
 
 def collect(counts, lists, x):
     dests, slots = lists.shape
+    shape = (dests * slots, x.shape[1])
     return pl.pallas_call(
         collect_kernel,
-        in_specs=[SMEM, VMEM, VMEM],
-        out_shape=jax.ShapeDtypeStruct((dests * slots, x.shape[1]), BF16),
+        in_specs=[SMEM, VMEM, HBM],
+        out_specs=HBM,
+        out_shape=far_made(shape, BF16),
+        scratch_shapes=[
+            pltpu.VMEM(x.shape, BF16),
+            pltpu.VMEM(shape, F32),
+            pltpu.VMEM(shape, BF16),
+            pltpu.SemaphoreType.DMA((4,)),
+            pltpu.SemaphoreType.DMA((shape[0] // BIG,)),
+        ],
         compiler_params=params(60),
         name="collect",
-    )(counts, lists, x)
+    )(counts, lists, *stored(x))
 
 
 def build_kernel(rows_ref, cols_ref, tiles_ref, x_ref, adj_ref, far_ref, own_ref, total, order, starts, cursor):
@@ -169,7 +196,7 @@
 def layer_kernel(
     far_hbm, own_hbm, cot_hbm, w_hbm, got_ref,
     act_hbm, hid_hbm, slope_hbm, grad_hbm, back_hbm,
-    far, own, cot, act, hid, slope, grad, w, back, sems, sent, w_sem,
+    far, own, cot, act, hid, slope, grad, w, pre, back, sems, sent, w_sem,
 ):
     blocks = sems.shape[1]
     views = [pl.ds(n * BIG, BIG) for n in range(blocks)]
@@ -190,25 +217,33 @@
     coming = fetch(0)
     weight = pltpu.make_async_copy(w_hbm, w, w_sem)
     weight.start()
-    for n, at in enumerate(views):
-        copies = coming
-        for copy in copies[:2]:
-            copy.wait()
-        if n + 1 < blocks:
-            coming = fetch(n + 1)
-        hid[at, :] = (own[at, :] + dot(far[at, :], got_ref[...])).astype(BF16)
-        send(0, n, hid, hid_hbm, at)
-        copies[2].wait()
-        if n == 0:
-            weight.wait()
-        preact = dot(hid[at, :], w[...])
-        gate = 0.5 + 0.5 * jnp.tanh(0.5 * preact)
-        act[at, :] = (preact * gate).astype(BF16)
-        send(1, n, act, act_hbm, at)
-        slope[at, :] = (cot[at, :].astype(F32) * gate * (1.0 + preact * (1.0 - gate))).astype(BF16)
-        send(2, n, slope, slope_hbm, at)
-        grad[at, :] = dot(slope[at, :], w[...], ((1,), (1,))).astype(BF16)
-        send(3, n, grad, grad_hbm, at)
+    for n in range(blocks + 1):
+        if n < blocks:
+            at = views[n]
+            for copy in coming:
+                copy.wait()
+            if n == 0:
+                weight.wait()
+            if n + 1 < blocks:
+                coming = fetch(n + 1)
+        if n > 0:
+            old = views[n - 1]
+            preact = pre[(n - 1) % 2]
+            gate = 0.5 + 0.5 * jnp.tanh(0.5 * preact)
+            activated = (preact * gate).astype(BF16)
+            slopes = (cot[old, :].astype(F32) * gate * (1.0 + preact * (1.0 - gate))).astype(BF16)
+        if n < blocks:
+            hidden = (own[at, :] + dot(far[at, :], got_ref[...])).astype(BF16)
+            hid[at, :] = hidden
+            pre[n % 2] = dot(hidden, w[...])
+        if n > 0:
+            act[old, :] = activated
+            slope[old, :] = slopes
+            grad[old, :] = dot(slopes, w[...], ((1,), (1,))).astype(BF16)
+            for k, (ref, ref_hbm) in enumerate(((act, act_hbm), (slope, slope_hbm), (grad, grad_hbm))):
+                send(k + 1, n - 1, ref, ref_hbm, old)
+        if n < blocks:
+            send(0, n, hid, hid_hbm, at)
     for n in range(back.shape[0] // BIG):
         at = pl.ds(n * BIG, BIG)
         back[at, :] = dot(far[:, at], grad[...], ((0,), (0,))).astype(BF16)
@@ -232,6 +267,7 @@
         + [pltpu.VMEM(rows, BF16)] * 5
         + [
             pltpu.VMEM(weight.shape, BF16),
+            pltpu.VMEM((2, BIG, width), F32),
             pltpu.VMEM(got.shape, BF16),
             pltpu.SemaphoreType.DMA((3, blocks)),
             pltpu.SemaphoreType.DMA((5, max(blocks, remote // BIG))),
@@ -386,25 +422,30 @@
     )(*stored(after), *pieces)
 
 
-def join_kernel(chips, me_ref, mine_ref, other_ref, out_ref):
-    half = mine_ref.shape[0]
+def place_kernel(chips, other, me_ref, half_ref, *refs):
+    out_hbm, placed, sem = refs[-3:]
+    half = half_ref.shape[0]
     height = half // chips
-    core, chip = me_ref[0] % 2, me_ref[0] // 2
-    for owner, ref in ((core, mine_ref), (1 - core, other_ref)):
-        for k in range(chips):
-            at = pl.multiple_of(owner * half + (chip ^ k) * height, height)
-            out_ref[pl.ds(at, height), :] = ref[k * height : (k + 1) * height, :].astype(F32)
-
-
-def join(me, mine, other, chips):
-    half, width = mine.shape
-    return pl.pallas_call(
-        functools.partial(join_kernel, chips),
-        in_specs=[SMEM, VMEM, VMEM],
-        out_shape=jax.ShapeDtypeStruct((2 * half, width), F32),
+    for k in range(chips):
+        at = pl.multiple_of(((me_ref[0] // 2) ^ k) * height, height)
+        placed[pl.ds(at, height), :] = half_ref[k * height : (k + 1) * height, :].astype(F32)
+    at = pl.multiple_of((me_ref[0] + other) % 2 * half, half)
+    copy = pltpu.make_async_copy(placed, out_hbm.at[pl.ds(at, half)], sem)
+    copy.start()
+    copy.wait()
+
+
+def place(me, half, chips, into=()):
+    return pl.pallas_call(
+        functools.partial(place_kernel, chips, len(into)),
+        in_specs=[SMEM, VMEM] + [HBM] * len(into),
+        out_specs=HBM,
+        out_shape=far_made((2 * half.shape[0], half.shape[1]), F32),
+        scratch_shapes=[pltpu.VMEM(half.shape, F32), pltpu.SemaphoreType.DMA],
+        input_output_aliases={2: 0} if into else {},
         compiler_params=params(8),
-        name="join",
-    )(me, mine, other)
+        name="place",
+    )(me, half, *stored(*into))
 
 
 def add_kernel(after_ref, *refs):
@@ -454,7 +495,7 @@
         step, after = 2 * step, second
     pieces = [piece] + [swap(piece, "local", locals_, 2 * k) for k in range(1, chips)]
     half = relay(feature_grad, pieces)
-    weight_grad = join(me, half, swap(half, "local", locals_, 1), chips)
+    weight_grad = place(me, swap(half, "local", locals_, 1), chips, [place(me, half, chips)])
     return activated, feature_grad, weight_grad
 
 

time: 95.3 us -> 96.7 us (1.015)
  Pallas kernels: 56.9 us -> 58.8 us
    pallas_call x1, Pallas kernels: 12 us -> 13 us  [layer(): pl.pallas_call(layer_kernel, in_specs=[HBM] * 4 + [VMEM], out_specs=[HBM]...]
    pallas_call x2 -> x3, Pallas kernels: 6.22 us -> 7.11 us  [the longest x1 5.42 us: collect(): pl.pallas_call(collect_kernel, in_specs=[SMEM, VMEM, HBM], out_specs=HBM,...]
where the time goes in v5:
time: 96.7 us; the launch traced here: 96.2 us
  Pallas kernels  58.8 us (61%)
  starting transfers between devices  22.6 us (23%)
  waiting for transfers between devices  13.6 us (14%)
  between operations  0.97 us (1%)
    pallas_call x1, Pallas kernels, build(): pl.pallas_call(build_kernel, grid_spec=pltpu.PrefetchScalarGridSpec(num_s...  19.5 us
    pallas_call x1, Pallas kernels, layer(): pl.pallas_call(layer_kernel, in_specs=[HBM] * 4 + [VMEM], out_specs=[HBM]...  13 us
    pallas_call x2, Pallas kernels, spread(): pl.pallas_call(spread_kernel, grid=(blocks,), in_specs=[pl.BlockSpec((own...  11.6 us
    ppermute x10, starting transfers between devices, swap(): return lax.ppermute(x, axis, [(i, i ^ k) for i in range(size)])  11.5 us
    all_to_all x2, starting transfers between devices, exchange(): return lax.all_to_all(x, axes, split_axis=0, concat_axis=0, tiled=True)  11.1 us
    ppermute x10, waiting for transfers between devices, swap(): return lax.ppermute(x, axis, [(i, i ^ k) for i in range(size)])  6.89 us
    all_to_all x2, waiting for transfers between devices, exchange(): return lax.all_to_all(x, axes, split_axis=0, concat_axis=0, tiled=True)  6.66 us
    pallas_call x1, Pallas kernels, collect(): pl.pallas_call(collect_kernel, in_specs=[SMEM, VMEM, HBM], out_specs=HBM,...  5.42 us
  transfers between devices with their start and end apart: 12, of which 6 were waited for; matrix products, arithmetic and copies ran while one was open for 0% of the time, Pallas kernels for 41%

profile of v5, /device:TPU:0, one launch (start us, length us, event | category | flops | bytes accessed | tf_op | source)
XLA Modules:
  0.0 96.2 jit_solution(7469149686371834365)
XLA Ops:
  0.7 5.4 %collect.1 = bf16[1024,512]{1,0:T(8,128)(2,1)} custom-call(s32[1,32]{1,0:T(1,128)} %counts_ref.1, s32[32,32]{1,0:T(8,128)} %bitcast.11, bf16[2048,512]{1,0:T(8,128)(2,1)} %x_hbm.1), custom_call_target="tpu_custom_call" | custom-call | tf_op jit(solution)/shard_map/collect/pallas_call | solution.py:89
  6.1 7.3 %all-to-all-start = ((bf16[32,32,512]{2,1,0:T(8,128)(2,1)}), bf16[32,32,512]{2,1,0:T(8,128)(2,1)S(1)}, u32[]{:S(2)}, u32[]{:S(2)}) async-start(bf16[32,32,512]{2,1,0:T(8,128)(2,1)} %bitcast.9), calls=%async_computation | async-start | bytes 2097152 | tf_op jit(solution)/shard_map/all_to_all | solution.py:387
  13.4 19.5 %build.1 = (bf16[2048,2048]{1,0:T(8,128)(2,1)}, bf16[2048,1024]{1,0:T(8,128)(2,1)}, f32[2048,512]{1,0:T(8,128)}) custom-call(s32[256]{0:T(256)S(1)} %copy-done.1, s32[256]{0:T(256)S(1)} %copy-done.2, bf16[256,128,128]{2,1,0:T(8,128)(2,1)} %tiles_ref.1, bf16[2048,512]{1,0:T(8,128)(2,1)S(1)} %copy-done), custom_call_target="tpu_custom_call" | custom-call | flops 4294967296 | bytes 41943040 | tf_op jit(solution)/shard_map/build/pallas_call | solution.py:165
  33.0 6.7 %all-to-all-done = bf16[32,32,512]{2,1,0:T(8,128)(2,1)S(1)} async-done(((bf16[32,32,512]{2,1,0:T(8,128)(2,1)}), bf16[32,32,512]{2,1,0:T(8,128)(2,1)S(1)}, u32[]{:S(2)}, u32[]{:S(2)}) %all-to-all-start) | async-done | bytes 1048608 | tf_op jit(solution)/shard_map/all_to_all | solution.py:387
  39.6 13.0 %layer.1 = (bf16[2048,512]{1,0:T(8,128)(2,1)}, bf16[2048,512]{1,0:T(8,128)(2,1)}, bf16[2048,512]{1,0:T(8,128)(2,1)}, bf16[2048,512]{1,0:T(8,128)(2,1)}, bf16[1024,512]{1,0:T(8,128)(2,1)}) custom-call(bf16[2048,1024]{1,0:T(8,128)(2,1)} %get-tuple-element.17.far_hbm, f32[2048,512]{1,0:T(8,128)} %get-tuple-element.18.own_hbm, bf16[2048,512]{1,0:T(8,128)(2,1)} %cot_hbm.1, ...), custom_call_target="tpu_custom_call" | custom-call | tf_op jit(solution)/shard_map/layer/pallas_call | solution.py:261
  52.7 3.8 %all-to-all-start.1 = ((bf16[32,32,512]{2,1,0:T(8,128)(2,1)}), bf16[32,32,512]{2,1,0:T(8,128)(2,1)S(1)}, u32[]{:S(2)}, u32[]{:S(2)}) async-start(bf16[32,32,512]{2,1,0:T(8,128)(2,1)} %bitcast.10), calls=%async_computation.1 | async-start | bytes 2097152 | tf_op jit(solution)/shard_map/all_to_all | solution.py:387
  56.5 2.9 %partial_grad.1 = (f32[256,512]{1,0:T(8,128)S(1)}, bf16[256,512]{1,0:T(8,128)(2,1)S(1)}) custom-call(s32[1]{0:T(128)} %bitcast.6.me_ref, bf16[2048,512]{1,0:T(8,128)(2,1)} %get-tuple-element.23.hid_hbm, bf16[2048,512]{1,0:T(8,128)(2,1)} %get-tuple-element.24.slope_hbm), custom_call_target="tpu_custom_call" | custom-call | tf_op jit(solution)/shard_map/partial_grad/pallas_call | solution.py:305
  59.4 0.1 collective-permute-start
  59.5 1.5 %collective-permute-done.got_ref = bf16[256,512]{1,0:T(8,128)(2,1)S(1)} collective-permute-done((bf16[256,512]{1,0:T(8,128)(2,1)S(1)}, bf16[256,512]{1,0:T(8,128)(2,1)S(1)}, u32[]{:S(2)}, u32[]{:S(2)}) %collective-permute-start) | collective-permute-done | bytes 262176 | tf_op jit(solution)/shard_map/ppermute | solution.py:469
  61.0 1.7 %collective-permute-start.1 = (bf16[64,512]{1,0:T(8,128)(2,1)S(1)}, bf16[64,512]{1,0:T(8,128)(2,1)S(1)}, u32[]{:S(2)}, u32[]{:S(2)}) collective-permute-start(bf16[64,512]{1,0:T(8,128)(2,1)S(1)} %get-tuple-element.28), channel_id=1, source_target_pairs={{0,2},{1,3},{2,0},{3,1},{4,6},{5,7},{6,4},{7,5},{8,10},{9,11},{10,... | collective-permute-start | bytes 196616 | tf_op jit(solution)/shard_map/ppermute | solution.py:469
  62.7 1.5 %collective-permute-start.2 = (bf16[64,512]{1,0:T(8,128)(2,1)S(1)}, bf16[64,512]{1,0:T(8,128)(2,1)S(1)}, u32[]{:S(2)}, u32[]{:S(2)}) collective-permute-start(bf16[64,512]{1,0:T(8,128)(2,1)S(1)} %get-tuple-element.29), channel_id=1, source_target_pairs={{0,4},{1,5},{2,6},{3,7},{4,0},{5,1},{6,2},{7,3},{8,12},{9,13},{10,... | collective-permute-start | bytes 196616 | tf_op jit(solution)/shard_map/ppermute | solution.py:469
  64.2 0.4 collective-permute-start.3
  64.6 5.8 %spread.2.first_hbm.after_ref = f32[1024,512]{1,0:T(8,128)} custom-call(bf16[2048,2048]{1,0:T(8,128)(2,1)} %get-tuple-element.20.adj_ref, bf16[2048,512]{1,0:T(8,128)(2,1)} %get-tuple-element.21.grad_ref), custom_call_target="tpu_custom_call" | custom-call | flops 4294967296 | bytes 16777216 | tf_op jit(solution)/shard_map/spread/pallas_call | solution.py:328
  70.4 0.9 collective-permute-done.3.refs_3_
  71.4 1.1 %collective-permute-start.4 = (bf16[64,512]{1,0:T(8,128)(2,1)S(1)}, bf16[64,512]{1,0:T(8,128)(2,1)S(1)}, u32[]{:S(2)}, u32[]{:S(2)}) collective-permute-start(bf16[64,512]{1,0:T(8,128)(2,1)S(1)} %add.3.refs_0_), channel_id=1, source_target_pairs={{0,8},{8,0},{16,24},{24,16},{1,9},{9,1},{17,25},{25,17},{2,10},{10... | collective-permute-start | bytes 196616 | tf_op jit(solution)/shard_map/ppermute | solution.py:469
  72.5 5.8 %spread.3.second_hbm.after_ref = f32[1024,512]{1,0:T(8,128)} custom-call(bf16[2048,2048]{1,0:T(8,128)(2,1)} %get-tuple-element.20.adj_ref, bf16[2048,512]{1,0:T(8,128)(2,1)} %get-tuple-element.21.grad_ref), custom_call_target="tpu_custom_call" | custom-call | flops 4294967296 | bytes 16777216 | tf_op jit(solution)/shard_map/spread/pallas_call | solution.py:328
  78.3 3.1 %collective-permute-start.5 = (bf16[64,512]{1,0:T(8,128)(2,1)S(1)}, bf16[64,512]{1,0:T(8,128)(2,1)S(1)}, u32[]{:S(2)}, u32[]{:S(2)}) collective-permute-start(bf16[64,512]{1,0:T(8,128)(2,1)S(1)} %add.4.refs_0_), channel_id=1, source_target_pairs={{0,16},{8,24},{16,0},{24,8},{1,17},{9,25},{17,1},{25,9},{2,18},{10... | collective-permute-start | bytes 196616 | tf_op jit(solution)/shard_map/ppermute | solution.py:469
  81.4 0.1 iota_compare_fusion
  81.4 0.1 squeeze.6
  81.5 0.1 lt.29
  81.6 3.8 %collective-permute-done.5.refs_1_ = bf16[64,512]{1,0:T(8,128)(2,1)S(1)} collective-permute-done((bf16[64,512]{1,0:T(8,128)(2,1)S(1)}, bf16[64,512]{1,0:T(8,128)(2,1)S(1)}, u32[]{:S(2)}, u32[]{:S(2)}) %collective-permute-start.5) | collective-permute-done | bytes 65568 | tf_op jit(solution)/shard_map/ppermute | solution.py:469
  85.4 1.5 %collective-permute-start.6 = (bf16[64,512]{1,0:T(8,128)(2,1)S(1)}, bf16[64,512]{1,0:T(8,128)(2,1)S(1)}, u32[]{:S(2)}, u32[]{:S(2)}) collective-permute-start(bf16[64,512]{1,0:T(8,128)(2,1)S(1)} %add.5.refs_0_), channel_id=1, source_target_pairs={{0,2},{1,3},{2,0},{3,1},{4,6},{5,7},{6,4},{7,5},{8,10},{9,11},{10,... | collective-permute-start | bytes 196616 | tf_op jit(solution)/shard_map/ppermute | solution.py:469
  86.9 1.5 %collective-permute-start.7 = (bf16[64,512]{1,0:T(8,128)(2,1)S(1)}, bf16[64,512]{1,0:T(8,128)(2,1)S(1)}, u32[]{:S(2)}, u32[]{:S(2)}) collective-permute-start(bf16[64,512]{1,0:T(8,128)(2,1)S(1)} %add.5.refs_0_), channel_id=1, source_target_pairs={{0,4},{1,5},{2,6},{3,7},{4,0},{5,1},{6,2},{7,3},{8,12},{9,13},{10,... | collective-permute-start | bytes 196616 | tf_op jit(solution)/shard_map/ppermute | solution.py:469
  88.4 0.5 collective-permute-start.8
  89.0 0.0 all-to-all-done.1
  89.0 4.5 %give_back.1.after_ref = bf16[2048,512]{1,0:T(8,128)(2,1)} custom-call(s32[1,1024]{1,0:T(1,128)S(1)} %broadcast_select_fusion.index_ref, f32[1024,512]{1,0:T(8,128)} %spread.2.first_hbm.after_ref, f32[1024,512]{1,0:T(8,128)} %spread.3.second_hbm.after_ref, bf16[1024,512]{1,0:T(8,128)(2,1)S(1)} %bitcast.7), custom_call_target="tpu_custom_call" | custom-call | tf_op jit(solution)/shard_map/give_back/pallas_call | solution.py:370
  93.5 0.0 collective-permute-done.7.refs_2_
  93.5 0.1 collective-permute-done.8.refs_3_
  93.6 0.1 collective-permute-start.9
  93.7 0.8 place.2.refs_0_
  94.5 0.7 collective-permute-done.9.half_ref
  95.2 0.8 place.3
  (20 shorter events, 0.2 us)
Async XLA Ops:
  0.6 12.8 %copy-start = (bf16[2048,512]{1,0:T(8,128)(2,1)S(1)}, bf16[2048,512]{1,0:T(8,128)(2,1)}, u32[]{:S(2)}) copy-start(bf16[2048,512]{1,0:T(8,128)(2,1)} %x_hbm.1) | copy-start | bytes 6291460
  0.6 12.8 %copy-start.1 = (s32[256]{0:T(256)S(1)}, s32[256]{0:T(256)}, u32[]{:S(2)}) copy-start(s32[256]{0:T(256)} %rows_ref.1) | copy-start | bytes 3076
  0.7 12.8 %copy-start.2 = (s32[256]{0:T(256)S(1)}, s32[256]{0:T(256)}, u32[]{:S(2)}) copy-start(s32[256]{0:T(256)} %cols_ref.1) | copy-start | bytes 3076
  6.1 33.5 %all-to-all-start = ((bf16[32,32,512]{2,1,0:T(8,128)(2,1)}), bf16[32,32,512]{2,1,0:T(8,128)(2,1)S(1)}, u32[]{:S(2)}, u32[]{:S(2)}) async-start(bf16[32,32,512]{2,1,0:T(8,128)(2,1)} %bitcast.9), calls=%async_computation | async-start | bytes 2097152 | tf_op jit(solution)/shard_map/all_to_all | solution.py:387
  52.7 36.3 %all-to-all-start.1 = ((bf16[32,32,512]{2,1,0:T(8,128)(2,1)}), bf16[32,32,512]{2,1,0:T(8,128)(2,1)S(1)}, u32[]{:S(2)}, u32[]{:S(2)}) async-start(bf16[32,32,512]{2,1,0:T(8,128)(2,1)} %bitcast.10), calls=%async_computation.1 | async-start | bytes 2097152 | tf_op jit(solution)/shard_map/all_to_all | solution.py:387
  59.4 1.6 %collective-permute-start = (bf16[256,512]{1,0:T(8,128)(2,1)S(1)}, bf16[256,512]{1,0:T(8,128)(2,1)S(1)}, u32[]{:S(2)}, u32[]{:S(2)}) collective-permute-start(bf16[256,512]{1,0:T(8,128)(2,1)S(1)} %get-tuple-element.26), channel_id=1, source_target_pairs={{0,1},{1,0},{2,3},{3,2},{4,5},{5,4},{6,7},{7,6},{8,9},{9,8},{10,11... | collective-permute-start | bytes 786440 | tf_op jit(solution)/shard_map/ppermute | solution.py:469
  61.0 9.4 %collective-permute-start.1 = (bf16[64,512]{1,0:T(8,128)(2,1)S(1)}, bf16[64,512]{1,0:T(8,128)(2,1)S(1)}, u32[]{:S(2)}, u32[]{:S(2)}) collective-permute-start(bf16[64,512]{1,0:T(8,128)(2,1)S(1)} %get-tuple-element.28), channel_id=1, source_target_pairs={{0,2},{1,3},{2,0},{3,1},{4,6},{5,7},{6,4},{7,5},{8,10},{9,11},{10,... | collective-permute-start | bytes 196616 | tf_op jit(solution)/shard_map/ppermute | solution.py:469
  62.7 7.7 %collective-permute-start.2 = (bf16[64,512]{1,0:T(8,128)(2,1)S(1)}, bf16[64,512]{1,0:T(8,128)(2,1)S(1)}, u32[]{:S(2)}, u32[]{:S(2)}) collective-permute-start(bf16[64,512]{1,0:T(8,128)(2,1)S(1)} %get-tuple-element.29), channel_id=1, source_target_pairs={{0,4},{1,5},{2,6},{3,7},{4,0},{5,1},{6,2},{7,3},{8,12},{9,13},{10,... | collective-permute-start | bytes 196616 | tf_op jit(solution)/shard_map/ppermute | solution.py:469
  64.2 7.2 %collective-permute-start.3 = (bf16[64,512]{1,0:T(8,128)(2,1)S(1)}, bf16[64,512]{1,0:T(8,128)(2,1)S(1)}, u32[]{:S(2)}, u32[]{:S(2)}) collective-permute-start(bf16[64,512]{1,0:T(8,128)(2,1)S(1)} %get-tuple-element.30), channel_id=1, source_target_pairs={{0,6},{1,7},{2,4},{3,5},{4,2},{5,3},{6,0},{7,1},{8,14},{9,15},{10,... | collective-permute-start | bytes 196616 | tf_op jit(solution)/shard_map/ppermute | solution.py:469
  71.4 6.9 %collective-permute-start.4 = (bf16[64,512]{1,0:T(8,128)(2,1)S(1)}, bf16[64,512]{1,0:T(8,128)(2,1)S(1)}, u32[]{:S(2)}, u32[]{:S(2)}) collective-permute-start(bf16[64,512]{1,0:T(8,128)(2,1)S(1)} %add.3.refs_0_), channel_id=1, source_target_pairs={{0,8},{8,0},{16,24},{24,16},{1,9},{9,1},{17,25},{25,17},{2,10},{10... | collective-permute-start | bytes 196616 | tf_op jit(solution)/shard_map/ppermute | solution.py:469
  78.3 3.1 %copy-start.4 = (s32[1,32]{1,0:T(1,128)S(1)}, s32[1,32]{1,0:T(1,128)}, u32[]{:S(2)}) copy-start(s32[1,32]{1,0:T(1,128)} %counts_ref.1) | copy-start | bytes 388
  78.3 3.2 %copy-start.3 = (s32[1,32,32]{2,1,0:T(8,128)S(1)}, s32[1,32,32]{2,1,0:T(8,128)}, u32[]{:S(2)}) copy-start(s32[1,32,32]{2,1,0:T(8,128)} %param.14) | copy-start | bytes 12292
  78.3 7.1 %collective-permute-start.5 = (bf16[64,512]{1,0:T(8,128)(2,1)S(1)}, bf16[64,512]{1,0:T(8,128)(2,1)S(1)}, u32[]{:S(2)}, u32[]{:S(2)}) collective-permute-start(bf16[64,512]{1,0:T(8,128)(2,1)S(1)} %add.4.refs_0_), channel_id=1, source_target_pairs={{0,16},{8,24},{16,0},{24,8},{1,17},{9,25},{17,1},{25,9},{2,18},{10... | collective-permute-start | bytes 196616 | tf_op jit(solution)/shard_map/ppermute | solution.py:469
  85.4 8.1 %collective-permute-start.6 = (bf16[64,512]{1,0:T(8,128)(2,1)S(1)}, bf16[64,512]{1,0:T(8,128)(2,1)S(1)}, u32[]{:S(2)}, u32[]{:S(2)}) collective-permute-start(bf16[64,512]{1,0:T(8,128)(2,1)S(1)} %add.5.refs_0_), channel_id=1, source_target_pairs={{0,2},{1,3},{2,0},{3,1},{4,6},{5,7},{6,4},{7,5},{8,10},{9,11},{10,... | collective-permute-start | bytes 196616 | tf_op jit(solution)/shard_map/ppermute | solution.py:469
  86.9 6.6 %collective-permute-start.7 = (bf16[64,512]{1,0:T(8,128)(2,1)S(1)}, bf16[64,512]{1,0:T(8,128)(2,1)S(1)}, u32[]{:S(2)}, u32[]{:S(2)}) collective-permute-start(bf16[64,512]{1,0:T(8,128)(2,1)S(1)} %add.5.refs_0_), channel_id=1, source_target_pairs={{0,4},{1,5},{2,6},{3,7},{4,0},{5,1},{6,2},{7,3},{8,12},{9,13},{10,... | collective-permute-start | bytes 196616 | tf_op jit(solution)/shard_map/ppermute | solution.py:469
  88.4 5.2 %collective-permute-start.8 = (bf16[64,512]{1,0:T(8,128)(2,1)S(1)}, bf16[64,512]{1,0:T(8,128)(2,1)S(1)}, u32[]{:S(2)}, u32[]{:S(2)}) collective-permute-start(bf16[64,512]{1,0:T(8,128)(2,1)S(1)} %add.5.refs_0_), channel_id=1, source_target_pairs={{0,6},{1,7},{2,4},{3,5},{4,2},{5,3},{6,0},{7,1},{8,14},{9,15},{10,... | collective-permute-start | bytes 196616 | tf_op jit(solution)/shard_map/ppermute | solution.py:469
  93.6 1.6 %collective-permute-start.9 = (bf16[256,512]{1,0:T(8,128)(2,1)S(1)}, bf16[256,512]{1,0:T(8,128)(2,1)S(1)}, u32[]{:S(2)}, u32[]{:S(2)}) collective-permute-start(bf16[256,512]{1,0:T(8,128)(2,1)S(1)} %relay.1.half_ref), channel_id=1, source_target_pairs={{0,1},{1,0},{2,3},{3,2},{4,5},{5,4},{6,7},{7,6},{8,9},{9,8},{10,11... | collective-permute-start | bytes 786440 | tf_op jit(solution)/shard_map/ppermute | solution.py:469

commit v6 on v4

--- a/solution.py
+++ b/solution.py
@@ -50,17 +50,25 @@
     return pl.BlockSpec(shape, lambda i, *unused: (0,) * len(shape))
 
 
+def digits(index):
+    return (index >> 7).astype(F32).astype(BF16), (index & 127).astype(F32).astype(BF16)
+
+
 def collect_kernel(counts_ref, lists_ref, x_ref, out_ref):
     dests, slots = lists_ref.shape
     step = BIG // slots
-    lane = lax.broadcasted_iota(jnp.int32, (slots, x_ref.shape[0]), 1)
+    lane = lax.broadcasted_iota(jnp.int32, (slots, 128), 1).astype(F32).astype(BF16)
     slot = lax.broadcasted_iota(jnp.int32, (slots, 1), 0)
+    one, zero = jnp.ones((slots, 128), BF16), jnp.zeros((slots, 128), BF16)
     turned = lists_ref[...].T
     for first in range(0, dests, step):
         parts = []
         for d in range(first, first + step):
             named = jnp.where(slot < counts_ref[0, d], turned[:, d : d + 1], -1)
-            parts.append(jnp.where(named == lane, 1.0, 0.0).astype(BF16))
+            high, low = digits(jnp.broadcast_to(named, (slots, 128)))
+            hit = jnp.where(low == lane, one, zero)
+            tiles = [jnp.where(high == t, hit, zero) for t in range(x_ref.shape[0] // 128)]
+            parts.append(jnp.concatenate(tiles, axis=1))
         pick = jnp.concatenate(parts, axis=0)
         out_ref[first * slots : (first + step) * slots, :] = dot(pick, x_ref[...]).astype(BF16)
 
@@ -313,9 +321,14 @@
     for copy in coming:
         copy.start()
 
+    shape = (128, index_ref.shape[1])
+    high, low = digits(jnp.broadcast_to(index_ref[...], shape))
+    row = lax.broadcasted_iota(jnp.int32, shape, 0).astype(F32).astype(BF16)
+    hit = jnp.where(low == row, jnp.ones(shape, BF16), jnp.zeros(shape, BF16))
+
     def pick(n):
-        row = lax.broadcasted_iota(jnp.int32, (BIG, index_ref.shape[1]), 0) + n * BIG
-        return jnp.where(row == index_ref[...], 1.0, 0.0).astype(BF16)
+        tiles = [jnp.where(high == n * (BIG // 128) + t, hit, jnp.zeros(shape, BF16)) for t in range(BIG // 128)]
+        return jnp.concatenate(tiles, axis=0)
 
     sending = []
     for n, at in enumerate(views):
@@ -386,25 +399,30 @@
     )(*stored(after), *pieces)
 
 
-def join_kernel(chips, me_ref, mine_ref, other_ref, out_ref):
-    half = mine_ref.shape[0]
+def place_kernel(chips, other, me_ref, half_ref, *refs):
+    out_hbm, placed, sem = refs[-3:]
+    half = half_ref.shape[0]
     height = half // chips
-    core, chip = me_ref[0] % 2, me_ref[0] // 2
-    for owner, ref in ((core, mine_ref), (1 - core, other_ref)):
-        for k in range(chips):
-            at = pl.multiple_of(owner * half + (chip ^ k) * height, height)
-            out_ref[pl.ds(at, height), :] = ref[k * height : (k + 1) * height, :].astype(F32)
-
-
-def join(me, mine, other, chips):
-    half, width = mine.shape
-    return pl.pallas_call(
-        functools.partial(join_kernel, chips),
-        in_specs=[SMEM, VMEM, VMEM],
-        out_shape=jax.ShapeDtypeStruct((2 * half, width), F32),
+    for k in range(chips):
+        at = pl.multiple_of(((me_ref[0] // 2) ^ k) * height, height)
+        placed[pl.ds(at, height), :] = half_ref[k * height : (k + 1) * height, :].astype(F32)
+    at = pl.multiple_of((me_ref[0] + other) % 2 * half, half)
+    copy = pltpu.make_async_copy(placed, out_hbm.at[pl.ds(at, half)], sem)
+    copy.start()
+    copy.wait()
+
+
+def place(me, half, chips, into=()):
+    return pl.pallas_call(
+        functools.partial(place_kernel, chips, len(into)),
+        in_specs=[SMEM, VMEM] + [HBM] * len(into),
+        out_specs=HBM,
+        out_shape=far_made((2 * half.shape[0], half.shape[1]), F32),
+        scratch_shapes=[pltpu.VMEM(half.shape, F32), pltpu.SemaphoreType.DMA],
+        input_output_aliases={2: 0} if into else {},
         compiler_params=params(8),
-        name="join",
-    )(me, mine, other)
+        name="place",
+    )(me, half, *stored(*into))
 
 
 def add_kernel(after_ref, *refs):
@@ -454,7 +472,7 @@
         step, after = 2 * step, second
     pieces = [piece] + [swap(piece, "local", locals_, 2 * k) for k in range(1, chips)]
     half = relay(feature_grad, pieces)
-    weight_grad = join(me, half, swap(half, "local", locals_, 1), chips)
+    weight_grad = place(me, swap(half, "local", locals_, 1), chips, [place(me, half, chips)])
     return activated, feature_grad, weight_grad
 
 

time: 95.3 us -> 95.7 us (level)
  Pallas kernels: 56.9 us -> 58 us
  transfers between devices with their start and end apart: 12 -> 12, of which waited for: 6 -> 5; matrix products, arithmetic and copies ran while one was open for 0% -> 0% of each run, Pallas kernels for 41% -> 42%
where the time goes in v6:
time: 95.7 us; the launch traced here: 95.3 us
  Pallas kernels  58 us (61%)
  starting transfers between devices  22.6 us (24%)
  waiting for transfers between devices  13.5 us (14%)
  between operations  0.98 us (1%)
    pallas_call x1, Pallas kernels, build(): pl.pallas_call(build_kernel, grid_spec=pltpu.PrefetchScalarGridSpec(num_s...  19.5 us
    pallas_call x1, Pallas kernels, layer(): pl.pallas_call(layer_kernel, in_specs=[HBM] * 4 + [VMEM], out_specs=[HBM]...  12 us
    pallas_call x2, Pallas kernels, spread(): pl.pallas_call(spread_kernel, grid=(blocks,), in_specs=[pl.BlockSpec((own...  11.6 us
    ppermute x10, starting transfers between devices, swap(): return lax.ppermute(x, axis, [(i, i ^ k) for i in range(size)])  11.5 us
    all_to_all x2, starting transfers between devices, exchange(): return lax.all_to_all(x, axes, split_axis=0, concat_axis=0, tiled=True)  11.1 us
    ppermute x10, waiting for transfers between devices, swap(): return lax.ppermute(x, axis, [(i, i ^ k) for i in range(size)])  6.84 us
    all_to_all x2, waiting for transfers between devices, exchange(): return lax.all_to_all(x, axes, split_axis=0, concat_axis=0, tiled=True)  6.67 us
    pallas_call x1, Pallas kernels, collect(): pl.pallas_call(collect_kernel, in_specs=[SMEM, VMEM, VMEM], out_shape=jax...  5.19 us
  transfers between devices with their start and end apart: 12, of which 5 were waited for; matrix products, arithmetic and copies ran while one was open for 0% of the time, Pallas kernels for 42%

profile of v6, /device:TPU:0, one launch (start us, length us, event | category | flops | bytes accessed | tf_op | source)
XLA Modules:
  0.0 95.3 jit_solution(14462412396645217569)
XLA Ops:
  0.7 5.2 %collect.1 = bf16[1024,512]{1,0:T(8,128)(2,1)} custom-call(s32[1,32]{1,0:T(1,128)} %counts_ref.1, s32[32,32]{1,0:T(8,128)} %bitcast.11, bf16[2048,512]{1,0:T(8,128)(2,1)} %x_ref.3), custom_call_target="tpu_custom_call" | custom-call | tf_op jit(solution)/shard_map/collect/pallas_call | solution.py:78
  5.8 7.3 %all-to-all-start = ((bf16[32,32,512]{2,1,0:T(8,128)(2,1)}), bf16[32,32,512]{2,1,0:T(8,128)(2,1)S(1)}, u32[]{:S(2)}, u32[]{:S(2)}) async-start(bf16[32,32,512]{2,1,0:T(8,128)(2,1)} %bitcast.9), calls=%async_computation | async-start | bytes 2097152 | tf_op jit(solution)/shard_map/all_to_all | solution.py:364
  13.2 19.5 %build.1 = (bf16[2048,2048]{1,0:T(8,128)(2,1)}, bf16[2048,1024]{1,0:T(8,128)(2,1)}, f32[2048,512]{1,0:T(8,128)}) custom-call(s32[256]{0:T(256)S(1)} %copy-done.1, s32[256]{0:T(256)S(1)} %copy-done.2, bf16[256,128,128]{2,1,0:T(8,128)(2,1)} %tiles_ref.1, bf16[2048,512]{1,0:T(8,128)(2,1)S(1)} %copy-done), custom_call_target="tpu_custom_call" | custom-call | flops 4294967296 | bytes 41943040 | tf_op jit(solution)/shard_map/build/pallas_call | solution.py:146
  32.7 6.7 %all-to-all-done = bf16[32,32,512]{2,1,0:T(8,128)(2,1)S(1)} async-done(((bf16[32,32,512]{2,1,0:T(8,128)(2,1)}), bf16[32,32,512]{2,1,0:T(8,128)(2,1)S(1)}, u32[]{:S(2)}, u32[]{:S(2)}) %all-to-all-start) | async-done | bytes 1048608 | tf_op jit(solution)/shard_map/all_to_all | solution.py:364
  39.4 12.0 %layer.1 = (bf16[2048,512]{1,0:T(8,128)(2,1)}, bf16[2048,512]{1,0:T(8,128)(2,1)}, bf16[2048,512]{1,0:T(8,128)(2,1)}, bf16[2048,512]{1,0:T(8,128)(2,1)}, bf16[1024,512]{1,0:T(8,128)(2,1)}) custom-call(bf16[2048,1024]{1,0:T(8,128)(2,1)} %get-tuple-element.17.far_hbm, f32[2048,512]{1,0:T(8,128)} %get-tuple-element.18.own_hbm, bf16[2048,512]{1,0:T(8,128)(2,1)} %cot_hbm.1, ...), custom_call_target="tpu_custom_call" | custom-call | tf_op jit(solution)/shard_map/layer/pallas_call | solution.py:234
  51.4 3.8 %all-to-all-start.1 = ((bf16[32,32,512]{2,1,0:T(8,128)(2,1)}), bf16[32,32,512]{2,1,0:T(8,128)(2,1)S(1)}, u32[]{:S(2)}, u32[]{:S(2)}) async-start(bf16[32,32,512]{2,1,0:T(8,128)(2,1)} %bitcast.10), calls=%async_computation.1 | async-start | bytes 2097152 | tf_op jit(solution)/shard_map/all_to_all | solution.py:364
  55.2 2.9 %partial_grad.1 = (f32[256,512]{1,0:T(8,128)S(1)}, bf16[256,512]{1,0:T(8,128)(2,1)S(1)}) custom-call(s32[1]{0:T(128)} %bitcast.6.me_ref, bf16[2048,512]{1,0:T(8,128)(2,1)} %get-tuple-element.23.hid_hbm, bf16[2048,512]{1,0:T(8,128)(2,1)} %get-tuple-element.24.slope_hbm), custom_call_target="tpu_custom_call" | custom-call | tf_op jit(solution)/shard_map/partial_grad/pallas_call | solution.py:277
  58.1 0.1 collective-permute-start
  58.3 1.5 %collective-permute-done.got_ref = bf16[256,512]{1,0:T(8,128)(2,1)S(1)} collective-permute-done((bf16[256,512]{1,0:T(8,128)(2,1)S(1)}, bf16[256,512]{1,0:T(8,128)(2,1)S(1)}, u32[]{:S(2)}, u32[]{:S(2)}) %collective-permute-start) | collective-permute-done | bytes 262176 | tf_op jit(solution)/shard_map/ppermute | solution.py:446
  59.8 1.7 %collective-permute-start.1 = (bf16[64,512]{1,0:T(8,128)(2,1)S(1)}, bf16[64,512]{1,0:T(8,128)(2,1)S(1)}, u32[]{:S(2)}, u32[]{:S(2)}) collective-permute-start(bf16[64,512]{1,0:T(8,128)(2,1)S(1)} %get-tuple-element.28), channel_id=1, source_target_pairs={{0,2},{1,3},{2,0},{3,1},{4,6},{5,7},{6,4},{7,5},{8,10},{9,11},{10,... | collective-permute-start | bytes 196616 | tf_op jit(solution)/shard_map/ppermute | solution.py:446
  61.4 1.5 %collective-permute-start.2 = (bf16[64,512]{1,0:T(8,128)(2,1)S(1)}, bf16[64,512]{1,0:T(8,128)(2,1)S(1)}, u32[]{:S(2)}, u32[]{:S(2)}) collective-permute-start(bf16[64,512]{1,0:T(8,128)(2,1)S(1)} %get-tuple-element.29), channel_id=1, source_target_pairs={{0,4},{1,5},{2,6},{3,7},{4,0},{5,1},{6,2},{7,3},{8,12},{9,13},{10,... | collective-permute-start | bytes 196616 | tf_op jit(solution)/shard_map/ppermute | solution.py:446
  62.9 0.4 collective-permute-start.3
  63.3 5.8 %spread.2.first_hbm.after_ref = f32[1024,512]{1,0:T(8,128)} custom-call(bf16[2048,2048]{1,0:T(8,128)(2,1)} %get-tuple-element.20.adj_ref, bf16[2048,512]{1,0:T(8,128)(2,1)} %get-tuple-element.21.grad_ref), custom_call_target="tpu_custom_call" | custom-call | flops 4294967296 | bytes 16777216 | tf_op jit(solution)/shard_map/spread/pallas_call | solution.py:300
  69.1 0.0 collective-permute-done.1.refs_1_
  69.1 0.0 collective-permute-done.2.refs_2_
  69.1 1.0 %collective-permute-done.3.refs_3_ = bf16[64,512]{1,0:T(8,128)(2,1)S(1)} collective-permute-done((bf16[64,512]{1,0:T(8,128)(2,1)S(1)}, bf16[64,512]{1,0:T(8,128)(2,1)S(1)}, u32[]{:S(2)}, u32[]{:S(2)}) %collective-permute-start.3) | collective-permute-done | bytes 65568 | tf_op jit(solution)/shard_map/ppermute | solution.py:446
  70.1 1.1 %collective-permute-start.4 = (bf16[64,512]{1,0:T(8,128)(2,1)S(1)}, bf16[64,512]{1,0:T(8,128)(2,1)S(1)}, u32[]{:S(2)}, u32[]{:S(2)}) collective-permute-start(bf16[64,512]{1,0:T(8,128)(2,1)S(1)} %add.3.refs_0_), channel_id=1, source_target_pairs={{0,8},{8,0},{16,24},{24,16},{1,9},{9,1},{17,25},{25,17},{2,10},{10... | collective-permute-start | bytes 196616 | tf_op jit(solution)/shard_map/ppermute | solution.py:446
  71.2 5.8 %spread.3.second_hbm.after_ref = f32[1024,512]{1,0:T(8,128)} custom-call(bf16[2048,2048]{1,0:T(8,128)(2,1)} %get-tuple-element.20.adj_ref, bf16[2048,512]{1,0:T(8,128)(2,1)} %get-tuple-element.21.grad_ref), custom_call_target="tpu_custom_call" | custom-call | flops 4294967296 | bytes 16777216 | tf_op jit(solution)/shard_map/spread/pallas_call | solution.py:300
  77.0 0.0 collective-permute-done.4.refs_1_
  77.0 3.1 %collective-permute-start.5 = (bf16[64,512]{1,0:T(8,128)(2,1)S(1)}, bf16[64,512]{1,0:T(8,128)(2,1)S(1)}, u32[]{:S(2)}, u32[]{:S(2)}) collective-permute-start(bf16[64,512]{1,0:T(8,128)(2,1)S(1)} %add.4.refs_0_), channel_id=1, source_target_pairs={{0,16},{8,24},{16,0},{24,8},{1,17},{9,25},{17,1},{25,9},{2,18},{10... | collective-permute-start | bytes 196616 | tf_op jit(solution)/shard_map/ppermute | solution.py:446
  80.1 0.1 iota_compare_fusion
  80.2 0.1 squeeze.6
  80.3 0.1 lt.29
  80.3 3.7 %collective-permute-done.5.refs_1_ = bf16[64,512]{1,0:T(8,128)(2,1)S(1)} collective-permute-done((bf16[64,512]{1,0:T(8,128)(2,1)S(1)}, bf16[64,512]{1,0:T(8,128)(2,1)S(1)}, u32[]{:S(2)}, u32[]{:S(2)}) %collective-permute-start.5) | collective-permute-done | bytes 65568 | tf_op jit(solution)/shard_map/ppermute | solution.py:446
  84.1 1.5 %collective-permute-start.6 = (bf16[64,512]{1,0:T(8,128)(2,1)S(1)}, bf16[64,512]{1,0:T(8,128)(2,1)S(1)}, u32[]{:S(2)}, u32[]{:S(2)}) collective-permute-start(bf16[64,512]{1,0:T(8,128)(2,1)S(1)} %add.5.refs_0_), channel_id=1, source_target_pairs={{0,2},{1,3},{2,0},{3,1},{4,6},{5,7},{6,4},{7,5},{8,10},{9,11},{10,... | collective-permute-start | bytes 196616 | tf_op jit(solution)/shard_map/ppermute | solution.py:446
  85.6 1.5 %collective-permute-start.7 = (bf16[64,512]{1,0:T(8,128)(2,1)S(1)}, bf16[64,512]{1,0:T(8,128)(2,1)S(1)}, u32[]{:S(2)}, u32[]{:S(2)}) collective-permute-start(bf16[64,512]{1,0:T(8,128)(2,1)S(1)} %add.5.refs_0_), channel_id=1, source_target_pairs={{0,4},{1,5},{2,6},{3,7},{4,0},{5,1},{6,2},{7,3},{8,12},{9,13},{10,... | collective-permute-start | bytes 196616 | tf_op jit(solution)/shard_map/ppermute | solution.py:446
  87.1 0.5 collective-permute-start.8
  87.7 5.0 %give_back.1.after_ref = bf16[2048,512]{1,0:T(8,128)(2,1)} custom-call(s32[1,1024]{1,0:T(1,128)S(1)} %broadcast_select_fusion.index_ref, f32[1024,512]{1,0:T(8,128)} %spread.2.first_hbm.after_ref, f32[1024,512]{1,0:T(8,128)} %spread.3.second_hbm.after_ref, bf16[1024,512]{1,0:T(8,128)(2,1)S(1)} %bitcast.7), custom_call_target="tpu_custom_call" | custom-call | tf_op jit(solution)/shard_map/give_back/pallas_call | solution.py:347
  92.7 0.1 collective-permute-start.9
  92.8 0.8 place.2.refs_0_
  93.7 0.7 collective-permute-done.9.half_ref
  94.3 0.8 place.3
  (20 shorter events, 0.2 us)
Async XLA Ops:
  0.6 12.5 %copy-start = (bf16[2048,512]{1,0:T(8,128)(2,1)S(1)}, bf16[2048,512]{1,0:T(8,128)(2,1)}, u32[]{:S(2)}) copy-start(bf16[2048,512]{1,0:T(8,128)(2,1)} %x_ref.3) | copy-start | bytes 6291460
  0.6 12.5 %copy-start.1 = (s32[256]{0:T(256)S(1)}, s32[256]{0:T(256)}, u32[]{:S(2)}) copy-start(s32[256]{0:T(256)} %rows_ref.1) | copy-start | bytes 3076
  0.7 12.5 %copy-start.2 = (s32[256]{0:T(256)S(1)}, s32[256]{0:T(256)}, u32[]{:S(2)}) copy-start(s32[256]{0:T(256)} %cols_ref.1) | copy-start | bytes 3076
  5.8 33.5 %all-to-all-start = ((bf16[32,32,512]{2,1,0:T(8,128)(2,1)}), bf16[32,32,512]{2,1,0:T(8,128)(2,1)S(1)}, u32[]{:S(2)}, u32[]{:S(2)}) async-start(bf16[32,32,512]{2,1,0:T(8,128)(2,1)} %bitcast.9), calls=%async_computation | async-start | bytes 2097152 | tf_op jit(solution)/shard_map/all_to_all | solution.py:364
  51.4 36.3 %all-to-all-start.1 = ((bf16[32,32,512]{2,1,0:T(8,128)(2,1)}), bf16[32,32,512]{2,1,0:T(8,128)(2,1)S(1)}, u32[]{:S(2)}, u32[]{:S(2)}) async-start(bf16[32,32,512]{2,1,0:T(8,128)(2,1)} %bitcast.10), calls=%async_computation.1 | async-start | bytes 2097152 | tf_op jit(solution)/shard_map/all_to_all | solution.py:364
  58.1 1.6 %collective-permute-start = (bf16[256,512]{1,0:T(8,128)(2,1)S(1)}, bf16[256,512]{1,0:T(8,128)(2,1)S(1)}, u32[]{:S(2)}, u32[]{:S(2)}) collective-permute-start(bf16[256,512]{1,0:T(8,128)(2,1)S(1)} %get-tuple-element.26), channel_id=1, source_target_pairs={{0,1},{1,0},{2,3},{3,2},{4,5},{5,4},{6,7},{7,6},{8,9},{9,8},{10,11... | collective-permute-start | bytes 786440 | tf_op jit(solution)/shard_map/ppermute | solution.py:446
  59.8 9.3 %collective-permute-start.1 = (bf16[64,512]{1,0:T(8,128)(2,1)S(1)}, bf16[64,512]{1,0:T(8,128)(2,1)S(1)}, u32[]{:S(2)}, u32[]{:S(2)}) collective-permute-start(bf16[64,512]{1,0:T(8,128)(2,1)S(1)} %get-tuple-element.28), channel_id=1, source_target_pairs={{0,2},{1,3},{2,0},{3,1},{4,6},{5,7},{6,4},{7,5},{8,10},{9,11},{10,... | collective-permute-start | bytes 196616 | tf_op jit(solution)/shard_map/ppermute | solution.py:446
  61.4 7.7 %collective-permute-start.2 = (bf16[64,512]{1,0:T(8,128)(2,1)S(1)}, bf16[64,512]{1,0:T(8,128)(2,1)S(1)}, u32[]{:S(2)}, u32[]{:S(2)}) collective-permute-start(bf16[64,512]{1,0:T(8,128)(2,1)S(1)} %get-tuple-element.29), channel_id=1, source_target_pairs={{0,4},{1,5},{2,6},{3,7},{4,0},{5,1},{6,2},{7,3},{8,12},{9,13},{10,... | collective-permute-start | bytes 196616 | tf_op jit(solution)/shard_map/ppermute | solution.py:446
  62.9 7.2 %collective-permute-start.3 = (bf16[64,512]{1,0:T(8,128)(2,1)S(1)}, bf16[64,512]{1,0:T(8,128)(2,1)S(1)}, u32[]{:S(2)}, u32[]{:S(2)}) collective-permute-start(bf16[64,512]{1,0:T(8,128)(2,1)S(1)} %get-tuple-element.30), channel_id=1, source_target_pairs={{0,6},{1,7},{2,4},{3,5},{4,2},{5,3},{6,0},{7,1},{8,14},{9,15},{10,... | collective-permute-start | bytes 196616 | tf_op jit(solution)/shard_map/ppermute | solution.py:446
  70.1 6.9 %collective-permute-start.4 = (bf16[64,512]{1,0:T(8,128)(2,1)S(1)}, bf16[64,512]{1,0:T(8,128)(2,1)S(1)}, u32[]{:S(2)}, u32[]{:S(2)}) collective-permute-start(bf16[64,512]{1,0:T(8,128)(2,1)S(1)} %add.3.refs_0_), channel_id=1, source_target_pairs={{0,8},{8,0},{16,24},{24,16},{1,9},{9,1},{17,25},{25,17},{2,10},{10... | collective-permute-start | bytes 196616 | tf_op jit(solution)/shard_map/ppermute | solution.py:446
  77.0 3.1 %copy-start.4 = (s32[1,32]{1,0:T(1,128)S(1)}, s32[1,32]{1,0:T(1,128)}, u32[]{:S(2)}) copy-start(s32[1,32]{1,0:T(1,128)} %counts_ref.1) | copy-start | bytes 388
  77.0 3.2 %copy-start.3 = (s32[1,32,32]{2,1,0:T(8,128)S(1)}, s32[1,32,32]{2,1,0:T(8,128)}, u32[]{:S(2)}) copy-start(s32[1,32,32]{2,1,0:T(8,128)} %param.14) | copy-start | bytes 12292
  77.0 7.1 %collective-permute-start.5 = (bf16[64,512]{1,0:T(8,128)(2,1)S(1)}, bf16[64,512]{1,0:T(8,128)(2,1)S(1)}, u32[]{:S(2)}, u32[]{:S(2)}) collective-permute-start(bf16[64,512]{1,0:T(8,128)(2,1)S(1)} %add.4.refs_0_), channel_id=1, source_target_pairs={{0,16},{8,24},{16,0},{24,8},{1,17},{9,25},{17,1},{25,9},{2,18},{10... | collective-permute-start | bytes 196616 | tf_op jit(solution)/shard_map/ppermute | solution.py:446
  84.1 8.5 %collective-permute-start.6 = (bf16[64,512]{1,0:T(8,128)(2,1)S(1)}, bf16[64,512]{1,0:T(8,128)(2,1)S(1)}, u32[]{:S(2)}, u32[]{:S(2)}) collective-permute-start(bf16[64,512]{1,0:T(8,128)(2,1)S(1)} %add.5.refs_0_), channel_id=1, source_target_pairs={{0,2},{1,3},{2,0},{3,1},{4,6},{5,7},{6,4},{7,5},{8,10},{9,11},{10,... | collective-permute-start | bytes 196616 | tf_op jit(solution)/shard_map/ppermute | solution.py:446
  85.6 7.0 %collective-permute-start.7 = (bf16[64,512]{1,0:T(8,128)(2,1)S(1)}, bf16[64,512]{1,0:T(8,128)(2,1)S(1)}, u32[]{:S(2)}, u32[]{:S(2)}) collective-permute-start(bf16[64,512]{1,0:T(8,128)(2,1)S(1)} %add.5.refs_0_), channel_id=1, source_target_pairs={{0,4},{1,5},{2,6},{3,7},{4,0},{5,1},{6,2},{7,3},{8,12},{9,13},{10,... | collective-permute-start | bytes 196616 | tf_op jit(solution)/shard_map/ppermute | solution.py:446
  87.1 5.5 %collective-permute-start.8 = (bf16[64,512]{1,0:T(8,128)(2,1)S(1)}, bf16[64,512]{1,0:T(8,128)(2,1)S(1)}, u32[]{:S(2)}, u32[]{:S(2)}) collective-permute-start(bf16[64,512]{1,0:T(8,128)(2,1)S(1)} %add.5.refs_0_), channel_id=1, source_target_pairs={{0,6},{1,7},{2,4},{3,5},{4,2},{5,3},{6,0},{7,1},{8,14},{9,15},{10,... | collective-permute-start | bytes 196616 | tf_op jit(solution)/shard_map/ppermute | solution.py:446
  92.7 1.6 %collective-permute-start.9 = (bf16[256,512]{1,0:T(8,128)(2,1)S(1)}, bf16[256,512]{1,0:T(8,128)(2,1)S(1)}, u32[]{:S(2)}, u32[]{:S(2)}) collective-permute-start(bf16[256,512]{1,0:T(8,128)(2,1)S(1)} %relay.1.half_ref), channel_id=1, source_target_pairs={{0,1},{1,0},{2,3},{3,2},{4,5},{5,4},{6,7},{7,6},{8,9},{9,8},{10,11... | collective-permute-start | bytes 786440 | tf_op jit(solution)/shard_map/ppermute | solution.py:446

commit v7 on v6

--- a/solution.py
+++ b/solution.py
@@ -50,25 +50,17 @@
     return pl.BlockSpec(shape, lambda i, *unused: (0,) * len(shape))
 
 
-def digits(index):
-    return (index >> 7).astype(F32).astype(BF16), (index & 127).astype(F32).astype(BF16)
-
-
 def collect_kernel(counts_ref, lists_ref, x_ref, out_ref):
     dests, slots = lists_ref.shape
     step = BIG // slots
-    lane = lax.broadcasted_iota(jnp.int32, (slots, 128), 1).astype(F32).astype(BF16)
+    lane = lax.broadcasted_iota(jnp.int32, (slots, x_ref.shape[0]), 1)
     slot = lax.broadcasted_iota(jnp.int32, (slots, 1), 0)
-    one, zero = jnp.ones((slots, 128), BF16), jnp.zeros((slots, 128), BF16)
     turned = lists_ref[...].T
     for first in range(0, dests, step):
         parts = []
         for d in range(first, first + step):
             named = jnp.where(slot < counts_ref[0, d], turned[:, d : d + 1], -1)
-            high, low = digits(jnp.broadcast_to(named, (slots, 128)))
-            hit = jnp.where(low == lane, one, zero)
-            tiles = [jnp.where(high == t, hit, zero) for t in range(x_ref.shape[0] // 128)]
-            parts.append(jnp.concatenate(tiles, axis=1))
+            parts.append(jnp.where(named == lane, 1.0, 0.0).astype(BF16))
         pick = jnp.concatenate(parts, axis=0)
         out_ref[first * slots : (first + step) * slots, :] = dot(pick, x_ref[...]).astype(BF16)
 
@@ -311,53 +303,47 @@
     )(*stored(adjacency, grad))
 
 
-def return_kernel(index_ref, first_hbm, second_hbm, got_ref, out_hbm, owned, out, sems, sent):
-    blocks = sems.shape[0]
-    views = [pl.ds(n * BIG, BIG) for n in range(blocks)]
-    coming = []
-    for n, at in enumerate(views):
-        half_hbm = (first_hbm, second_hbm)[2 * n // blocks]
-        coming.append(pltpu.make_async_copy(half_hbm.at[views[n % (blocks // 2)]], owned.at[at], sems.at[n]))
+def return_kernel(part, index_ref, owned_hbm, got_ref, *refs):
+    out_hbm, owned, out, sems, sent = refs[-5:]
+    views = [pl.ds(n * BIG, BIG) for n in range(sems.shape[0])]
+    coming = [pltpu.make_async_copy(owned_hbm.at[at], owned.at[at], sems.at[n]) for n, at in enumerate(views)]
     for copy in coming:
         copy.start()
-
-    shape = (128, index_ref.shape[1])
-    high, low = digits(jnp.broadcast_to(index_ref[...], shape))
-    row = lax.broadcasted_iota(jnp.int32, shape, 0).astype(F32).astype(BF16)
-    hit = jnp.where(low == row, jnp.ones(shape, BF16), jnp.zeros(shape, BF16))
+    base = part * owned.shape[0]
 
     def pick(n):
-        tiles = [jnp.where(high == n * (BIG // 128) + t, hit, jnp.zeros(shape, BF16)) for t in range(BIG // 128)]
-        return jnp.concatenate(tiles, axis=0)
+        row = lax.broadcasted_iota(jnp.int32, (BIG, index_ref.shape[1]), 0) + (base + n * BIG)
+        return jnp.where(row == index_ref[...], 1.0, 0.0).astype(BF16)
 
     sending = []
     for n, at in enumerate(views):
         added = dot(pick(n), got_ref[...])
         coming[n].wait()
         out[at, :] = (owned[at, :] + added).astype(BF16)
-        sending.append(pltpu.make_async_copy(out.at[at], out_hbm.at[at], sent.at[n]))
+        sending.append(pltpu.make_async_copy(out.at[at], out_hbm.at[pl.ds(base + n * BIG, BIG)], sent.at[n]))
         sending[n].start()
     for copy in sending:
         copy.wait()
 
 
-def give_back(keep, index, first, second, got):
-    rows, width = 2 * first.shape[0], first.shape[1]
+def give_back(keep, index, owned, got, part, parts, into=()):
+    rows, width = owned.shape
     (got,) = held(keep, got)
     return pl.pallas_call(
-        return_kernel,
-        in_specs=[VMEM, HBM, HBM, VMEM],
+        functools.partial(return_kernel, part),
+        in_specs=[VMEM, HBM, VMEM] + [HBM] * len(into[:1]) + [VMEM] * len(into[1:]),
         out_specs=HBM,
-        out_shape=far_made((rows, width), BF16),
+        out_shape=far_made((parts * rows, width), BF16),
         scratch_shapes=[
             pltpu.VMEM((rows, width), F32),
             pltpu.VMEM((rows, width), BF16),
             pltpu.SemaphoreType.DMA((rows // BIG,)),
             pltpu.SemaphoreType.DMA((rows // BIG,)),
         ],
+        input_output_aliases={3: 0} if into else {},
         compiler_params=params(28 if keep else 60),
         name="give_back",
-    )(index, *stored(first, second), got)
+    )(index, *stored(owned), got, *stored(*into[:1]), *into[1:])
 
 
 def exchange(x, axes):
@@ -461,7 +447,8 @@
     first = spread(adjacency, grad, 0, 2)
     second = spread(adjacency, grad, 1, 2)
     live = jnp.arange(slots)[None, :] < counts[0][:, None]
-    feature_grad = give_back(keep, jnp.where(live, lists, -1).reshape(1, remote), first, second, returned)
+    index = jnp.where(live, lists, -1).reshape(1, remote)
+    feature_grad = give_back(keep, index, first, returned, 0, 2)
     chips = locals_ // 2
     mine, other = partial_grad(keep, me, hidden, slope)
     pieces = cut(me, mine, swap(other, "local", locals_, 1), chips)
@@ -469,8 +456,9 @@
     step, after = 1, second
     while step < groups:
         piece = add(after, [piece, swap(piece, "group", groups, step)])
-        step, after = 2 * step, second
+        step, after = 2 * step, feature_grad
     pieces = [piece] + [swap(piece, "local", locals_, 2 * k) for k in range(1, chips)]
+    feature_grad = give_back(keep, index, second, returned, 1, 2, [feature_grad, piece])
     half = relay(feature_grad, pieces)
     weight_grad = place(me, swap(half, "local", locals_, 1), chips, [place(me, half, chips)])
     return activated, feature_grad, weight_grad

time: 95.7 us -> 97.4 us (1.018)
  Pallas kernels: 58 us -> 59 us
    all_to_all x2, waiting for transfers between devices: 6.67 us -> 9.74 us  [exchange(): return lax.all_to_all(x, axes, split_axis=0, concat_axis=0, tiled=True)]
    ppermute x10, waiting for transfers between devices: 6.84 us -> 4.43 us  [swap(): return lax.ppermute(x, axis, [(i, i ^ k) for i in range(size)])]
    pallas_call x1 -> x2, Pallas kernels: 4.96 us -> 5.95 us  [give_back(): pl.pallas_call(functools.partial(return_kernel, part), in_specs=[VMEM, HB...]
  transfers between devices with their start and end apart: 12 -> 12, of which waited for: 5 -> 6; matrix products, arithmetic and copies ran while one was open for 0% -> 0% of each run, Pallas kernels for 42% -> 42%
where the time goes in v7:
time: 97.4 us; the launch traced here: 97 us
  Pallas kernels  59 us (61%)
  starting transfers between devices  22.6 us (23%)
  waiting for transfers between devices  14.2 us (15%)
  between operations  0.99 us (1%)
    pallas_call x1, Pallas kernels, build(): pl.pallas_call(build_kernel, grid_spec=pltpu.PrefetchScalarGridSpec(num_s...  19.5 us
    pallas_call x1, Pallas kernels, layer(): pl.pallas_call(layer_kernel, in_specs=[HBM] * 4 + [VMEM], out_specs=[HBM]...  12 us
    pallas_call x2, Pallas kernels, spread(): pl.pallas_call(spread_kernel, grid=(blocks,), in_specs=[pl.BlockSpec((own...  11.6 us
    ppermute x10, starting transfers between devices, swap(): return lax.ppermute(x, axis, [(i, i ^ k) for i in range(size)])  11.5 us
    all_to_all x2, starting transfers between devices, exchange(): return lax.all_to_all(x, axes, split_axis=0, concat_axis=0, tiled=True)  11.1 us
    all_to_all x2, waiting for transfers between devices, exchange(): return lax.all_to_all(x, axes, split_axis=0, concat_axis=0, tiled=True)  9.74 us
    pallas_call x2, Pallas kernels, give_back(): pl.pallas_call(functools.partial(return_kernel, part), in_specs=[VMEM, HB...  5.95 us
    pallas_call x1, Pallas kernels, collect(): pl.pallas_call(collect_kernel, in_specs=[SMEM, VMEM, VMEM], out_shape=jax...  5.17 us
  transfers between devices with their start and end apart: 12, of which 6 were waited for; matrix products, arithmetic and copies ran while one was open for 0% of the time, Pallas kernels for 42%

profile of v7, /device:TPU:0, one launch (start us, length us, event | category | flops | bytes accessed | tf_op | source)
XLA Modules:
  0.0 97.0 jit_solution(4452072442486079873)
XLA Ops:
  0.7 5.2 %collect.1 = bf16[1024,512]{1,0:T(8,128)(2,1)} custom-call(s32[1,32]{1,0:T(1,128)} %counts_ref.1, s32[32,32]{1,0:T(8,128)} %bitcast.12, bf16[2048,512]{1,0:T(8,128)(2,1)} %x_ref.3), custom_call_target="tpu_custom_call" | custom-call | tf_op jit(solution)/shard_map/collect/pallas_call | solution.py:70
  5.8 7.3 %all-to-all-start = ((bf16[32,32,512]{2,1,0:T(8,128)(2,1)}), bf16[32,32,512]{2,1,0:T(8,128)(2,1)S(1)}, u32[]{:S(2)}, u32[]{:S(2)}) async-start(bf16[32,32,512]{2,1,0:T(8,128)(2,1)} %bitcast.10), calls=%async_computation | async-start | bytes 2097152 | tf_op jit(solution)/shard_map/all_to_all | solution.py:350
  13.2 19.5 %build.1 = (bf16[2048,2048]{1,0:T(8,128)(2,1)}, bf16[2048,1024]{1,0:T(8,128)(2,1)}, f32[2048,512]{1,0:T(8,128)}) custom-call(s32[256]{0:T(256)S(1)} %copy-done.1, s32[256]{0:T(256)S(1)} %copy-done.2, bf16[256,128,128]{2,1,0:T(8,128)(2,1)} %tiles_ref.1, bf16[2048,512]{1,0:T(8,128)(2,1)S(1)} %copy-done), custom_call_target="tpu_custom_call" | custom-call | flops 4294967296 | bytes 41943040 | tf_op jit(solution)/shard_map/build/pallas_call | solution.py:138
  32.7 6.7 %all-to-all-done = bf16[32,32,512]{2,1,0:T(8,128)(2,1)S(1)} async-done(((bf16[32,32,512]{2,1,0:T(8,128)(2,1)}), bf16[32,32,512]{2,1,0:T(8,128)(2,1)S(1)}, u32[]{:S(2)}, u32[]{:S(2)}) %all-to-all-start) | async-done | bytes 1048608 | tf_op jit(solution)/shard_map/all_to_all | solution.py:350
  39.4 12.0 %layer.1 = (bf16[2048,512]{1,0:T(8,128)(2,1)}, bf16[2048,512]{1,0:T(8,128)(2,1)}, bf16[2048,512]{1,0:T(8,128)(2,1)}, bf16[2048,512]{1,0:T(8,128)(2,1)}, bf16[1024,512]{1,0:T(8,128)(2,1)}) custom-call(bf16[2048,1024]{1,0:T(8,128)(2,1)} %get-tuple-element.17.far_hbm, f32[2048,512]{1,0:T(8,128)} %get-tuple-element.18.own_hbm, bf16[2048,512]{1,0:T(8,128)(2,1)} %cot_hbm.1, ...), custom_call_target="tpu_custom_call" | custom-call | tf_op jit(solution)/shard_map/layer/pallas_call | solution.py:226
  51.4 3.8 %all-to-all-start.1 = ((bf16[32,32,512]{2,1,0:T(8,128)(2,1)}), bf16[32,32,512]{2,1,0:T(8,128)(2,1)S(1)}, u32[]{:S(2)}, u32[]{:S(2)}) async-start(bf16[32,32,512]{2,1,0:T(8,128)(2,1)} %bitcast.11), calls=%async_computation.1 | async-start | bytes 2097152 | tf_op jit(solution)/shard_map/all_to_all | solution.py:350
  55.2 0.0 copy-start.3
  55.2 2.9 %partial_grad.1 = (f32[256,512]{1,0:T(8,128)S(1)}, bf16[256,512]{1,0:T(8,128)(2,1)S(1)}) custom-call(s32[1]{0:T(128)} %bitcast.6.me_ref, bf16[2048,512]{1,0:T(8,128)(2,1)} %get-tuple-element.23.hid_hbm, bf16[2048,512]{1,0:T(8,128)(2,1)} %get-tuple-element.24.slope_hbm), custom_call_target="tpu_custom_call" | custom-call | tf_op jit(solution)/shard_map/partial_grad/pallas_call | solution.py:269
  58.1 0.1 collective-permute-start
  58.3 0.1 squeeze.6
  58.4 0.1 iota_compare_fusion
  58.4 0.1 lt.29
  58.5 1.2 %collective-permute-done.got_ref = bf16[256,512]{1,0:T(8,128)(2,1)S(1)} collective-permute-done((bf16[256,512]{1,0:T(8,128)(2,1)S(1)}, bf16[256,512]{1,0:T(8,128)(2,1)S(1)}, u32[]{:S(2)}, u32[]{:S(2)}) %collective-permute-start) | collective-permute-done | bytes 262176 | tf_op jit(solution)/shard_map/ppermute | solution.py:432
  59.8 1.7 %collective-permute-start.1 = (bf16[64,512]{1,0:T(8,128)(2,1)S(1)}, bf16[64,512]{1,0:T(8,128)(2,1)S(1)}, u32[]{:S(2)}, u32[]{:S(2)}) collective-permute-start(bf16[64,512]{1,0:T(8,128)(2,1)S(1)} %get-tuple-element.28), channel_id=1, source_target_pairs={{0,2},{1,3},{2,0},{3,1},{4,6},{5,7},{6,4},{7,5},{8,10},{9,11},{10,... | collective-permute-start | bytes 196616 | tf_op jit(solution)/shard_map/ppermute | solution.py:432
  61.4 1.5 %collective-permute-start.2 = (bf16[64,512]{1,0:T(8,128)(2,1)S(1)}, bf16[64,512]{1,0:T(8,128)(2,1)S(1)}, u32[]{:S(2)}, u32[]{:S(2)}) collective-permute-start(bf16[64,512]{1,0:T(8,128)(2,1)S(1)} %get-tuple-element.29), channel_id=1, source_target_pairs={{0,4},{1,5},{2,6},{3,7},{4,0},{5,1},{6,2},{7,3},{8,12},{9,13},{10,... | collective-permute-start | bytes 196616 | tf_op jit(solution)/shard_map/ppermute | solution.py:432
  62.9 0.4 collective-permute-start.3
  63.3 5.8 %spread.3.owned_hbm.after_ref = f32[1024,512]{1,0:T(8,128)} custom-call(bf16[2048,2048]{1,0:T(8,128)(2,1)} %get-tuple-element.20.adj_ref, bf16[2048,512]{1,0:T(8,128)(2,1)} %get-tuple-element.21.grad_ref), custom_call_target="tpu_custom_call" | custom-call | flops 4294967296 | bytes 16777216 | tf_op jit(solution)/shard_map/spread/pallas_call | solution.py:292
  69.2 0.9 collective-permute-done.3.refs_3_
  70.1 1.1 %collective-permute-start.4 = (bf16[64,512]{1,0:T(8,128)(2,1)S(1)}, bf16[64,512]{1,0:T(8,128)(2,1)S(1)}, u32[]{:S(2)}, u32[]{:S(2)}) collective-permute-start(bf16[64,512]{1,0:T(8,128)(2,1)S(1)} %add.3.refs_0_), channel_id=1, source_target_pairs={{0,8},{8,0},{16,24},{24,16},{1,9},{9,1},{17,25},{25,17},{2,10},{10... | collective-permute-start | bytes 196616 | tf_op jit(solution)/shard_map/ppermute | solution.py:432
  71.2 5.8 %spread.2.after_ref.owned_hbm = f32[1024,512]{1,0:T(8,128)} custom-call(bf16[2048,2048]{1,0:T(8,128)(2,1)} %get-tuple-element.20.adj_ref, bf16[2048,512]{1,0:T(8,128)(2,1)} %get-tuple-element.21.grad_ref), custom_call_target="tpu_custom_call" | custom-call | flops 4294967296 | bytes 16777216 | tf_op jit(solution)/shard_map/spread/pallas_call | solution.py:292
  77.0 3.0 %collective-permute-start.5 = (bf16[64,512]{1,0:T(8,128)(2,1)S(1)}, bf16[64,512]{1,0:T(8,128)(2,1)S(1)}, u32[]{:S(2)}, u32[]{:S(2)}) collective-permute-start(bf16[64,512]{1,0:T(8,128)(2,1)S(1)} %add.4.refs_0_), channel_id=1, source_target_pairs={{0,16},{8,24},{16,0},{24,8},{1,17},{9,25},{17,1},{25,9},{2,18},{10... | collective-permute-start | bytes 196616 | tf_op jit(solution)/shard_map/ppermute | solution.py:432
  80.1 3.1 %all-to-all-done.1 = bf16[32,32,512]{2,1,0:T(8,128)(2,1)S(1)} async-done(((bf16[32,32,512]{2,1,0:T(8,128)(2,1)}), bf16[32,32,512]{2,1,0:T(8,128)(2,1)S(1)}, u32[]{:S(2)}, u32[]{:S(2)}) %all-to-all-start.1) | async-done | bytes 1048608 | tf_op jit(solution)/shard_map/all_to_all | solution.py:350
  83.1 3.0 %give_back.2.after_ref.refs_0_ = bf16[2048,512]{1,0:T(8,128)(2,1)} custom-call(s32[1,1024]{1,0:T(1,128)S(1)} %broadcast_select_fusion.index_ref, f32[1024,512]{1,0:T(8,128)} %spread.3.owned_hbm.after_ref, bf16[1024,512]{1,0:T(8,128)(2,1)S(1)} %bitcast.7), custom_call_target="tpu_custom_call" | custom-call | tf_op jit(solution)/shard_map/give_back/pallas_call | solution.py:332
  86.2 1.5 %collective-permute-start.6 = (bf16[64,512]{1,0:T(8,128)(2,1)S(1)}, bf16[64,512]{1,0:T(8,128)(2,1)S(1)}, u32[]{:S(2)}, u32[]{:S(2)}) collective-permute-start(bf16[64,512]{1,0:T(8,128)(2,1)S(1)} %add.5.refs_1_.refs_0_), channel_id=1, source_target_pairs={{0,2},{1,3},{2,0},{3,1},{4,6},{5,7},{6,4},{7,5},{8,10},{9,11},{10,... | collective-permute-start | bytes 196616 | tf_op jit(solution)/shard_map/ppermute | solution.py:432
  87.7 1.5 %collective-permute-start.7 = (bf16[64,512]{1,0:T(8,128)(2,1)S(1)}, bf16[64,512]{1,0:T(8,128)(2,1)S(1)}, u32[]{:S(2)}, u32[]{:S(2)}) collective-permute-start(bf16[64,512]{1,0:T(8,128)(2,1)S(1)} %add.5.refs_1_.refs_0_), channel_id=1, source_target_pairs={{0,4},{1,5},{2,6},{3,7},{4,0},{5,1},{6,2},{7,3},{8,12},{9,13},{10,... | collective-permute-start | bytes 196616 | tf_op jit(solution)/shard_map/ppermute | solution.py:432
  89.2 0.5 collective-permute-start.8
  89.7 3.0 %give_back.3.after_ref = bf16[2048,512]{1,0:T(8,128)(2,1)} custom-call(s32[1,1024]{1,0:T(1,128)S(1)} %broadcast_select_fusion.index_ref, f32[1024,512]{1,0:T(8,128)} %spread.2.after_ref.owned_hbm, bf16[1024,512]{1,0:T(8,128)(2,1)S(1)} %bitcast.8, bf16[2048,512]{1,0:T(8,128)(2,1)} %give_back.2.after_ref.refs_0_, ...), custom_call_target="tpu_custom_call", output_to_operand_aliasing={{}: (3, {})} | custom-call | tf_op jit(solution)/shard_map/give_back/pallas_call | solution.py:332
  92.7 1.6 %collective-permute-done.8.refs_3_ = bf16[64,512]{1,0:T(8,128)(2,1)S(1)} collective-permute-done((bf16[64,512]{1,0:T(8,128)(2,1)S(1)}, bf16[64,512]{1,0:T(8,128)(2,1)S(1)}, u32[]{:S(2)}, u32[]{:S(2)}) %collective-permute-start.8) | collective-permute-done | bytes 65568 | tf_op jit(solution)/shard_map/ppermute | solution.py:432
  94.4 0.1 collective-permute-start.9
  94.5 0.8 place.2.refs_0_
  95.3 0.7 collective-permute-done.9.half_ref
  96.0 0.8 place.3
  (21 shorter events, 0.2 us)
Async XLA Ops:
  0.6 12.5 %copy-start = (bf16[2048,512]{1,0:T(8,128)(2,1)S(1)}, bf16[2048,512]{1,0:T(8,128)(2,1)}, u32[]{:S(2)}) copy-start(bf16[2048,512]{1,0:T(8,128)(2,1)} %x_ref.3) | copy-start | bytes 6291460
  0.6 12.5 %copy-start.1 = (s32[256]{0:T(256)S(1)}, s32[256]{0:T(256)}, u32[]{:S(2)}) copy-start(s32[256]{0:T(256)} %rows_ref.1) | copy-start | bytes 3076
  0.7 12.5 %copy-start.2 = (s32[256]{0:T(256)S(1)}, s32[256]{0:T(256)}, u32[]{:S(2)}) copy-start(s32[256]{0:T(256)} %cols_ref.1) | copy-start | bytes 3076
  5.8 33.5 %all-to-all-start = ((bf16[32,32,512]{2,1,0:T(8,128)(2,1)}), bf16[32,32,512]{2,1,0:T(8,128)(2,1)S(1)}, u32[]{:S(2)}, u32[]{:S(2)}) async-start(bf16[32,32,512]{2,1,0:T(8,128)(2,1)} %bitcast.10), calls=%async_computation | async-start | bytes 2097152 | tf_op jit(solution)/shard_map/all_to_all | solution.py:350
  51.4 31.7 %all-to-all-start.1 = ((bf16[32,32,512]{2,1,0:T(8,128)(2,1)}), bf16[32,32,512]{2,1,0:T(8,128)(2,1)S(1)}, u32[]{:S(2)}, u32[]{:S(2)}) async-start(bf16[32,32,512]{2,1,0:T(8,128)(2,1)} %bitcast.11), calls=%async_computation.1 | async-start | bytes 2097152 | tf_op jit(solution)/shard_map/all_to_all | solution.py:350
  55.2 3.1 %copy-start.3 = (s32[1,32,32]{2,1,0:T(8,128)S(1)}, s32[1,32,32]{2,1,0:T(8,128)}, u32[]{:S(2)}) copy-start(s32[1,32,32]{2,1,0:T(8,128)} %param.14) | copy-start | bytes 12292
  55.2 3.1 %copy-start.4 = (s32[1,32]{1,0:T(1,128)S(1)}, s32[1,32]{1,0:T(1,128)}, u32[]{:S(2)}) copy-start(s32[1,32]{1,0:T(1,128)} %counts_ref.1) | copy-start | bytes 388
  58.1 1.6 %collective-permute-start = (bf16[256,512]{1,0:T(8,128)(2,1)S(1)}, bf16[256,512]{1,0:T(8,128)(2,1)S(1)}, u32[]{:S(2)}, u32[]{:S(2)}) collective-permute-start(bf16[256,512]{1,0:T(8,128)(2,1)S(1)} %get-tuple-element.26), channel_id=1, source_target_pairs={{0,1},{1,0},{2,3},{3,2},{4,5},{5,4},{6,7},{7,6},{8,9},{9,8},{10,11... | collective-permute-start | bytes 786440 | tf_op jit(solution)/shard_map/ppermute | solution.py:432
  59.8 9.4 %collective-permute-start.1 = (bf16[64,512]{1,0:T(8,128)(2,1)S(1)}, bf16[64,512]{1,0:T(8,128)(2,1)S(1)}, u32[]{:S(2)}, u32[]{:S(2)}) collective-permute-start(bf16[64,512]{1,0:T(8,128)(2,1)S(1)} %get-tuple-element.28), channel_id=1, source_target_pairs={{0,2},{1,3},{2,0},{3,1},{4,6},{5,7},{6,4},{7,5},{8,10},{9,11},{10,... | collective-permute-start | bytes 196616 | tf_op jit(solution)/shard_map/ppermute | solution.py:432
  61.4 7.7 %collective-permute-start.2 = (bf16[64,512]{1,0:T(8,128)(2,1)S(1)}, bf16[64,512]{1,0:T(8,128)(2,1)S(1)}, u32[]{:S(2)}, u32[]{:S(2)}) collective-permute-start(bf16[64,512]{1,0:T(8,128)(2,1)S(1)} %get-tuple-element.29), channel_id=1, source_target_pairs={{0,4},{1,5},{2,6},{3,7},{4,0},{5,1},{6,2},{7,3},{8,12},{9,13},{10,... | collective-permute-start | bytes 196616 | tf_op jit(solution)/shard_map/ppermute | solution.py:432
  62.9 7.1 %collective-permute-start.3 = (bf16[64,512]{1,0:T(8,128)(2,1)S(1)}, bf16[64,512]{1,0:T(8,128)(2,1)S(1)}, u32[]{:S(2)}, u32[]{:S(2)}) collective-permute-start(bf16[64,512]{1,0:T(8,128)(2,1)S(1)} %get-tuple-element.30), channel_id=1, source_target_pairs={{0,6},{1,7},{2,4},{3,5},{4,2},{5,3},{6,0},{7,1},{8,14},{9,15},{10,... | collective-permute-start | bytes 196616 | tf_op jit(solution)/shard_map/ppermute | solution.py:432
  70.1 6.9 %collective-permute-start.4 = (bf16[64,512]{1,0:T(8,128)(2,1)S(1)}, bf16[64,512]{1,0:T(8,128)(2,1)S(1)}, u32[]{:S(2)}, u32[]{:S(2)}) collective-permute-start(bf16[64,512]{1,0:T(8,128)(2,1)S(1)} %add.3.refs_0_), channel_id=1, source_target_pairs={{0,8},{8,0},{16,24},{24,16},{1,9},{9,1},{17,25},{25,17},{2,10},{10... | collective-permute-start | bytes 196616 | tf_op jit(solution)/shard_map/ppermute | solution.py:432
  77.0 9.1 %collective-permute-start.5 = (bf16[64,512]{1,0:T(8,128)(2,1)S(1)}, bf16[64,512]{1,0:T(8,128)(2,1)S(1)}, u32[]{:S(2)}, u32[]{:S(2)}) collective-permute-start(bf16[64,512]{1,0:T(8,128)(2,1)S(1)} %add.4.refs_0_), channel_id=1, source_target_pairs={{0,16},{8,24},{16,0},{24,8},{1,17},{9,25},{17,1},{25,9},{2,18},{10... | collective-permute-start | bytes 196616 | tf_op jit(solution)/shard_map/ppermute | solution.py:432
  86.2 6.5 %collective-permute-start.6 = (bf16[64,512]{1,0:T(8,128)(2,1)S(1)}, bf16[64,512]{1,0:T(8,128)(2,1)S(1)}, u32[]{:S(2)}, u32[]{:S(2)}) collective-permute-start(bf16[64,512]{1,0:T(8,128)(2,1)S(1)} %add.5.refs_1_.refs_0_), channel_id=1, source_target_pairs={{0,2},{1,3},{2,0},{3,1},{4,6},{5,7},{6,4},{7,5},{8,10},{9,11},{10,... | collective-permute-start | bytes 196616 | tf_op jit(solution)/shard_map/ppermute | solution.py:432
  87.7 5.0 %collective-permute-start.7 = (bf16[64,512]{1,0:T(8,128)(2,1)S(1)}, bf16[64,512]{1,0:T(8,128)(2,1)S(1)}, u32[]{:S(2)}, u32[]{:S(2)}) collective-permute-start(bf16[64,512]{1,0:T(8,128)(2,1)S(1)} %add.5.refs_1_.refs_0_), channel_id=1, source_target_pairs={{0,4},{1,5},{2,6},{3,7},{4,0},{5,1},{6,2},{7,3},{8,12},{9,13},{10,... | collective-permute-start | bytes 196616 | tf_op jit(solution)/shard_map/ppermute | solution.py:432
  89.2 5.2 %collective-permute-start.8 = (bf16[64,512]{1,0:T(8,128)(2,1)S(1)}, bf16[64,512]{1,0:T(8,128)(2,1)S(1)}, u32[]{:S(2)}, u32[]{:S(2)}) collective-permute-start(bf16[64,512]{1,0:T(8,128)(2,1)S(1)} %add.5.refs_1_.refs_0_), channel_id=1, source_target_pairs={{0,6},{1,7},{2,4},{3,5},{4,2},{5,3},{6,0},{7,1},{8,14},{9,15},{10,... | collective-permute-start | bytes 196616 | tf_op jit(solution)/shard_map/ppermute | solution.py:432
  94.4 1.6 %collective-permute-start.9 = (bf16[256,512]{1,0:T(8,128)(2,1)S(1)}, bf16[256,512]{1,0:T(8,128)(2,1)S(1)}, u32[]{:S(2)}, u32[]{:S(2)}) collective-permute-start(bf16[256,512]{1,0:T(8,128)(2,1)S(1)} %relay.1.half_ref), channel_id=1, source_target_pairs={{0,1},{1,0},{2,3},{3,2},{4,5},{5,4},{6,7},{7,6},{8,9},{9,8},{10,11... | collective-permute-start | bytes 786440 | tf_op jit(solution)/shard_map/ppermute | solution.py:432

commit v8 on v6

--- a/solution.py
+++ b/solution.py
@@ -50,25 +50,17 @@
     return pl.BlockSpec(shape, lambda i, *unused: (0,) * len(shape))
 
 
-def digits(index):
-    return (index >> 7).astype(F32).astype(BF16), (index & 127).astype(F32).astype(BF16)
-
-
 def collect_kernel(counts_ref, lists_ref, x_ref, out_ref):
     dests, slots = lists_ref.shape
     step = BIG // slots
-    lane = lax.broadcasted_iota(jnp.int32, (slots, 128), 1).astype(F32).astype(BF16)
+    lane = lax.broadcasted_iota(jnp.int32, (slots, x_ref.shape[0]), 1)
     slot = lax.broadcasted_iota(jnp.int32, (slots, 1), 0)
-    one, zero = jnp.ones((slots, 128), BF16), jnp.zeros((slots, 128), BF16)
     turned = lists_ref[...].T
     for first in range(0, dests, step):
         parts = []
         for d in range(first, first + step):
             named = jnp.where(slot < counts_ref[0, d], turned[:, d : d + 1], -1)
-            high, low = digits(jnp.broadcast_to(named, (slots, 128)))
-            hit = jnp.where(low == lane, one, zero)
-            tiles = [jnp.where(high == t, hit, zero) for t in range(x_ref.shape[0] // 128)]
-            parts.append(jnp.concatenate(tiles, axis=1))
+            parts.append(jnp.where(named == lane, 1.0, 0.0).astype(BF16))
         pick = jnp.concatenate(parts, axis=0)
         out_ref[first * slots : (first + step) * slots, :] = dot(pick, x_ref[...]).astype(BF16)
 
@@ -84,7 +76,7 @@
     )(counts, lists, x)
 
 
-def build_kernel(rows_ref, cols_ref, tiles_ref, x_ref, adj_ref, far_ref, own_ref, total, order, starts, cursor):
+def build_kernel(rows_ref, cols_ref, tiles_ref, x_ref, adj_ref, far_ref, own_ref, head_ref, total, order, starts, cursor):
     num_tiles, edge = tiles_ref.shape[0], tiles_ref.shape[1]
     per = ROWS // edge
     blocks = pl.num_programs(0)
@@ -137,6 +129,10 @@
     adj_ref[...] = total[:, :owned].astype(BF16)
     own_ref[...] = dot(adj_ref[...], x_ref[...])
     far_ref[...] = total[:, owned:].astype(BF16)
+
+    @pl.when(i < head_ref.shape[0] // ROWS)
+    def _():
+        head_ref[pl.ds(pl.multiple_of(i * ROWS, ROWS), ROWS), :] = far_ref[...]
 
 
 def build(tile_rows, tile_cols, tile_vals, x, remote):
@@ -153,6 +149,7 @@
                 pl.BlockSpec((ROWS, owned), lambda i, *unused: (i, 0)),
                 pl.BlockSpec((ROWS, remote), lambda i, *unused: (i, 0)),
                 pl.BlockSpec((ROWS, width), lambda i, *unused: (i, 0)),
+                whole((BIG, remote)),
             ],
             scratch_shapes=[
                 pltpu.VMEM((ROWS, owned + remote), F32),
@@ -165,6 +162,7 @@
             far_made((owned, owned), BF16),
             far_made((owned, remote), BF16),
             far_made((owned, width), F32),
+            far_made((BIG, remote), BF16),
         ],
         compiler_params=params(48),
         cost_estimate=pl.CostEstimate(
@@ -175,7 +173,7 @@
 
 
 def layer_kernel(
-    far_hbm, own_hbm, cot_hbm, w_hbm, got_ref,
+    far_hbm, own_hbm, cot_hbm, w_hbm, head_ref, got_ref,
     act_hbm, hid_hbm, slope_hbm, grad_hbm, back_hbm,
     far, own, cot, act, hid, slope, grad, w, back, sems, sent, w_sem,
 ):
@@ -200,15 +198,20 @@
     weight.start()
     for n, at in enumerate(views):
         copies = coming
-        for copy in copies[:2]:
-            copy.wait()
+        if n == 0:
+            summed = dot(head_ref[...], got_ref[...])
+        else:
+            copies[0].wait()
+            summed = dot(far[at, :], got_ref[...])
+        copies[1].wait()
         if n + 1 < blocks:
             coming = fetch(n + 1)
-        hid[at, :] = (own[at, :] + dot(far[at, :], got_ref[...])).astype(BF16)
+        hid[at, :] = (own[at, :] + summed).astype(BF16)
         send(0, n, hid, hid_hbm, at)
         copies[2].wait()
         if n == 0:
             weight.wait()
+            copies[0].wait()
         preact = dot(hid[at, :], w[...])
         gate = 0.5 + 0.5 * jnp.tanh(0.5 * preact)
         act[at, :] = (preact * gate).astype(BF16)
@@ -225,15 +228,15 @@
         copy.wait()
 
 
-def layer(keep, far, own, got, cotangent, weight):
+def layer(keep, far, own, head, got, cotangent, weight):
     owned, width = own.shape
     remote = got.shape[0]
     blocks = owned // BIG
-    (got,) = held(keep, got)
+    head, got = held(keep, head, got)
     rows = (owned, width)
     return pl.pallas_call(
         layer_kernel,
-        in_specs=[HBM] * 4 + [VMEM],
+        in_specs=[HBM] * 4 + [VMEM] * 2,
         out_specs=[HBM] * 5,
         out_shape=[far_made(rows, BF16)] * 4 + [far_made(got.shape, BF16)],
         scratch_shapes=[pltpu.VMEM(far.shape, BF16), pltpu.VMEM(rows, F32)]
@@ -247,7 +250,7 @@
         ],
         compiler_params=params(40 if keep else 60),
         name="layer",
-    )(*stored(far, own, cotangent, weight), got)
+    )(*stored(far, own, cotangent, weight), head, got)
 
 
 def partial_kernel(me_ref, hid_hbm, slope_hbm, mine_ref, other_ref, hid, slope, total, sems):
@@ -318,22 +321,19 @@
     for n, at in enumerate(views):
         half_hbm = (first_hbm, second_hbm)[2 * n // blocks]
         coming.append(pltpu.make_async_copy(half_hbm.at[views[n % (blocks // 2)]], owned.at[at], sems.at[n]))
-    for copy in coming:
-        copy.start()
-
-    shape = (128, index_ref.shape[1])
-    high, low = digits(jnp.broadcast_to(index_ref[...], shape))
-    row = lax.broadcasted_iota(jnp.int32, shape, 0).astype(F32).astype(BF16)
-    hit = jnp.where(low == row, jnp.ones(shape, BF16), jnp.zeros(shape, BF16))
+    coming[0].start()
+    coming[1].start()
 
     def pick(n):
-        tiles = [jnp.where(high == n * (BIG // 128) + t, hit, jnp.zeros(shape, BF16)) for t in range(BIG // 128)]
-        return jnp.concatenate(tiles, axis=0)
+        row = lax.broadcasted_iota(jnp.int32, (BIG, index_ref.shape[1]), 0) + n * BIG
+        return jnp.where(row == index_ref[...], 1.0, 0.0).astype(BF16)
 
     sending = []
     for n, at in enumerate(views):
         added = dot(pick(n), got_ref[...])
         coming[n].wait()
+        if n + 2 < blocks:
+            coming[n + 2].start()
         out[at, :] = (owned[at, :] + added).astype(BF16)
         sending.append(pltpu.make_async_copy(out.at[at], out_hbm.at[at], sent.at[n]))
         sending[n].start()
@@ -455,8 +455,8 @@
     me = lax.axis_index("local").astype(jnp.int32).reshape(1)
     outgoing = collect(counts, lists, features)
     arrived = exchange(outgoing.reshape(peers, slots, width), AXES).reshape(remote, width)
-    adjacency, far, own = build(tile_rows, tile_cols, tile_vals, features, remote)
-    activated, hidden, slope, grad, back = layer(keep, far, own, arrived, cotangent, weight)
+    adjacency, far, own, head = build(tile_rows, tile_cols, tile_vals, features, remote)
+    activated, hidden, slope, grad, back = layer(keep, far, own, head, arrived, cotangent, weight)
     returned = exchange(back.reshape(peers, slots, width), AXES).reshape(remote, width)
     first = spread(adjacency, grad, 0, 2)
     second = spread(adjacency, grad, 1, 2)

time: 95.7 us -> 97.4 us (1.018)
  local copies, waits for them, and re-layouts: 0.19 us -> 1.41 us
    unnamed x10 -> x12, local copies, waits for them, and re-layouts: 0.02 us -> 1.24 us
  transfers between devices with their start and end apart: 12 -> 12, of which waited for: 5 -> 6; matrix products, arithmetic and copies ran while one was open for 0% -> 0% of each run, Pallas kernels for 42% -> 41%
where the time goes in v8:
time: 97.4 us; the launch traced here: 96.9 us
  Pallas kernels  58.9 us (60%)
  starting transfers between devices  22.6 us (23%)
  waiting for transfers between devices  12.9 us (13%)
  local copies, waits for them, and re-layouts  1.41 us (1%)
    pallas_call x1, Pallas kernels, build(): pl.pallas_call(build_kernel, grid_spec=pltpu.PrefetchScalarGridSpec(num_s...  20.2 us
    pallas_call x1, Pallas kernels, layer(): pl.pallas_call(layer_kernel, in_specs=[HBM] * 4 + [VMEM] * 2, out_specs=[...  12.8 us
    pallas_call x2, Pallas kernels, spread(): pl.pallas_call(spread_kernel, grid=(blocks,), in_specs=[pl.BlockSpec((own...  11.6 us
    ppermute x10, starting transfers between devices, swap(): return lax.ppermute(x, axis, [(i, i ^ k) for i in range(size)])  11.5 us
    all_to_all x2, starting transfers between devices, exchange(): return lax.all_to_all(x, axes, split_axis=0, concat_axis=0, tiled=True)  11.1 us
    ppermute x10, waiting for transfers between devices, swap(): return lax.ppermute(x, axis, [(i, i ^ k) for i in range(size)])  6.9 us
    all_to_all x2, waiting for transfers between devices, exchange(): return lax.all_to_all(x, axes, split_axis=0, concat_axis=0, tiled=True)  6 us
    pallas_call x1, Pallas kernels, collect(): pl.pallas_call(collect_kernel, in_specs=[SMEM, VMEM, VMEM], out_shape=jax...  5.17 us
  transfers between devices with their start and end apart: 12, of which 6 were waited for; matrix products, arithmetic and copies ran while one was open for 0% of the time, Pallas kernels for 41%

profile of v8, /device:TPU:0, one launch (start us, length us, event | category | flops | bytes accessed | tf_op | source)
XLA Modules:
  0.0 96.9 jit_solution(15349500980435935552)
XLA Ops:
  0.7 5.2 %collect.1 = bf16[1024,512]{1,0:T(8,128)(2,1)} custom-call(s32[1,32]{1,0:T(1,128)} %counts_ref.1, s32[32,32]{1,0:T(8,128)} %bitcast.11, bf16[2048,512]{1,0:T(8,128)(2,1)} %x_ref.3), custom_call_target="tpu_custom_call" | custom-call | tf_op jit(solution)/shard_map/collect/pallas_call | solution.py:70
  5.8 7.3 %all-to-all-start = ((bf16[32,32,512]{2,1,0:T(8,128)(2,1)}), bf16[32,32,512]{2,1,0:T(8,128)(2,1)S(1)}, u32[]{:S(2)}, u32[]{:S(2)}) async-start(bf16[32,32,512]{2,1,0:T(8,128)(2,1)} %bitcast.9), calls=%async_computation | async-start | bytes 2097152 | tf_op jit(solution)/shard_map/all_to_all | solution.py:364
  13.2 20.2 %build.1 = (bf16[2048,2048]{1,0:T(8,128)(2,1)}, bf16[2048,1024]{1,0:T(8,128)(2,1)}, f32[2048,512]{1,0:T(8,128)}, bf16[512,1024]{1,0:T(8,128)(2,1)}) custom-call(s32[256]{0:T(256)S(1)} %copy-done.2, s32[256]{0:T(256)S(1)} %copy-done.3, bf16[256,128,128]{2,1,0:T(8,128)(2,1)} %tiles_ref.1, bf16[2048,512]{1,0:T(8,128)(2,1)S(1)} %copy-done), custom_call_target="tpu_custom_call" | custom-call | flops 4294967296 | bytes 41943040 | tf_op jit(solution)/shard_map/build/pallas_call | solution.py:142
  33.4 6.0 %all-to-all-done = bf16[32,32,512]{2,1,0:T(8,128)(2,1)S(1)} async-done(((bf16[32,32,512]{2,1,0:T(8,128)(2,1)}), bf16[32,32,512]{2,1,0:T(8,128)(2,1)S(1)}, u32[]{:S(2)}, u32[]{:S(2)}) %all-to-all-start) | async-done | bytes 1048608 | tf_op jit(solution)/shard_map/all_to_all | solution.py:364
  39.4 1.2 %copy-done.1 = bf16[512,1024]{1,0:T(8,128)(2,1)S(1)} copy-done((bf16[512,1024]{1,0:T(8,128)(2,1)S(1)}, bf16[512,1024]{1,0:T(8,128)(2,1)}, u32[]{:S(2)}) %copy-start.1) | copy-done | bytes 1048600
  40.6 12.8 %layer.1 = (bf16[2048,512]{1,0:T(8,128)(2,1)}, bf16[2048,512]{1,0:T(8,128)(2,1)}, bf16[2048,512]{1,0:T(8,128)(2,1)}, bf16[2048,512]{1,0:T(8,128)(2,1)}, bf16[1024,512]{1,0:T(8,128)(2,1)}) custom-call(bf16[2048,1024]{1,0:T(8,128)(2,1)} %get-tuple-element.18.far_hbm, f32[2048,512]{1,0:T(8,128)} %get-tuple-element.19.own_hbm, bf16[2048,512]{1,0:T(8,128)(2,1)} %cot_hbm.1, ...), custom_call_target="tpu_custom_call" | custom-call | tf_op jit(solution)/shard_map/layer/pallas_call | solution.py:237
  53.4 3.8 %all-to-all-start.1 = ((bf16[32,32,512]{2,1,0:T(8,128)(2,1)}), bf16[32,32,512]{2,1,0:T(8,128)(2,1)S(1)}, u32[]{:S(2)}, u32[]{:S(2)}) async-start(bf16[32,32,512]{2,1,0:T(8,128)(2,1)} %bitcast.10), calls=%async_computation.1 | async-start | bytes 2097152 | tf_op jit(solution)/shard_map/all_to_all | solution.py:364
  57.2 2.9 %partial_grad.1 = (f32[256,512]{1,0:T(8,128)S(1)}, bf16[256,512]{1,0:T(8,128)(2,1)S(1)}) custom-call(s32[1]{0:T(128)} %bitcast.6.me_ref, bf16[2048,512]{1,0:T(8,128)(2,1)} %get-tuple-element.25.hid_hbm, bf16[2048,512]{1,0:T(8,128)(2,1)} %get-tuple-element.26.slope_hbm), custom_call_target="tpu_custom_call" | custom-call | tf_op jit(solution)/shard_map/partial_grad/pallas_call | solution.py:280
  60.1 0.1 collective-permute-start
  60.2 1.5 %collective-permute-done.got_ref = bf16[256,512]{1,0:T(8,128)(2,1)S(1)} collective-permute-done((bf16[256,512]{1,0:T(8,128)(2,1)S(1)}, bf16[256,512]{1,0:T(8,128)(2,1)S(1)}, u32[]{:S(2)}, u32[]{:S(2)}) %collective-permute-start) | collective-permute-done | bytes 262176 | tf_op jit(solution)/shard_map/ppermute | solution.py:446
  61.7 1.7 %collective-permute-start.1 = (bf16[64,512]{1,0:T(8,128)(2,1)S(1)}, bf16[64,512]{1,0:T(8,128)(2,1)S(1)}, u32[]{:S(2)}, u32[]{:S(2)}) collective-permute-start(bf16[64,512]{1,0:T(8,128)(2,1)S(1)} %get-tuple-element.30), channel_id=1, source_target_pairs={{0,2},{1,3},{2,0},{3,1},{4,6},{5,7},{6,4},{7,5},{8,10},{9,11},{10,... | collective-permute-start | bytes 196616 | tf_op jit(solution)/shard_map/ppermute | solution.py:446
  63.4 1.5 %collective-permute-start.2 = (bf16[64,512]{1,0:T(8,128)(2,1)S(1)}, bf16[64,512]{1,0:T(8,128)(2,1)S(1)}, u32[]{:S(2)}, u32[]{:S(2)}) collective-permute-start(bf16[64,512]{1,0:T(8,128)(2,1)S(1)} %get-tuple-element.31), channel_id=1, source_target_pairs={{0,4},{1,5},{2,6},{3,7},{4,0},{5,1},{6,2},{7,3},{8,12},{9,13},{10,... | collective-permute-start | bytes 196616 | tf_op jit(solution)/shard_map/ppermute | solution.py:446
  64.9 0.4 collective-permute-start.3
  65.3 5.8 %spread.2.first_hbm.after_ref = f32[1024,512]{1,0:T(8,128)} custom-call(bf16[2048,2048]{1,0:T(8,128)(2,1)} %get-tuple-element.22.adj_ref, bf16[2048,512]{1,0:T(8,128)(2,1)} %get-tuple-element.23.grad_ref), custom_call_target="tpu_custom_call" | custom-call | flops 4294967296 | bytes 16777216 | tf_op jit(solution)/shard_map/spread/pallas_call | solution.py:303
  71.1 0.0 collective-permute-done.1.refs_1_
  71.1 0.9 collective-permute-done.3.refs_3_
  72.1 1.1 %collective-permute-start.4 = (bf16[64,512]{1,0:T(8,128)(2,1)S(1)}, bf16[64,512]{1,0:T(8,128)(2,1)S(1)}, u32[]{:S(2)}, u32[]{:S(2)}) collective-permute-start(bf16[64,512]{1,0:T(8,128)(2,1)S(1)} %add.3.refs_0_), channel_id=1, source_target_pairs={{0,8},{8,0},{16,24},{24,16},{1,9},{9,1},{17,25},{25,17},{2,10},{10... | collective-permute-start | bytes 196616 | tf_op jit(solution)/shard_map/ppermute | solution.py:446
  73.1 5.8 %spread.3.second_hbm.after_ref = f32[1024,512]{1,0:T(8,128)} custom-call(bf16[2048,2048]{1,0:T(8,128)(2,1)} %get-tuple-element.22.adj_ref, bf16[2048,512]{1,0:T(8,128)(2,1)} %get-tuple-element.23.grad_ref), custom_call_target="tpu_custom_call" | custom-call | flops 4294967296 | bytes 16777216 | tf_op jit(solution)/shard_map/spread/pallas_call | solution.py:303
  79.0 3.1 %collective-permute-start.5 = (bf16[64,512]{1,0:T(8,128)(2,1)S(1)}, bf16[64,512]{1,0:T(8,128)(2,1)S(1)}, u32[]{:S(2)}, u32[]{:S(2)}) collective-permute-start(bf16[64,512]{1,0:T(8,128)(2,1)S(1)} %add.4.refs_0_), channel_id=1, source_target_pairs={{0,16},{8,24},{16,0},{24,8},{1,17},{9,25},{17,1},{25,9},{2,18},{10... | collective-permute-start | bytes 196616 | tf_op jit(solution)/shard_map/ppermute | solution.py:446
  82.0 0.1 iota_compare_fusion
  82.1 0.1 squeeze.6
  82.2 0.1 lt.29
  82.3 3.8 %collective-permute-done.5.refs_1_ = bf16[64,512]{1,0:T(8,128)(2,1)S(1)} collective-permute-done((bf16[64,512]{1,0:T(8,128)(2,1)S(1)}, bf16[64,512]{1,0:T(8,128)(2,1)S(1)}, u32[]{:S(2)}, u32[]{:S(2)}) %collective-permute-start.5) | collective-permute-done | bytes 65568 | tf_op jit(solution)/shard_map/ppermute | solution.py:446
  86.1 1.5 %collective-permute-start.6 = (bf16[64,512]{1,0:T(8,128)(2,1)S(1)}, bf16[64,512]{1,0:T(8,128)(2,1)S(1)}, u32[]{:S(2)}, u32[]{:S(2)}) collective-permute-start(bf16[64,512]{1,0:T(8,128)(2,1)S(1)} %add.5.refs_0_), channel_id=1, source_target_pairs={{0,2},{1,3},{2,0},{3,1},{4,6},{5,7},{6,4},{7,5},{8,10},{9,11},{10,... | collective-permute-start | bytes 196616 | tf_op jit(solution)/shard_map/ppermute | solution.py:446
  87.6 1.5 %collective-permute-start.7 = (bf16[64,512]{1,0:T(8,128)(2,1)S(1)}, bf16[64,512]{1,0:T(8,128)(2,1)S(1)}, u32[]{:S(2)}, u32[]{:S(2)}) collective-permute-start(bf16[64,512]{1,0:T(8,128)(2,1)S(1)} %add.5.refs_0_), channel_id=1, source_target_pairs={{0,4},{1,5},{2,6},{3,7},{4,0},{5,1},{6,2},{7,3},{8,12},{9,13},{10,... | collective-permute-start | bytes 196616 | tf_op jit(solution)/shard_map/ppermute | solution.py:446
  89.1 0.5 collective-permute-start.8
  89.6 4.5 %give_back.1.after_ref = bf16[2048,512]{1,0:T(8,128)(2,1)} custom-call(s32[1,1024]{1,0:T(1,128)S(1)} %broadcast_select_fusion.index_ref, f32[1024,512]{1,0:T(8,128)} %spread.2.first_hbm.after_ref, f32[1024,512]{1,0:T(8,128)} %spread.3.second_hbm.after_ref, bf16[1024,512]{1,0:T(8,128)(2,1)S(1)} %bitcast.7), custom_call_target="tpu_custom_call" | custom-call | tf_op jit(solution)/shard_map/give_back/pallas_call | solution.py:347
  94.2 0.1 collective-permute-done.8.refs_3_
  94.3 0.1 collective-permute-start.9
  94.4 0.8 place.2.refs_0_
  95.2 0.7 collective-permute-done.9.half_ref
  95.9 0.8 place.3
  (22 shorter events, 0.2 us)
Async XLA Ops:
  0.6 12.5 %copy-start = (bf16[2048,512]{1,0:T(8,128)(2,1)S(1)}, bf16[2048,512]{1,0:T(8,128)(2,1)}, u32[]{:S(2)}) copy-start(bf16[2048,512]{1,0:T(8,128)(2,1)} %x_ref.3) | copy-start | bytes 6291460
  0.6 12.5 %copy-start.2 = (s32[256]{0:T(256)S(1)}, s32[256]{0:T(256)}, u32[]{:S(2)}) copy-start(s32[256]{0:T(256)} %rows_ref.1) | copy-start | bytes 3076
  0.7 12.5 %copy-start.3 = (s32[256]{0:T(256)S(1)}, s32[256]{0:T(256)}, u32[]{:S(2)}) copy-start(s32[256]{0:T(256)} %cols_ref.1) | copy-start | bytes 3076
  5.8 33.5 %all-to-all-start = ((bf16[32,32,512]{2,1,0:T(8,128)(2,1)}), bf16[32,32,512]{2,1,0:T(8,128)(2,1)S(1)}, u32[]{:S(2)}, u32[]{:S(2)}) async-start(bf16[32,32,512]{2,1,0:T(8,128)(2,1)} %bitcast.9), calls=%async_computation | async-start | bytes 2097152 | tf_op jit(solution)/shard_map/all_to_all | solution.py:364
  39.4 1.2 %copy-start.1 = (bf16[512,1024]{1,0:T(8,128)(2,1)S(1)}, bf16[512,1024]{1,0:T(8,128)(2,1)}, u32[]{:S(2)}) copy-start(bf16[512,1024]{1,0:T(8,128)(2,1)} %get-tuple-element.20.head_ref) | copy-start | bytes 3145732
  53.4 36.3 %all-to-all-start.1 = ((bf16[32,32,512]{2,1,0:T(8,128)(2,1)}), bf16[32,32,512]{2,1,0:T(8,128)(2,1)S(1)}, u32[]{:S(2)}, u32[]{:S(2)}) async-start(bf16[32,32,512]{2,1,0:T(8,128)(2,1)} %bitcast.10), calls=%async_computation.1 | async-start | bytes 2097152 | tf_op jit(solution)/shard_map/all_to_all | solution.py:364
  60.1 1.6 %collective-permute-start = (bf16[256,512]{1,0:T(8,128)(2,1)S(1)}, bf16[256,512]{1,0:T(8,128)(2,1)S(1)}, u32[]{:S(2)}, u32[]{:S(2)}) collective-permute-start(bf16[256,512]{1,0:T(8,128)(2,1)S(1)} %get-tuple-element.28), channel_id=1, source_target_pairs={{0,1},{1,0},{2,3},{3,2},{4,5},{5,4},{6,7},{7,6},{8,9},{9,8},{10,11... | collective-permute-start | bytes 786440 | tf_op jit(solution)/shard_map/ppermute | solution.py:446
  61.7 9.3 %collective-permute-start.1 = (bf16[64,512]{1,0:T(8,128)(2,1)S(1)}, bf16[64,512]{1,0:T(8,128)(2,1)S(1)}, u32[]{:S(2)}, u32[]{:S(2)}) collective-permute-start(bf16[64,512]{1,0:T(8,128)(2,1)S(1)} %get-tuple-element.30), channel_id=1, source_target_pairs={{0,2},{1,3},{2,0},{3,1},{4,6},{5,7},{6,4},{7,5},{8,10},{9,11},{10,... | collective-permute-start | bytes 196616 | tf_op jit(solution)/shard_map/ppermute | solution.py:446
  63.4 7.7 %collective-permute-start.2 = (bf16[64,512]{1,0:T(8,128)(2,1)S(1)}, bf16[64,512]{1,0:T(8,128)(2,1)S(1)}, u32[]{:S(2)}, u32[]{:S(2)}) collective-permute-start(bf16[64,512]{1,0:T(8,128)(2,1)S(1)} %get-tuple-element.31), channel_id=1, source_target_pairs={{0,4},{1,5},{2,6},{3,7},{4,0},{5,1},{6,2},{7,3},{8,12},{9,13},{10,... | collective-permute-start | bytes 196616 | tf_op jit(solution)/shard_map/ppermute | solution.py:446
  64.9 7.2 %collective-permute-start.3 = (bf16[64,512]{1,0:T(8,128)(2,1)S(1)}, bf16[64,512]{1,0:T(8,128)(2,1)S(1)}, u32[]{:S(2)}, u32[]{:S(2)}) collective-permute-start(bf16[64,512]{1,0:T(8,128)(2,1)S(1)} %get-tuple-element.32), channel_id=1, source_target_pairs={{0,6},{1,7},{2,4},{3,5},{4,2},{5,3},{6,0},{7,1},{8,14},{9,15},{10,... | collective-permute-start | bytes 196616 | tf_op jit(solution)/shard_map/ppermute | solution.py:446
  72.1 6.9 %collective-permute-start.4 = (bf16[64,512]{1,0:T(8,128)(2,1)S(1)}, bf16[64,512]{1,0:T(8,128)(2,1)S(1)}, u32[]{:S(2)}, u32[]{:S(2)}) collective-permute-start(bf16[64,512]{1,0:T(8,128)(2,1)S(1)} %add.3.refs_0_), channel_id=1, source_target_pairs={{0,8},{8,0},{16,24},{24,16},{1,9},{9,1},{17,25},{25,17},{2,10},{10... | collective-permute-start | bytes 196616 | tf_op jit(solution)/shard_map/ppermute | solution.py:446
  78.9 3.1 %copy-start.5 = (s32[1,32]{1,0:T(1,128)S(1)}, s32[1,32]{1,0:T(1,128)}, u32[]{:S(2)}) copy-start(s32[1,32]{1,0:T(1,128)} %counts_ref.1) | copy-start | bytes 388
  78.9 3.2 %copy-start.4 = (s32[1,32,32]{2,1,0:T(8,128)S(1)}, s32[1,32,32]{2,1,0:T(8,128)}, u32[]{:S(2)}) copy-start(s32[1,32,32]{2,1,0:T(8,128)} %param.14) | copy-start | bytes 12292
  79.0 7.1 %collective-permute-start.5 = (bf16[64,512]{1,0:T(8,128)(2,1)S(1)}, bf16[64,512]{1,0:T(8,128)(2,1)S(1)}, u32[]{:S(2)}, u32[]{:S(2)}) collective-permute-start(bf16[64,512]{1,0:T(8,128)(2,1)S(1)} %add.4.refs_0_), channel_id=1, source_target_pairs={{0,16},{8,24},{16,0},{24,8},{1,17},{9,25},{17,1},{25,9},{2,18},{10... | collective-permute-start | bytes 196616 | tf_op jit(solution)/shard_map/ppermute | solution.py:446
  86.1 8.1 %collective-permute-start.6 = (bf16[64,512]{1,0:T(8,128)(2,1)S(1)}, bf16[64,512]{1,0:T(8,128)(2,1)S(1)}, u32[]{:S(2)}, u32[]{:S(2)}) collective-permute-start(bf16[64,512]{1,0:T(8,128)(2,1)S(1)} %add.5.refs_0_), channel_id=1, source_target_pairs={{0,2},{1,3},{2,0},{3,1},{4,6},{5,7},{6,4},{7,5},{8,10},{9,11},{10,... | collective-permute-start | bytes 196616 | tf_op jit(solution)/shard_map/ppermute | solution.py:446
  87.6 6.6 %collective-permute-start.7 = (bf16[64,512]{1,0:T(8,128)(2,1)S(1)}, bf16[64,512]{1,0:T(8,128)(2,1)S(1)}, u32[]{:S(2)}, u32[]{:S(2)}) collective-permute-start(bf16[64,512]{1,0:T(8,128)(2,1)S(1)} %add.5.refs_0_), channel_id=1, source_target_pairs={{0,4},{1,5},{2,6},{3,7},{4,0},{5,1},{6,2},{7,3},{8,12},{9,13},{10,... | collective-permute-start | bytes 196616 | tf_op jit(solution)/shard_map/ppermute | solution.py:446
  89.1 5.2 %collective-permute-start.8 = (bf16[64,512]{1,0:T(8,128)(2,1)S(1)}, bf16[64,512]{1,0:T(8,128)(2,1)S(1)}, u32[]{:S(2)}, u32[]{:S(2)}) collective-permute-start(bf16[64,512]{1,0:T(8,128)(2,1)S(1)} %add.5.refs_0_), channel_id=1, source_target_pairs={{0,6},{1,7},{2,4},{3,5},{4,2},{5,3},{6,0},{7,1},{8,14},{9,15},{10,... | collective-permute-start | bytes 196616 | tf_op jit(solution)/shard_map/ppermute | solution.py:446
  94.3 1.6 %collective-permute-start.9 = (bf16[256,512]{1,0:T(8,128)(2,1)S(1)}, bf16[256,512]{1,0:T(8,128)(2,1)S(1)}, u32[]{:S(2)}, u32[]{:S(2)}) collective-permute-start(bf16[256,512]{1,0:T(8,128)(2,1)S(1)} %relay.1.half_ref), channel_id=1, source_target_pairs={{0,1},{1,0},{2,3},{3,2},{4,5},{5,4},{6,7},{7,6},{8,9},{9,8},{10,11... | collective-permute-start | bytes 786440 | tf_op jit(solution)/shard_map/ppermute | solution.py:446

commit v9 on v6

--- a/solution.py
+++ b/solution.py
@@ -50,25 +50,17 @@
     return pl.BlockSpec(shape, lambda i, *unused: (0,) * len(shape))
 
 
-def digits(index):
-    return (index >> 7).astype(F32).astype(BF16), (index & 127).astype(F32).astype(BF16)
-
-
 def collect_kernel(counts_ref, lists_ref, x_ref, out_ref):
     dests, slots = lists_ref.shape
     step = BIG // slots
-    lane = lax.broadcasted_iota(jnp.int32, (slots, 128), 1).astype(F32).astype(BF16)
+    lane = lax.broadcasted_iota(jnp.int32, (slots, x_ref.shape[0]), 1)
     slot = lax.broadcasted_iota(jnp.int32, (slots, 1), 0)
-    one, zero = jnp.ones((slots, 128), BF16), jnp.zeros((slots, 128), BF16)
     turned = lists_ref[...].T
     for first in range(0, dests, step):
         parts = []
         for d in range(first, first + step):
             named = jnp.where(slot < counts_ref[0, d], turned[:, d : d + 1], -1)
-            high, low = digits(jnp.broadcast_to(named, (slots, 128)))
-            hit = jnp.where(low == lane, one, zero)
-            tiles = [jnp.where(high == t, hit, zero) for t in range(x_ref.shape[0] // 128)]
-            parts.append(jnp.concatenate(tiles, axis=1))
+            parts.append(jnp.where(named == lane, 1.0, 0.0).astype(BF16))
         pick = jnp.concatenate(parts, axis=0)
         out_ref[first * slots : (first + step) * slots, :] = dot(pick, x_ref[...]).astype(BF16)
 
@@ -195,15 +187,15 @@
         sending.append(pltpu.make_async_copy(a.at[at], b.at[at], sent.at[k, n]))
         sending[-1].start()
 
-    coming = fetch(0)
+    coming = [fetch(0)]
     weight = pltpu.make_async_copy(w_hbm, w, w_sem)
     weight.start()
     for n, at in enumerate(views):
-        copies = coming
+        copies = coming[n]
         for copy in copies[:2]:
             copy.wait()
-        if n + 1 < blocks:
-            coming = fetch(n + 1)
+        while len(coming) < min(n + 3, blocks):
+            coming.append(fetch(len(coming)))
         hid[at, :] = (own[at, :] + dot(far[at, :], got_ref[...])).astype(BF16)
         send(0, n, hid, hid_hbm, at)
         copies[2].wait()
@@ -321,14 +313,9 @@
     for copy in coming:
         copy.start()
 
-    shape = (128, index_ref.shape[1])
-    high, low = digits(jnp.broadcast_to(index_ref[...], shape))
-    row = lax.broadcasted_iota(jnp.int32, shape, 0).astype(F32).astype(BF16)
-    hit = jnp.where(low == row, jnp.ones(shape, BF16), jnp.zeros(shape, BF16))
-
     def pick(n):
-        tiles = [jnp.where(high == n * (BIG // 128) + t, hit, jnp.zeros(shape, BF16)) for t in range(BIG // 128)]
-        return jnp.concatenate(tiles, axis=0)
+        row = lax.broadcasted_iota(jnp.int32, (BIG, index_ref.shape[1]), 0) + n * BIG
+        return jnp.where(row == index_ref[...], 1.0, 0.0).astype(BF16)
 
     sending = []
     for n, at in enumerate(views):

time: 95.7 us -> 95 us (level)
  transfers between devices with their start and end apart: 12 -> 12, of which waited for: 5 -> 6; matrix products, arithmetic and copies ran while one was open for 0% -> 0% of each run, Pallas kernels for 42% -> 42%
where the time goes in v9:
time: 95 us; the launch traced here: 94.6 us
  Pallas kernels  57.2 us (60%)
  starting transfers between devices  22.6 us (24%)
  waiting for transfers between devices  13.6 us (14%)
  between operations  0.97 us (1%)
    pallas_call x1, Pallas kernels, build(): pl.pallas_call(build_kernel, grid_spec=pltpu.PrefetchScalarGridSpec(num_s...  19.5 us
    pallas_call x1, Pallas kernels, layer(): pl.pallas_call(layer_kernel, in_specs=[HBM] * 4 + [VMEM], out_specs=[HBM]...  11.7 us
    pallas_call x2, Pallas kernels, spread(): pl.pallas_call(spread_kernel, grid=(blocks,), in_specs=[pl.BlockSpec((own...  11.6 us
    ppermute x10, starting transfers between devices, swap(): return lax.ppermute(x, axis, [(i, i ^ k) for i in range(size)])  11.5 us
    all_to_all x2, starting transfers between devices, exchange(): return lax.all_to_all(x, axes, split_axis=0, concat_axis=0, tiled=True)  11.1 us
    ppermute x10, waiting for transfers between devices, swap(): return lax.ppermute(x, axis, [(i, i ^ k) for i in range(size)])  6.9 us
    all_to_all x2, waiting for transfers between devices, exchange(): return lax.all_to_all(x, axes, split_axis=0, concat_axis=0, tiled=True)  6.68 us
    pallas_call x1, Pallas kernels, collect(): pl.pallas_call(collect_kernel, in_specs=[SMEM, VMEM, VMEM], out_shape=jax...  5.17 us
  transfers between devices with their start and end apart: 12, of which 6 were waited for; matrix products, arithmetic and copies ran while one was open for 0% of the time, Pallas kernels for 42%

profile of v9, /device:TPU:0, one launch (start us, length us, event | category | flops | bytes accessed | tf_op | source)
XLA Modules:
  0.0 94.6 jit_solution(15627106509485087246)
XLA Ops:
  0.7 5.2 %collect.1 = bf16[1024,512]{1,0:T(8,128)(2,1)} custom-call(s32[1,32]{1,0:T(1,128)} %counts_ref.1, s32[32,32]{1,0:T(8,128)} %bitcast.11, bf16[2048,512]{1,0:T(8,128)(2,1)} %x_ref.3), custom_call_target="tpu_custom_call" | custom-call | tf_op jit(solution)/shard_map/collect/pallas_call | solution.py:70
  5.8 7.3 %all-to-all-start = ((bf16[32,32,512]{2,1,0:T(8,128)(2,1)}), bf16[32,32,512]{2,1,0:T(8,128)(2,1)S(1)}, u32[]{:S(2)}, u32[]{:S(2)}) async-start(bf16[32,32,512]{2,1,0:T(8,128)(2,1)} %bitcast.9), calls=%async_computation | async-start | bytes 2097152 | tf_op jit(solution)/shard_map/all_to_all | solution.py:351
  13.2 19.5 %build.1 = (bf16[2048,2048]{1,0:T(8,128)(2,1)}, bf16[2048,1024]{1,0:T(8,128)(2,1)}, f32[2048,512]{1,0:T(8,128)}) custom-call(s32[256]{0:T(256)S(1)} %copy-done.1, s32[256]{0:T(256)S(1)} %copy-done.2, bf16[256,128,128]{2,1,0:T(8,128)(2,1)} %tiles_ref.1, bf16[2048,512]{1,0:T(8,128)(2,1)S(1)} %copy-done), custom_call_target="tpu_custom_call" | custom-call | flops 4294967296 | bytes 41943040 | tf_op jit(solution)/shard_map/build/pallas_call | solution.py:138
  32.7 6.7 %all-to-all-done = bf16[32,32,512]{2,1,0:T(8,128)(2,1)S(1)} async-done(((bf16[32,32,512]{2,1,0:T(8,128)(2,1)}), bf16[32,32,512]{2,1,0:T(8,128)(2,1)S(1)}, u32[]{:S(2)}, u32[]{:S(2)}) %all-to-all-start) | async-done | bytes 1048608 | tf_op jit(solution)/shard_map/all_to_all | solution.py:351
  39.4 11.7 %layer.1 = (bf16[2048,512]{1,0:T(8,128)(2,1)}, bf16[2048,512]{1,0:T(8,128)(2,1)}, bf16[2048,512]{1,0:T(8,128)(2,1)}, bf16[2048,512]{1,0:T(8,128)(2,1)}, bf16[1024,512]{1,0:T(8,128)(2,1)}) custom-call(bf16[2048,1024]{1,0:T(8,128)(2,1)} %get-tuple-element.17.far_hbm, f32[2048,512]{1,0:T(8,128)} %get-tuple-element.18.own_hbm, bf16[2048,512]{1,0:T(8,128)(2,1)} %cot_hbm.1, ...), custom_call_target="tpu_custom_call" | custom-call | tf_op jit(solution)/shard_map/layer/pallas_call | solution.py:226
  51.1 3.8 %all-to-all-start.1 = ((bf16[32,32,512]{2,1,0:T(8,128)(2,1)}), bf16[32,32,512]{2,1,0:T(8,128)(2,1)S(1)}, u32[]{:S(2)}, u32[]{:S(2)}) async-start(bf16[32,32,512]{2,1,0:T(8,128)(2,1)} %bitcast.10), calls=%async_computation.1 | async-start | bytes 2097152 | tf_op jit(solution)/shard_map/all_to_all | solution.py:351
  54.9 2.9 %partial_grad.1 = (f32[256,512]{1,0:T(8,128)S(1)}, bf16[256,512]{1,0:T(8,128)(2,1)S(1)}) custom-call(s32[1]{0:T(128)} %bitcast.6.me_ref, bf16[2048,512]{1,0:T(8,128)(2,1)} %get-tuple-element.23.hid_hbm, bf16[2048,512]{1,0:T(8,128)(2,1)} %get-tuple-element.24.slope_hbm), custom_call_target="tpu_custom_call" | custom-call | tf_op jit(solution)/shard_map/partial_grad/pallas_call | solution.py:269
  57.8 0.1 collective-permute-start
  58.0 1.5 %collective-permute-done.got_ref = bf16[256,512]{1,0:T(8,128)(2,1)S(1)} collective-permute-done((bf16[256,512]{1,0:T(8,128)(2,1)S(1)}, bf16[256,512]{1,0:T(8,128)(2,1)S(1)}, u32[]{:S(2)}, u32[]{:S(2)}) %collective-permute-start) | collective-permute-done | bytes 262176 | tf_op jit(solution)/shard_map/ppermute | solution.py:433
  59.5 1.7 %collective-permute-start.1 = (bf16[64,512]{1,0:T(8,128)(2,1)S(1)}, bf16[64,512]{1,0:T(8,128)(2,1)S(1)}, u32[]{:S(2)}, u32[]{:S(2)}) collective-permute-start(bf16[64,512]{1,0:T(8,128)(2,1)S(1)} %get-tuple-element.28), channel_id=1, source_target_pairs={{0,2},{1,3},{2,0},{3,1},{4,6},{5,7},{6,4},{7,5},{8,10},{9,11},{10,... | collective-permute-start | bytes 196616 | tf_op jit(solution)/shard_map/ppermute | solution.py:433
  61.1 1.5 %collective-permute-start.2 = (bf16[64,512]{1,0:T(8,128)(2,1)S(1)}, bf16[64,512]{1,0:T(8,128)(2,1)S(1)}, u32[]{:S(2)}, u32[]{:S(2)}) collective-permute-start(bf16[64,512]{1,0:T(8,128)(2,1)S(1)} %get-tuple-element.29), channel_id=1, source_target_pairs={{0,4},{1,5},{2,6},{3,7},{4,0},{5,1},{6,2},{7,3},{8,12},{9,13},{10,... | collective-permute-start | bytes 196616 | tf_op jit(solution)/shard_map/ppermute | solution.py:433
  62.6 0.4 collective-permute-start.3
  63.0 5.8 %spread.2.first_hbm.after_ref = f32[1024,512]{1,0:T(8,128)} custom-call(bf16[2048,2048]{1,0:T(8,128)(2,1)} %get-tuple-element.20.adj_ref, bf16[2048,512]{1,0:T(8,128)(2,1)} %get-tuple-element.21.grad_ref), custom_call_target="tpu_custom_call" | custom-call | flops 4294967296 | bytes 16777216 | tf_op jit(solution)/shard_map/spread/pallas_call | solution.py:292
  68.8 0.0 collective-permute-done.1.refs_1_
  68.8 0.0 collective-permute-done.2.refs_2_
  68.8 1.0 %collective-permute-done.3.refs_3_ = bf16[64,512]{1,0:T(8,128)(2,1)S(1)} collective-permute-done((bf16[64,512]{1,0:T(8,128)(2,1)S(1)}, bf16[64,512]{1,0:T(8,128)(2,1)S(1)}, u32[]{:S(2)}, u32[]{:S(2)}) %collective-permute-start.3) | collective-permute-done | bytes 65568 | tf_op jit(solution)/shard_map/ppermute | solution.py:433
  69.8 1.1 %collective-permute-start.4 = (bf16[64,512]{1,0:T(8,128)(2,1)S(1)}, bf16[64,512]{1,0:T(8,128)(2,1)S(1)}, u32[]{:S(2)}, u32[]{:S(2)}) collective-permute-start(bf16[64,512]{1,0:T(8,128)(2,1)S(1)} %add.3.refs_0_), channel_id=1, source_target_pairs={{0,8},{8,0},{16,24},{24,16},{1,9},{9,1},{17,25},{25,17},{2,10},{10... | collective-permute-start | bytes 196616 | tf_op jit(solution)/shard_map/ppermute | solution.py:433
  70.9 5.8 %spread.3.second_hbm.after_ref = f32[1024,512]{1,0:T(8,128)} custom-call(bf16[2048,2048]{1,0:T(8,128)(2,1)} %get-tuple-element.20.adj_ref, bf16[2048,512]{1,0:T(8,128)(2,1)} %get-tuple-element.21.grad_ref), custom_call_target="tpu_custom_call" | custom-call | flops 4294967296 | bytes 16777216 | tf_op jit(solution)/shard_map/spread/pallas_call | solution.py:292
  76.7 3.1 %collective-permute-start.5 = (bf16[64,512]{1,0:T(8,128)(2,1)S(1)}, bf16[64,512]{1,0:T(8,128)(2,1)S(1)}, u32[]{:S(2)}, u32[]{:S(2)}) collective-permute-start(bf16[64,512]{1,0:T(8,128)(2,1)S(1)} %add.4.refs_0_), channel_id=1, source_target_pairs={{0,16},{8,24},{16,0},{24,8},{1,17},{9,25},{17,1},{25,9},{2,18},{10... | collective-permute-start | bytes 196616 | tf_op jit(solution)/shard_map/ppermute | solution.py:433
  79.8 0.1 iota_compare_fusion
  79.9 0.1 squeeze.6
  79.9 0.1 lt.29
  80.0 3.7 %collective-permute-done.5.refs_1_ = bf16[64,512]{1,0:T(8,128)(2,1)S(1)} collective-permute-done((bf16[64,512]{1,0:T(8,128)(2,1)S(1)}, bf16[64,512]{1,0:T(8,128)(2,1)S(1)}, u32[]{:S(2)}, u32[]{:S(2)}) %collective-permute-start.5) | collective-permute-done | bytes 65568 | tf_op jit(solution)/shard_map/ppermute | solution.py:433
  83.8 1.5 %collective-permute-start.6 = (bf16[64,512]{1,0:T(8,128)(2,1)S(1)}, bf16[64,512]{1,0:T(8,128)(2,1)S(1)}, u32[]{:S(2)}, u32[]{:S(2)}) collective-permute-start(bf16[64,512]{1,0:T(8,128)(2,1)S(1)} %add.5.refs_0_), channel_id=1, source_target_pairs={{0,2},{1,3},{2,0},{3,1},{4,6},{5,7},{6,4},{7,5},{8,10},{9,11},{10,... | collective-permute-start | bytes 196616 | tf_op jit(solution)/shard_map/ppermute | solution.py:433
  85.3 1.5 %collective-permute-start.7 = (bf16[64,512]{1,0:T(8,128)(2,1)S(1)}, bf16[64,512]{1,0:T(8,128)(2,1)S(1)}, u32[]{:S(2)}, u32[]{:S(2)}) collective-permute-start(bf16[64,512]{1,0:T(8,128)(2,1)S(1)} %add.5.refs_0_), channel_id=1, source_target_pairs={{0,4},{1,5},{2,6},{3,7},{4,0},{5,1},{6,2},{7,3},{8,12},{9,13},{10,... | collective-permute-start | bytes 196616 | tf_op jit(solution)/shard_map/ppermute | solution.py:433
  86.8 0.5 collective-permute-start.8
  87.4 4.5 %give_back.1.after_ref = bf16[2048,512]{1,0:T(8,128)(2,1)} custom-call(s32[1,1024]{1,0:T(1,128)S(1)} %broadcast_select_fusion.index_ref, f32[1024,512]{1,0:T(8,128)} %spread.2.first_hbm.after_ref, f32[1024,512]{1,0:T(8,128)} %spread.3.second_hbm.after_ref, bf16[1024,512]{1,0:T(8,128)(2,1)S(1)} %bitcast.7), custom_call_target="tpu_custom_call" | custom-call | tf_op jit(solution)/shard_map/give_back/pallas_call | solution.py:334
  91.9 0.1 collective-permute-done.8.refs_3_
  92.0 0.1 collective-permute-start.9
  92.1 0.8 place.2.refs_0_
  92.9 0.7 collective-permute-done.9.half_ref
  93.6 0.8 place.3
  (20 shorter events, 0.2 us)
Async XLA Ops:
  0.6 12.5 %copy-start = (bf16[2048,512]{1,0:T(8,128)(2,1)S(1)}, bf16[2048,512]{1,0:T(8,128)(2,1)}, u32[]{:S(2)}) copy-start(bf16[2048,512]{1,0:T(8,128)(2,1)} %x_ref.3) | copy-start | bytes 6291460
  0.6 12.5 %copy-start.1 = (s32[256]{0:T(256)S(1)}, s32[256]{0:T(256)}, u32[]{:S(2)}) copy-start(s32[256]{0:T(256)} %rows_ref.1) | copy-start | bytes 3076
  0.7 12.5 %copy-start.2 = (s32[256]{0:T(256)S(1)}, s32[256]{0:T(256)}, u32[]{:S(2)}) copy-start(s32[256]{0:T(256)} %cols_ref.1) | copy-start | bytes 3076
  5.8 33.5 %all-to-all-start = ((bf16[32,32,512]{2,1,0:T(8,128)(2,1)}), bf16[32,32,512]{2,1,0:T(8,128)(2,1)S(1)}, u32[]{:S(2)}, u32[]{:S(2)}) async-start(bf16[32,32,512]{2,1,0:T(8,128)(2,1)} %bitcast.9), calls=%async_computation | async-start | bytes 2097152 | tf_op jit(solution)/shard_map/all_to_all | solution.py:351
  51.1 36.3 %all-to-all-start.1 = ((bf16[32,32,512]{2,1,0:T(8,128)(2,1)}), bf16[32,32,512]{2,1,0:T(8,128)(2,1)S(1)}, u32[]{:S(2)}, u32[]{:S(2)}) async-start(bf16[32,32,512]{2,1,0:T(8,128)(2,1)} %bitcast.10), calls=%async_computation.1 | async-start | bytes 2097152 | tf_op jit(solution)/shard_map/all_to_all | solution.py:351
  57.8 1.6 %collective-permute-start = (bf16[256,512]{1,0:T(8,128)(2,1)S(1)}, bf16[256,512]{1,0:T(8,128)(2,1)S(1)}, u32[]{:S(2)}, u32[]{:S(2)}) collective-permute-start(bf16[256,512]{1,0:T(8,128)(2,1)S(1)} %get-tuple-element.26), channel_id=1, source_target_pairs={{0,1},{1,0},{2,3},{3,2},{4,5},{5,4},{6,7},{7,6},{8,9},{9,8},{10,11... | collective-permute-start | bytes 786440 | tf_op jit(solution)/shard_map/ppermute | solution.py:433
  59.5 9.3 %collective-permute-start.1 = (bf16[64,512]{1,0:T(8,128)(2,1)S(1)}, bf16[64,512]{1,0:T(8,128)(2,1)S(1)}, u32[]{:S(2)}, u32[]{:S(2)}) collective-permute-start(bf16[64,512]{1,0:T(8,128)(2,1)S(1)} %get-tuple-element.28), channel_id=1, source_target_pairs={{0,2},{1,3},{2,0},{3,1},{4,6},{5,7},{6,4},{7,5},{8,10},{9,11},{10,... | collective-permute-start | bytes 196616 | tf_op jit(solution)/shard_map/ppermute | solution.py:433
  61.1 7.7 %collective-permute-start.2 = (bf16[64,512]{1,0:T(8,128)(2,1)S(1)}, bf16[64,512]{1,0:T(8,128)(2,1)S(1)}, u32[]{:S(2)}, u32[]{:S(2)}) collective-permute-start(bf16[64,512]{1,0:T(8,128)(2,1)S(1)} %get-tuple-element.29), channel_id=1, source_target_pairs={{0,4},{1,5},{2,6},{3,7},{4,0},{5,1},{6,2},{7,3},{8,12},{9,13},{10,... | collective-permute-start | bytes 196616 | tf_op jit(solution)/shard_map/ppermute | solution.py:433
  62.6 7.2 %collective-permute-start.3 = (bf16[64,512]{1,0:T(8,128)(2,1)S(1)}, bf16[64,512]{1,0:T(8,128)(2,1)S(1)}, u32[]{:S(2)}, u32[]{:S(2)}) collective-permute-start(bf16[64,512]{1,0:T(8,128)(2,1)S(1)} %get-tuple-element.30), channel_id=1, source_target_pairs={{0,6},{1,7},{2,4},{3,5},{4,2},{5,3},{6,0},{7,1},{8,14},{9,15},{10,... | collective-permute-start | bytes 196616 | tf_op jit(solution)/shard_map/ppermute | solution.py:433
  69.8 6.9 %collective-permute-start.4 = (bf16[64,512]{1,0:T(8,128)(2,1)S(1)}, bf16[64,512]{1,0:T(8,128)(2,1)S(1)}, u32[]{:S(2)}, u32[]{:S(2)}) collective-permute-start(bf16[64,512]{1,0:T(8,128)(2,1)S(1)} %add.3.refs_0_), channel_id=1, source_target_pairs={{0,8},{8,0},{16,24},{24,16},{1,9},{9,1},{17,25},{25,17},{2,10},{10... | collective-permute-start | bytes 196616 | tf_op jit(solution)/shard_map/ppermute | solution.py:433
  76.7 3.1 %copy-start.4 = (s32[1,32]{1,0:T(1,128)S(1)}, s32[1,32]{1,0:T(1,128)}, u32[]{:S(2)}) copy-start(s32[1,32]{1,0:T(1,128)} %counts_ref.1) | copy-start | bytes 388
  76.7 3.2 %copy-start.3 = (s32[1,32,32]{2,1,0:T(8,128)S(1)}, s32[1,32,32]{2,1,0:T(8,128)}, u32[]{:S(2)}) copy-start(s32[1,32,32]{2,1,0:T(8,128)} %param.14) | copy-start | bytes 12292
  76.7 7.1 %collective-permute-start.5 = (bf16[64,512]{1,0:T(8,128)(2,1)S(1)}, bf16[64,512]{1,0:T(8,128)(2,1)S(1)}, u32[]{:S(2)}, u32[]{:S(2)}) collective-permute-start(bf16[64,512]{1,0:T(8,128)(2,1)S(1)} %add.4.refs_0_), channel_id=1, source_target_pairs={{0,16},{8,24},{16,0},{24,8},{1,17},{9,25},{17,1},{25,9},{2,18},{10... | collective-permute-start | bytes 196616 | tf_op jit(solution)/shard_map/ppermute | solution.py:433
  83.8 8.1 %collective-permute-start.6 = (bf16[64,512]{1,0:T(8,128)(2,1)S(1)}, bf16[64,512]{1,0:T(8,128)(2,1)S(1)}, u32[]{:S(2)}, u32[]{:S(2)}) collective-permute-start(bf16[64,512]{1,0:T(8,128)(2,1)S(1)} %add.5.refs_0_), channel_id=1, source_target_pairs={{0,2},{1,3},{2,0},{3,1},{4,6},{5,7},{6,4},{7,5},{8,10},{9,11},{10,... | collective-permute-start | bytes 196616 | tf_op jit(solution)/shard_map/ppermute | solution.py:433
  85.3 6.6 %collective-permute-start.7 = (bf16[64,512]{1,0:T(8,128)(2,1)S(1)}, bf16[64,512]{1,0:T(8,128)(2,1)S(1)}, u32[]{:S(2)}, u32[]{:S(2)}) collective-permute-start(bf16[64,512]{1,0:T(8,128)(2,1)S(1)} %add.5.refs_0_), channel_id=1, source_target_pairs={{0,4},{1,5},{2,6},{3,7},{4,0},{5,1},{6,2},{7,3},{8,12},{9,13},{10,... | collective-permute-start | bytes 196616 | tf_op jit(solution)/shard_map/ppermute | solution.py:433
  86.8 5.2 %collective-permute-start.8 = (bf16[64,512]{1,0:T(8,128)(2,1)S(1)}, bf16[64,512]{1,0:T(8,128)(2,1)S(1)}, u32[]{:S(2)}, u32[]{:S(2)}) collective-permute-start(bf16[64,512]{1,0:T(8,128)(2,1)S(1)} %add.5.refs_0_), channel_id=1, source_target_pairs={{0,6},{1,7},{2,4},{3,5},{4,2},{5,3},{6,0},{7,1},{8,14},{9,15},{10,... | collective-permute-start | bytes 196616 | tf_op jit(solution)/shard_map/ppermute | solution.py:433
  92.0 1.6 %collective-permute-start.9 = (bf16[256,512]{1,0:T(8,128)(2,1)S(1)}, bf16[256,512]{1,0:T(8,128)(2,1)S(1)}, u32[]{:S(2)}, u32[]{:S(2)}) collective-permute-start(bf16[256,512]{1,0:T(8,128)(2,1)S(1)} %relay.1.half_ref), channel_id=1, source_target_pairs={{0,1},{1,0},{2,3},{3,2},{4,5},{5,4},{6,7},{7,6},{8,9},{9,8},{10,11... | collective-permute-start | bytes 786440 | tf_op jit(solution)/shard_map/ppermute | solution.py:433

commit v10 on v9

--- a/solution.py
+++ b/solution.py
@@ -8,6 +8,7 @@
 from jax.sharding import PartitionSpec as P
 
 AXES = ("group", "local")
+RANKS = ("local", "group")
 BF16 = jnp.bfloat16
 F32 = jnp.float32
 ROWS = 256
@@ -50,7 +51,7 @@
     return pl.BlockSpec(shape, lambda i, *unused: (0,) * len(shape))
 
 
-def collect_kernel(counts_ref, lists_ref, x_ref, out_ref):
+def collect_kernel(order, counts_ref, lists_ref, x_ref, out_ref):
     dests, slots = lists_ref.shape
     step = BIG // slots
     lane = lax.broadcasted_iota(jnp.int32, (slots, x_ref.shape[0]), 1)
@@ -58,17 +59,17 @@
     turned = lists_ref[...].T
     for first in range(0, dests, step):
         parts = []
-        for d in range(first, first + step):
+        for d in order[first : first + step]:
             named = jnp.where(slot < counts_ref[0, d], turned[:, d : d + 1], -1)
             parts.append(jnp.where(named == lane, 1.0, 0.0).astype(BF16))
         pick = jnp.concatenate(parts, axis=0)
         out_ref[first * slots : (first + step) * slots, :] = dot(pick, x_ref[...]).astype(BF16)
 
 
-def collect(counts, lists, x):
+def collect(order, counts, lists, x):
     dests, slots = lists.shape
     return pl.pallas_call(
-        collect_kernel,
+        functools.partial(collect_kernel, order),
         in_specs=[SMEM, VMEM, VMEM],
         out_shape=jax.ShapeDtypeStruct((dests * slots, x.shape[1]), BF16),
         compiler_params=params(60),
@@ -167,9 +168,9 @@
 
 
 def layer_kernel(
-    far_hbm, own_hbm, cot_hbm, w_hbm, got_ref,
+    order, far_hbm, own_hbm, cot_hbm, w_hbm, got_ref,
     act_hbm, hid_hbm, slope_hbm, grad_hbm, back_hbm,
-    far, own, cot, act, hid, slope, grad, w, back, sems, sent, w_sem,
+    far, own, cot, act, hid, slope, grad, w, near, back, sems, sent, w_sem, back_sems,
 ):
     blocks = sems.shape[1]
     views = [pl.ds(n * BIG, BIG) for n in range(blocks)]
@@ -190,13 +191,16 @@
     coming = [fetch(0)]
     weight = pltpu.make_async_copy(w_hbm, w, w_sem)
     weight.start()
+    slots = near.shape[0] // len(order)
+    for p, s in enumerate(order):
+        near[s * slots : (s + 1) * slots, :] = got_ref[p * slots : (p + 1) * slots, :]
     for n, at in enumerate(views):
         copies = coming[n]
         for copy in copies[:2]:
             copy.wait()
         while len(coming) < min(n + 3, blocks):
             coming.append(fetch(len(coming)))
-        hid[at, :] = (own[at, :] + dot(far[at, :], got_ref[...])).astype(BF16)
+        hid[at, :] = (own[at, :] + dot(far[at, :], near[...])).astype(BF16)
         send(0, n, hid, hid_hbm, at)
         copies[2].wait()
         if n == 0:
@@ -209,22 +213,25 @@
         send(2, n, slope, slope_hbm, at)
         grad[at, :] = dot(slope[at, :], w[...], ((1,), (1,))).astype(BF16)
         send(3, n, grad, grad_hbm, at)
+    place_of = {s: p for p, s in enumerate(order)}
     for n in range(back.shape[0] // BIG):
         at = pl.ds(n * BIG, BIG)
         back[at, :] = dot(far[:, at], grad[...], ((0,), (0,))).astype(BF16)
-        send(4, n, back, back_hbm, at)
+        for s in range(n * BIG // slots, (n + 1) * BIG // slots):
+            rows = back.at[pl.ds(s * slots, slots)]
+            sending.append(pltpu.make_async_copy(rows, back_hbm.at[pl.ds(place_of[s] * slots, slots)], back_sems.at[s]))
+            sending[-1].start()
     for copy in sending:
         copy.wait()
 
 
-def layer(keep, far, own, got, cotangent, weight):
+def layer(keep, order, far, own, got, cotangent, weight):
     owned, width = own.shape
-    remote = got.shape[0]
     blocks = owned // BIG
     (got,) = held(keep, got)
     rows = (owned, width)
     return pl.pallas_call(
-        layer_kernel,
+        functools.partial(layer_kernel, order),
         in_specs=[HBM] * 4 + [VMEM],
         out_specs=[HBM] * 5,
         out_shape=[far_made(rows, BF16)] * 4 + [far_made(got.shape, BF16)],
@@ -233,9 +240,11 @@
         + [
             pltpu.VMEM(weight.shape, BF16),
             pltpu.VMEM(got.shape, BF16),
+            pltpu.VMEM(got.shape, BF16),
             pltpu.SemaphoreType.DMA((3, blocks)),
-            pltpu.SemaphoreType.DMA((5, max(blocks, remote // BIG))),
+            pltpu.SemaphoreType.DMA((4, blocks)),
             pltpu.SemaphoreType.DMA,
+            pltpu.SemaphoreType.DMA((len(order),)),
         ],
         compiler_params=params(40 if keep else 60),
         name="layer",
@@ -440,15 +449,17 @@
     remote = peers * slots
     keep = remote <= rows_own
     me = lax.axis_index("local").astype(jnp.int32).reshape(1)
-    outgoing = collect(counts, lists, features)
-    arrived = exchange(outgoing.reshape(peers, slots, width), AXES).reshape(remote, width)
+    order = [g * locals_ + l for l in range(locals_) for g in range(groups)]
+    outgoing = collect(order, counts, lists, features)
+    arrived = exchange(outgoing.reshape(peers, slots, width), RANKS).reshape(remote, width)
     adjacency, far, own = build(tile_rows, tile_cols, tile_vals, features, remote)
-    activated, hidden, slope, grad, back = layer(keep, far, own, arrived, cotangent, weight)
-    returned = exchange(back.reshape(peers, slots, width), AXES).reshape(remote, width)
+    activated, hidden, slope, grad, back = layer(keep, order, far, own, arrived, cotangent, weight)
+    returned = exchange(back.reshape(peers, slots, width), RANKS).reshape(remote, width)
     first = spread(adjacency, grad, 0, 2)
     second = spread(adjacency, grad, 1, 2)
     live = jnp.arange(slots)[None, :] < counts[0][:, None]
-    feature_grad = give_back(keep, jnp.where(live, lists, -1).reshape(1, remote), first, second, returned)
+    index = jnp.where(live, lists, -1).reshape(groups, locals_, slots).swapaxes(0, 1).reshape(1, remote)
+    feature_grad = give_back(keep, index, first, second, returned)
     chips = locals_ // 2
     mine, other = partial_grad(keep, me, hidden, slope)
     pieces = cut(me, mine, swap(other, "local", locals_, 1), chips)

time: 95 us -> 95 us (level)
  waiting for transfers between devices: 13.6 us -> 10.3 us
  starting transfers between devices: 22.6 us -> 24.4 us
    ppermute x10, waiting for transfers between devices: 6.9 us -> 4.77 us  [swap(): return lax.ppermute(x, axis, [(i, i ^ k) for i in range(size)])]
    all_to_all x2, waiting for transfers between devices: 6.68 us -> 5.5 us  [exchange(): return lax.all_to_all(x, axes, split_axis=0, concat_axis=0, tiled=True)]
    ppermute x10, starting transfers between devices: 11.5 us -> 12.4 us  [swap(): return lax.ppermute(x, axis, [(i, i ^ k) for i in range(size)])]
  transfers between devices with their start and end apart: 12 -> 12, of which waited for: 6 -> 5; matrix products, arithmetic and copies ran while one was open for 0% -> 2% of each run, Pallas kernels for 42% -> 42%
where the time goes in v10:
time: 95 us; the launch traced here: 94.6 us
  Pallas kernels  57.5 us (61%)
  starting transfers between devices  24.4 us (26%)
  waiting for transfers between devices  10.3 us (11%)
  between operations  0.97 us (1%)
    pallas_call x1, Pallas kernels, build(): pl.pallas_call(build_kernel, grid_spec=pltpu.PrefetchScalarGridSpec(num_s...  19.5 us
    ppermute x10, starting transfers between devices, swap(): return lax.ppermute(x, axis, [(i, i ^ k) for i in range(size)])  12.4 us
    all_to_all x2, starting transfers between devices, exchange(): return lax.all_to_all(x, axes, split_axis=0, concat_axis=0, tiled=True)  11.9 us
    pallas_call x1, Pallas kernels, layer(): pl.pallas_call(functools.partial(layer_kernel, order), in_specs=[HBM] * 4...  11.9 us
    pallas_call x2, Pallas kernels, spread(): pl.pallas_call(spread_kernel, grid=(blocks,), in_specs=[pl.BlockSpec((own...  11.6 us
    all_to_all x2, waiting for transfers between devices, exchange(): return lax.all_to_all(x, axes, split_axis=0, concat_axis=0, tiled=True)  5.5 us
    pallas_call x1, Pallas kernels, collect(): pl.pallas_call(functools.partial(collect_kernel, order), in_specs=[SMEM,...  5.17 us
    ppermute x10, waiting for transfers between devices, swap(): return lax.ppermute(x, axis, [(i, i ^ k) for i in range(size)])  4.77 us
  transfers between devices with their start and end apart: 12, of which 5 were waited for; matrix products, arithmetic and copies ran while one was open for 2% of the time, Pallas kernels for 42%

profile of v10, /device:TPU:0, one launch (start us, length us, event | category | flops | bytes accessed | tf_op | source)
XLA Modules:
  0.0 94.6 jit_solution(4804713703809032397)
XLA Ops:
  0.7 5.2 %collect.1 = bf16[1024,512]{1,0:T(8,128)(2,1)} custom-call(s32[1,32]{1,0:T(1,128)} %counts_ref.1, s32[32,32]{1,0:T(8,128)} %bitcast.13, bf16[2048,512]{1,0:T(8,128)(2,1)} %x_ref.3), custom_call_target="tpu_custom_call" | custom-call | tf_op jit(solution)/shard_map/collect/pallas_call | solution.py:71
  5.8 7.3 %all-to-all-start = ((bf16[32,32,512]{2,1,0:T(8,128)(2,1)}), bf16[32,32,512]{2,1,0:T(8,128)(2,1)S(1)}, u32[]{:S(2)}, u32[]{:S(2)}) async-start(bf16[32,32,512]{2,1,0:T(8,128)(2,1)} %bitcast.11), calls=%async_computation | async-start | bytes 2097152 | tf_op jit(solution)/shard_map/all_to_all | solution.py:360
  13.2 19.5 %build.1 = (bf16[2048,2048]{1,0:T(8,128)(2,1)}, bf16[2048,1024]{1,0:T(8,128)(2,1)}, f32[2048,512]{1,0:T(8,128)}) custom-call(s32[256]{0:T(256)S(1)} %copy-done.1, s32[256]{0:T(256)S(1)} %copy-done.2, bf16[256,128,128]{2,1,0:T(8,128)(2,1)} %tiles_ref.1, bf16[2048,512]{1,0:T(8,128)(2,1)S(1)} %copy-done), custom_call_target="tpu_custom_call" | custom-call | flops 4294967296 | bytes 41943040 | tf_op jit(solution)/shard_map/build/pallas_call | solution.py:139
  32.7 5.5 %all-to-all-done = bf16[32,32,512]{2,1,0:T(8,128)(2,1)S(1)} async-done(((bf16[32,32,512]{2,1,0:T(8,128)(2,1)}), bf16[32,32,512]{2,1,0:T(8,128)(2,1)S(1)}, u32[]{:S(2)}, u32[]{:S(2)}) %all-to-all-start) | async-done | bytes 1048608 | tf_op jit(solution)/shard_map/all_to_all | solution.py:360
  38.2 11.9 %layer.1 = (bf16[2048,512]{1,0:T(8,128)(2,1)}, bf16[2048,512]{1,0:T(8,128)(2,1)}, bf16[2048,512]{1,0:T(8,128)(2,1)}, bf16[2048,512]{1,0:T(8,128)(2,1)}, bf16[1024,512]{1,0:T(8,128)(2,1)}) custom-call(bf16[2048,1024]{1,0:T(8,128)(2,1)} %get-tuple-element.17.far_hbm, f32[2048,512]{1,0:T(8,128)} %get-tuple-element.18.own_hbm, bf16[2048,512]{1,0:T(8,128)(2,1)} %cot_hbm.1, ...), custom_call_target="tpu_custom_call" | custom-call | tf_op jit(solution)/shard_map/layer/pallas_call | solution.py:233
  50.1 4.6 %all-to-all-start.1 = ((bf16[32,32,512]{2,1,0:T(8,128)(2,1)}), bf16[32,32,512]{2,1,0:T(8,128)(2,1)S(1)}, u32[]{:S(2)}, u32[]{:S(2)}) async-start(bf16[32,32,512]{2,1,0:T(8,128)(2,1)} %bitcast.12), calls=%async_computation.1 | async-start | bytes 2097152 | tf_op jit(solution)/shard_map/all_to_all | solution.py:360
  54.8 2.9 %partial_grad.1 = (f32[256,512]{1,0:T(8,128)S(1)}, bf16[256,512]{1,0:T(8,128)(2,1)S(1)}) custom-call(s32[1]{0:T(128)} %bitcast.7.me_ref, bf16[2048,512]{1,0:T(8,128)(2,1)} %get-tuple-element.23.hid_hbm, bf16[2048,512]{1,0:T(8,128)(2,1)} %get-tuple-element.24.slope_hbm), custom_call_target="tpu_custom_call" | custom-call | tf_op jit(solution)/shard_map/partial_grad/pallas_call | solution.py:278
  57.7 0.1 collective-permute-start
  57.8 1.5 %collective-permute-done.got_ref = bf16[256,512]{1,0:T(8,128)(2,1)S(1)} collective-permute-done((bf16[256,512]{1,0:T(8,128)(2,1)S(1)}, bf16[256,512]{1,0:T(8,128)(2,1)S(1)}, u32[]{:S(2)}, u32[]{:S(2)}) %collective-permute-start) | collective-permute-done | bytes 262176 | tf_op jit(solution)/shard_map/ppermute | solution.py:442
  59.3 1.7 %collective-permute-start.1 = (bf16[64,512]{1,0:T(8,128)(2,1)S(1)}, bf16[64,512]{1,0:T(8,128)(2,1)S(1)}, u32[]{:S(2)}, u32[]{:S(2)}) collective-permute-start(bf16[64,512]{1,0:T(8,128)(2,1)S(1)} %get-tuple-element.28), channel_id=1, source_target_pairs={{0,2},{1,3},{2,0},{3,1},{4,6},{5,7},{6,4},{7,5},{8,10},{9,11},{10,... | collective-permute-start | bytes 196616 | tf_op jit(solution)/shard_map/ppermute | solution.py:442
  61.0 1.5 %collective-permute-start.2 = (bf16[64,512]{1,0:T(8,128)(2,1)S(1)}, bf16[64,512]{1,0:T(8,128)(2,1)S(1)}, u32[]{:S(2)}, u32[]{:S(2)}) collective-permute-start(bf16[64,512]{1,0:T(8,128)(2,1)S(1)} %get-tuple-element.29), channel_id=1, source_target_pairs={{0,4},{1,5},{2,6},{3,7},{4,0},{5,1},{6,2},{7,3},{8,12},{9,13},{10,... | collective-permute-start | bytes 196616 | tf_op jit(solution)/shard_map/ppermute | solution.py:442
  62.5 0.4 collective-permute-start.3
  62.9 5.8 %spread.2.first_hbm.after_ref = f32[1024,512]{1,0:T(8,128)} custom-call(bf16[2048,2048]{1,0:T(8,128)(2,1)} %get-tuple-element.20.adj_ref, bf16[2048,512]{1,0:T(8,128)(2,1)} %get-tuple-element.21.grad_ref), custom_call_target="tpu_custom_call" | custom-call | flops 4294967296 | bytes 16777216 | tf_op jit(solution)/shard_map/spread/pallas_call | solution.py:301
  68.7 0.6 collective-permute-done.2.refs_2_
  69.3 1.1 %collective-permute-start.4 = (bf16[64,512]{1,0:T(8,128)(2,1)S(1)}, bf16[64,512]{1,0:T(8,128)(2,1)S(1)}, u32[]{:S(2)}, u32[]{:S(2)}) collective-permute-start(bf16[64,512]{1,0:T(8,128)(2,1)S(1)} %add.7.refs_0_), channel_id=1, source_target_pairs={{0,8},{8,0},{16,24},{24,16},{1,9},{9,1},{17,25},{25,17},{2,10},{10... | collective-permute-start | bytes 196616 | tf_op jit(solution)/shard_map/ppermute | solution.py:442
  70.4 5.8 %spread.3.second_hbm.after_ref = f32[1024,512]{1,0:T(8,128)} custom-call(bf16[2048,2048]{1,0:T(8,128)(2,1)} %get-tuple-element.20.adj_ref, bf16[2048,512]{1,0:T(8,128)(2,1)} %get-tuple-element.21.grad_ref), custom_call_target="tpu_custom_call" | custom-call | flops 4294967296 | bytes 16777216 | tf_op jit(solution)/shard_map/spread/pallas_call | solution.py:301
  76.3 4.0 %collective-permute-start.5 = (bf16[64,512]{1,0:T(8,128)(2,1)S(1)}, bf16[64,512]{1,0:T(8,128)(2,1)S(1)}, u32[]{:S(2)}, u32[]{:S(2)}) collective-permute-start(bf16[64,512]{1,0:T(8,128)(2,1)S(1)} %add.8.refs_0_), channel_id=1, source_target_pairs={{0,16},{8,24},{16,0},{24,8},{1,17},{9,25},{17,1},{25,9},{2,18},{10... | collective-permute-start | bytes 196616 | tf_op jit(solution)/shard_map/ppermute | solution.py:442
  80.2 0.5 broadcast.9
  80.7 0.7 reduce.3
  81.4 0.1 lt.17
  81.5 0.1 copy.12
  81.6 2.1 %collective-permute-done.5.refs_1_ = bf16[64,512]{1,0:T(8,128)(2,1)S(1)} collective-permute-done((bf16[64,512]{1,0:T(8,128)(2,1)S(1)}, bf16[64,512]{1,0:T(8,128)(2,1)S(1)}, u32[]{:S(2)}, u32[]{:S(2)}) %collective-permute-start.5) | collective-permute-done | bytes 65568 | tf_op jit(solution)/shard_map/ppermute | solution.py:442
  83.7 1.5 %collective-permute-start.6 = (bf16[64,512]{1,0:T(8,128)(2,1)S(1)}, bf16[64,512]{1,0:T(8,128)(2,1)S(1)}, u32[]{:S(2)}, u32[]{:S(2)}) collective-permute-start(bf16[64,512]{1,0:T(8,128)(2,1)S(1)} %add.9.refs_0_), channel_id=1, source_target_pairs={{0,2},{1,3},{2,0},{3,1},{4,6},{5,7},{6,4},{7,5},{8,10},{9,11},{10,... | collective-permute-start | bytes 196616 | tf_op jit(solution)/shard_map/ppermute | solution.py:442
  85.2 1.5 %collective-permute-start.7 = (bf16[64,512]{1,0:T(8,128)(2,1)S(1)}, bf16[64,512]{1,0:T(8,128)(2,1)S(1)}, u32[]{:S(2)}, u32[]{:S(2)}) collective-permute-start(bf16[64,512]{1,0:T(8,128)(2,1)S(1)} %add.9.refs_0_), channel_id=1, source_target_pairs={{0,4},{1,5},{2,6},{3,7},{4,0},{5,1},{6,2},{7,3},{8,12},{9,13},{10,... | collective-permute-start | bytes 196616 | tf_op jit(solution)/shard_map/ppermute | solution.py:442
  86.7 0.5 collective-permute-start.8
  87.2 0.1 fusion
  87.3 0.1 reshape.37.index_ref
  87.4 4.5 %give_back.1.after_ref = bf16[2048,512]{1,0:T(8,128)(2,1)} custom-call(s32[1,1024]{1,0:T(1,128)S(1)} %reshape.37.index_ref, f32[1024,512]{1,0:T(8,128)} %spread.2.first_hbm.after_ref, f32[1024,512]{1,0:T(8,128)} %spread.3.second_hbm.after_ref, bf16[1024,512]{1,0:T(8,128)(2,1)S(1)} %bitcast.9), custom_call_target="tpu_custom_call" | custom-call | tf_op jit(solution)/shard_map/give_back/pallas_call | solution.py:343
  92.0 0.1 collective-permute-start.9
  92.1 0.8 place.2.refs_0_
  92.9 0.7 collective-permute-done.9.half_ref
  93.6 0.8 place.3
  (22 shorter events, 0.2 us)
Async XLA Ops:
  0.6 12.5 %copy-start = (bf16[2048,512]{1,0:T(8,128)(2,1)S(1)}, bf16[2048,512]{1,0:T(8,128)(2,1)}, u32[]{:S(2)}) copy-start(bf16[2048,512]{1,0:T(8,128)(2,1)} %x_ref.3) | copy-start | bytes 6291460
  0.6 12.5 %copy-start.1 = (s32[256]{0:T(256)S(1)}, s32[256]{0:T(256)}, u32[]{:S(2)}) copy-start(s32[256]{0:T(256)} %rows_ref.1) | copy-start | bytes 3076
  0.7 12.5 %copy-start.2 = (s32[256]{0:T(256)S(1)}, s32[256]{0:T(256)}, u32[]{:S(2)}) copy-start(s32[256]{0:T(256)} %cols_ref.1) | copy-start | bytes 3076
  5.8 32.4 %all-to-all-start = ((bf16[32,32,512]{2,1,0:T(8,128)(2,1)}), bf16[32,32,512]{2,1,0:T(8,128)(2,1)S(1)}, u32[]{:S(2)}, u32[]{:S(2)}) async-start(bf16[32,32,512]{2,1,0:T(8,128)(2,1)} %bitcast.11), calls=%async_computation | async-start | bytes 2097152 | tf_op jit(solution)/shard_map/all_to_all | solution.py:360
  50.1 37.3 %all-to-all-start.1 = ((bf16[32,32,512]{2,1,0:T(8,128)(2,1)}), bf16[32,32,512]{2,1,0:T(8,128)(2,1)S(1)}, u32[]{:S(2)}, u32[]{:S(2)}) async-start(bf16[32,32,512]{2,1,0:T(8,128)(2,1)} %bitcast.12), calls=%async_computation.1 | async-start | bytes 2097152 | tf_op jit(solution)/shard_map/all_to_all | solution.py:360
  57.7 1.6 %collective-permute-start = (bf16[256,512]{1,0:T(8,128)(2,1)S(1)}, bf16[256,512]{1,0:T(8,128)(2,1)S(1)}, u32[]{:S(2)}, u32[]{:S(2)}) collective-permute-start(bf16[256,512]{1,0:T(8,128)(2,1)S(1)} %get-tuple-element.26), channel_id=1, source_target_pairs={{0,1},{1,0},{2,3},{3,2},{4,5},{5,4},{6,7},{7,6},{8,9},{9,8},{10,11... | collective-permute-start | bytes 786440 | tf_op jit(solution)/shard_map/ppermute | solution.py:442
  59.3 9.3 %collective-permute-start.1 = (bf16[64,512]{1,0:T(8,128)(2,1)S(1)}, bf16[64,512]{1,0:T(8,128)(2,1)S(1)}, u32[]{:S(2)}, u32[]{:S(2)}) collective-permute-start(bf16[64,512]{1,0:T(8,128)(2,1)S(1)} %get-tuple-element.28), channel_id=1, source_target_pairs={{0,2},{1,3},{2,0},{3,1},{4,6},{5,7},{6,4},{7,5},{8,10},{9,11},{10,... | collective-permute-start | bytes 196616 | tf_op jit(solution)/shard_map/ppermute | solution.py:442
  61.0 8.2 %collective-permute-start.2 = (bf16[64,512]{1,0:T(8,128)(2,1)S(1)}, bf16[64,512]{1,0:T(8,128)(2,1)S(1)}, u32[]{:S(2)}, u32[]{:S(2)}) collective-permute-start(bf16[64,512]{1,0:T(8,128)(2,1)S(1)} %get-tuple-element.29), channel_id=1, source_target_pairs={{0,4},{1,5},{2,6},{3,7},{4,0},{5,1},{6,2},{7,3},{8,12},{9,13},{10,... | collective-permute-start | bytes 196616 | tf_op jit(solution)/shard_map/ppermute | solution.py:442
  62.5 6.8 %collective-permute-start.3 = (bf16[64,512]{1,0:T(8,128)(2,1)S(1)}, bf16[64,512]{1,0:T(8,128)(2,1)S(1)}, u32[]{:S(2)}, u32[]{:S(2)}) collective-permute-start(bf16[64,512]{1,0:T(8,128)(2,1)S(1)} %get-tuple-element.30), channel_id=1, source_target_pairs={{0,6},{1,7},{2,4},{3,5},{4,2},{5,3},{6,0},{7,1},{8,14},{9,15},{10,... | collective-permute-start | bytes 196616 | tf_op jit(solution)/shard_map/ppermute | solution.py:442
  69.3 7.0 %collective-permute-start.4 = (bf16[64,512]{1,0:T(8,128)(2,1)S(1)}, bf16[64,512]{1,0:T(8,128)(2,1)S(1)}, u32[]{:S(2)}, u32[]{:S(2)}) collective-permute-start(bf16[64,512]{1,0:T(8,128)(2,1)S(1)} %add.7.refs_0_), channel_id=1, source_target_pairs={{0,8},{8,0},{16,24},{24,16},{1,9},{9,1},{17,25},{25,17},{2,10},{10... | collective-permute-start | bytes 196616 | tf_op jit(solution)/shard_map/ppermute | solution.py:442
  76.2 4.5 %copy-start.4 = (s32[1,32]{1,0:T(1,128)S(1)}, s32[1,32]{1,0:T(1,128)}, u32[]{:S(2)}) copy-start(s32[1,32]{1,0:T(1,128)} %counts_ref.1) | copy-start | bytes 388
  76.2 11.0 %copy-start.3 = (s32[1,32,32]{2,1,0:T(8,128)S(1)}, s32[1,32,32]{2,1,0:T(8,128)}, u32[]{:S(2)}) copy-start(s32[1,32,32]{2,1,0:T(8,128)} %param.14) | copy-start | bytes 12292
  76.3 7.4 %collective-permute-start.5 = (bf16[64,512]{1,0:T(8,128)(2,1)S(1)}, bf16[64,512]{1,0:T(8,128)(2,1)S(1)}, u32[]{:S(2)}, u32[]{:S(2)}) collective-permute-start(bf16[64,512]{1,0:T(8,128)(2,1)S(1)} %add.8.refs_0_), channel_id=1, source_target_pairs={{0,16},{8,24},{16,0},{24,8},{1,17},{9,25},{17,1},{25,9},{2,18},{10... | collective-permute-start | bytes 196616 | tf_op jit(solution)/shard_map/ppermute | solution.py:442
  83.7 8.3 %collective-permute-start.6 = (bf16[64,512]{1,0:T(8,128)(2,1)S(1)}, bf16[64,512]{1,0:T(8,128)(2,1)S(1)}, u32[]{:S(2)}, u32[]{:S(2)}) collective-permute-start(bf16[64,512]{1,0:T(8,128)(2,1)S(1)} %add.9.refs_0_), channel_id=1, source_target_pairs={{0,2},{1,3},{2,0},{3,1},{4,6},{5,7},{6,4},{7,5},{8,10},{9,11},{10,... | collective-permute-start | bytes 196616 | tf_op jit(solution)/shard_map/ppermute | solution.py:442
  85.2 6.7 %collective-permute-start.7 = (bf16[64,512]{1,0:T(8,128)(2,1)S(1)}, bf16[64,512]{1,0:T(8,128)(2,1)S(1)}, u32[]{:S(2)}, u32[]{:S(2)}) collective-permute-start(bf16[64,512]{1,0:T(8,128)(2,1)S(1)} %add.9.refs_0_), channel_id=1, source_target_pairs={{0,4},{1,5},{2,6},{3,7},{4,0},{5,1},{6,2},{7,3},{8,12},{9,13},{10,... | collective-permute-start | bytes 196616 | tf_op jit(solution)/shard_map/ppermute | solution.py:442
  86.7 5.3 %collective-permute-start.8 = (bf16[64,512]{1,0:T(8,128)(2,1)S(1)}, bf16[64,512]{1,0:T(8,128)(2,1)S(1)}, u32[]{:S(2)}, u32[]{:S(2)}) collective-permute-start(bf16[64,512]{1,0:T(8,128)(2,1)S(1)} %add.9.refs_0_), channel_id=1, source_target_pairs={{0,6},{1,7},{2,4},{3,5},{4,2},{5,3},{6,0},{7,1},{8,14},{9,15},{10,... | collective-permute-start | bytes 196616 | tf_op jit(solution)/shard_map/ppermute | solution.py:442
  92.0 1.6 %collective-permute-start.9 = (bf16[256,512]{1,0:T(8,128)(2,1)S(1)}, bf16[256,512]{1,0:T(8,128)(2,1)S(1)}, u32[]{:S(2)}, u32[]{:S(2)}) collective-permute-start(bf16[256,512]{1,0:T(8,128)(2,1)S(1)} %relay.1.half_ref), channel_id=1, source_target_pairs={{0,1},{1,0},{2,3},{3,2},{4,5},{5,4},{6,7},{7,6},{8,9},{9,8},{10,11... | collective-permute-start | bytes 786440 | tf_op jit(solution)/shard_map/ppermute | solution.py:442

commit v11 on v10

--- a/solution.py
+++ b/solution.py
@@ -53,7 +53,7 @@
 
 def collect_kernel(order, counts_ref, lists_ref, x_ref, out_ref):
     dests, slots = lists_ref.shape
-    step = BIG // slots
+    step = 2 * BIG // slots
     lane = lax.broadcasted_iota(jnp.int32, (slots, x_ref.shape[0]), 1)
     slot = lax.broadcasted_iota(jnp.int32, (slots, 1), 0)
     turned = lists_ref[...].T

time: 95 us -> 95 us (level)
  no operation moved by 1% of the time
where the time goes in v11:
time: 95 us; the launch traced here: 94.6 us
  Pallas kernels  57.5 us (61%)
  starting transfers between devices  24.4 us (26%)
  waiting for transfers between devices  10.3 us (11%)
  between operations  0.97 us (1%)
    pallas_call x1, Pallas kernels, build(): pl.pallas_call(build_kernel, grid_spec=pltpu.PrefetchScalarGridSpec(num_s...  19.5 us
    ppermute x10, starting transfers between devices, swap(): return lax.ppermute(x, axis, [(i, i ^ k) for i in range(size)])  12.4 us
    all_to_all x2, starting transfers between devices, exchange(): return lax.all_to_all(x, axes, split_axis=0, concat_axis=0, tiled=True)  11.9 us
    pallas_call x1, Pallas kernels, layer(): pl.pallas_call(functools.partial(layer_kernel, order), in_specs=[HBM] * 4...  11.9 us
    pallas_call x2, Pallas kernels, spread(): pl.pallas_call(spread_kernel, grid=(blocks,), in_specs=[pl.BlockSpec((own...  11.6 us
    all_to_all x2, waiting for transfers between devices, exchange(): return lax.all_to_all(x, axes, split_axis=0, concat_axis=0, tiled=True)  5.51 us
    pallas_call x1, Pallas kernels, collect(): pl.pallas_call(functools.partial(collect_kernel, order), in_specs=[SMEM,...  5.17 us
    ppermute x10, waiting for transfers between devices, swap(): return lax.ppermute(x, axis, [(i, i ^ k) for i in range(size)])  4.76 us
  transfers between devices with their start and end apart: 12, of which 5 were waited for; matrix products, arithmetic and copies ran while one was open for 2% of the time, Pallas kernels for 42%

profile of v11, /device:TPU:0, one launch (start us, length us, event | category | flops | bytes accessed | tf_op | source)
XLA Modules:
  0.0 94.6 jit_solution(10944011636059428881)
XLA Ops:
  0.7 5.2 %collect.1 = bf16[1024,512]{1,0:T(8,128)(2,1)} custom-call(s32[1,32]{1,0:T(1,128)} %counts_ref.1, s32[32,32]{1,0:T(8,128)} %bitcast.13, bf16[2048,512]{1,0:T(8,128)(2,1)} %x_ref.3), custom_call_target="tpu_custom_call" | custom-call | tf_op jit(solution)/shard_map/collect/pallas_call | solution.py:71
  5.8 7.3 %all-to-all-start = ((bf16[32,32,512]{2,1,0:T(8,128)(2,1)}), bf16[32,32,512]{2,1,0:T(8,128)(2,1)S(1)}, u32[]{:S(2)}, u32[]{:S(2)}) async-start(bf16[32,32,512]{2,1,0:T(8,128)(2,1)} %bitcast.11), calls=%async_computation | async-start | bytes 2097152 | tf_op jit(solution)/shard_map/all_to_all | solution.py:360
  13.2 19.5 %build.1 = (bf16[2048,2048]{1,0:T(8,128)(2,1)}, bf16[2048,1024]{1,0:T(8,128)(2,1)}, f32[2048,512]{1,0:T(8,128)}) custom-call(s32[256]{0:T(256)S(1)} %copy-done.1, s32[256]{0:T(256)S(1)} %copy-done.2, bf16[256,128,128]{2,1,0:T(8,128)(2,1)} %tiles_ref.1, bf16[2048,512]{1,0:T(8,128)(2,1)S(1)} %copy-done), custom_call_target="tpu_custom_call" | custom-call | flops 4294967296 | bytes 41943040 | tf_op jit(solution)/shard_map/build/pallas_call | solution.py:139
  32.7 5.5 %all-to-all-done = bf16[32,32,512]{2,1,0:T(8,128)(2,1)S(1)} async-done(((bf16[32,32,512]{2,1,0:T(8,128)(2,1)}), bf16[32,32,512]{2,1,0:T(8,128)(2,1)S(1)}, u32[]{:S(2)}, u32[]{:S(2)}) %all-to-all-start) | async-done | bytes 1048608 | tf_op jit(solution)/shard_map/all_to_all | solution.py:360
  38.2 11.9 %layer.1 = (bf16[2048,512]{1,0:T(8,128)(2,1)}, bf16[2048,512]{1,0:T(8,128)(2,1)}, bf16[2048,512]{1,0:T(8,128)(2,1)}, bf16[2048,512]{1,0:T(8,128)(2,1)}, bf16[1024,512]{1,0:T(8,128)(2,1)}) custom-call(bf16[2048,1024]{1,0:T(8,128)(2,1)} %get-tuple-element.17.far_hbm, f32[2048,512]{1,0:T(8,128)} %get-tuple-element.18.own_hbm, bf16[2048,512]{1,0:T(8,128)(2,1)} %cot_hbm.1, ...), custom_call_target="tpu_custom_call" | custom-call | tf_op jit(solution)/shard_map/layer/pallas_call | solution.py:233
  50.1 4.6 %all-to-all-start.1 = ((bf16[32,32,512]{2,1,0:T(8,128)(2,1)}), bf16[32,32,512]{2,1,0:T(8,128)(2,1)S(1)}, u32[]{:S(2)}, u32[]{:S(2)}) async-start(bf16[32,32,512]{2,1,0:T(8,128)(2,1)} %bitcast.12), calls=%async_computation.1 | async-start | bytes 2097152 | tf_op jit(solution)/shard_map/all_to_all | solution.py:360
  54.8 2.9 %partial_grad.1 = (f32[256,512]{1,0:T(8,128)S(1)}, bf16[256,512]{1,0:T(8,128)(2,1)S(1)}) custom-call(s32[1]{0:T(128)} %bitcast.7.me_ref, bf16[2048,512]{1,0:T(8,128)(2,1)} %get-tuple-element.23.hid_hbm, bf16[2048,512]{1,0:T(8,128)(2,1)} %get-tuple-element.24.slope_hbm), custom_call_target="tpu_custom_call" | custom-call | tf_op jit(solution)/shard_map/partial_grad/pallas_call | solution.py:278
  57.7 0.1 collective-permute-start
  57.8 1.5 %collective-permute-done.got_ref = bf16[256,512]{1,0:T(8,128)(2,1)S(1)} collective-permute-done((bf16[256,512]{1,0:T(8,128)(2,1)S(1)}, bf16[256,512]{1,0:T(8,128)(2,1)S(1)}, u32[]{:S(2)}, u32[]{:S(2)}) %collective-permute-start) | collective-permute-done | bytes 262176 | tf_op jit(solution)/shard_map/ppermute | solution.py:442
  59.3 1.7 %collective-permute-start.1 = (bf16[64,512]{1,0:T(8,128)(2,1)S(1)}, bf16[64,512]{1,0:T(8,128)(2,1)S(1)}, u32[]{:S(2)}, u32[]{:S(2)}) collective-permute-start(bf16[64,512]{1,0:T(8,128)(2,1)S(1)} %get-tuple-element.28), channel_id=1, source_target_pairs={{0,2},{1,3},{2,0},{3,1},{4,6},{5,7},{6,4},{7,5},{8,10},{9,11},{10,... | collective-permute-start | bytes 196616 | tf_op jit(solution)/shard_map/ppermute | solution.py:442
  61.0 1.5 %collective-permute-start.2 = (bf16[64,512]{1,0:T(8,128)(2,1)S(1)}, bf16[64,512]{1,0:T(8,128)(2,1)S(1)}, u32[]{:S(2)}, u32[]{:S(2)}) collective-permute-start(bf16[64,512]{1,0:T(8,128)(2,1)S(1)} %get-tuple-element.29), channel_id=1, source_target_pairs={{0,4},{1,5},{2,6},{3,7},{4,0},{5,1},{6,2},{7,3},{8,12},{9,13},{10,... | collective-permute-start | bytes 196616 | tf_op jit(solution)/shard_map/ppermute | solution.py:442
  62.5 0.4 collective-permute-start.3
  62.9 5.8 %spread.2.first_hbm.after_ref = f32[1024,512]{1,0:T(8,128)} custom-call(bf16[2048,2048]{1,0:T(8,128)(2,1)} %get-tuple-element.20.adj_ref, bf16[2048,512]{1,0:T(8,128)(2,1)} %get-tuple-element.21.grad_ref), custom_call_target="tpu_custom_call" | custom-call | flops 4294967296 | bytes 16777216 | tf_op jit(solution)/shard_map/spread/pallas_call | solution.py:301
  68.7 0.5 collective-permute-done.2.refs_2_
  69.3 1.1 %collective-permute-start.4 = (bf16[64,512]{1,0:T(8,128)(2,1)S(1)}, bf16[64,512]{1,0:T(8,128)(2,1)S(1)}, u32[]{:S(2)}, u32[]{:S(2)}) collective-permute-start(bf16[64,512]{1,0:T(8,128)(2,1)S(1)} %add.7.refs_0_), channel_id=1, source_target_pairs={{0,8},{8,0},{16,24},{24,16},{1,9},{9,1},{17,25},{25,17},{2,10},{10... | collective-permute-start | bytes 196616 | tf_op jit(solution)/shard_map/ppermute | solution.py:442
  70.4 5.8 %spread.3.second_hbm.after_ref = f32[1024,512]{1,0:T(8,128)} custom-call(bf16[2048,2048]{1,0:T(8,128)(2,1)} %get-tuple-element.20.adj_ref, bf16[2048,512]{1,0:T(8,128)(2,1)} %get-tuple-element.21.grad_ref), custom_call_target="tpu_custom_call" | custom-call | flops 4294967296 | bytes 16777216 | tf_op jit(solution)/shard_map/spread/pallas_call | solution.py:301
  76.2 4.0 %collective-permute-start.5 = (bf16[64,512]{1,0:T(8,128)(2,1)S(1)}, bf16[64,512]{1,0:T(8,128)(2,1)S(1)}, u32[]{:S(2)}, u32[]{:S(2)}) collective-permute-start(bf16[64,512]{1,0:T(8,128)(2,1)S(1)} %add.8.refs_0_), channel_id=1, source_target_pairs={{0,16},{8,24},{16,0},{24,8},{1,17},{9,25},{17,1},{25,9},{2,18},{10... | collective-permute-start | bytes 196616 | tf_op jit(solution)/shard_map/ppermute | solution.py:442
  80.2 0.5 broadcast.9
  80.7 0.7 reduce.3
  81.4 0.1 lt.17
  81.5 0.1 copy.12
  81.6 2.1 %collective-permute-done.5.refs_1_ = bf16[64,512]{1,0:T(8,128)(2,1)S(1)} collective-permute-done((bf16[64,512]{1,0:T(8,128)(2,1)S(1)}, bf16[64,512]{1,0:T(8,128)(2,1)S(1)}, u32[]{:S(2)}, u32[]{:S(2)}) %collective-permute-start.5) | collective-permute-done | bytes 65568 | tf_op jit(solution)/shard_map/ppermute | solution.py:442
  83.7 1.5 %collective-permute-start.6 = (bf16[64,512]{1,0:T(8,128)(2,1)S(1)}, bf16[64,512]{1,0:T(8,128)(2,1)S(1)}, u32[]{:S(2)}, u32[]{:S(2)}) collective-permute-start(bf16[64,512]{1,0:T(8,128)(2,1)S(1)} %add.9.refs_0_), channel_id=1, source_target_pairs={{0,2},{1,3},{2,0},{3,1},{4,6},{5,7},{6,4},{7,5},{8,10},{9,11},{10,... | collective-permute-start | bytes 196616 | tf_op jit(solution)/shard_map/ppermute | solution.py:442
  85.2 1.5 %collective-permute-start.7 = (bf16[64,512]{1,0:T(8,128)(2,1)S(1)}, bf16[64,512]{1,0:T(8,128)(2,1)S(1)}, u32[]{:S(2)}, u32[]{:S(2)}) collective-permute-start(bf16[64,512]{1,0:T(8,128)(2,1)S(1)} %add.9.refs_0_), channel_id=1, source_target_pairs={{0,4},{1,5},{2,6},{3,7},{4,0},{5,1},{6,2},{7,3},{8,12},{9,13},{10,... | collective-permute-start | bytes 196616 | tf_op jit(solution)/shard_map/ppermute | solution.py:442
  86.7 0.5 collective-permute-start.8
  87.2 0.1 fusion
  87.3 0.1 reshape.37.index_ref
  87.4 4.5 %give_back.1.after_ref = bf16[2048,512]{1,0:T(8,128)(2,1)} custom-call(s32[1,1024]{1,0:T(1,128)S(1)} %reshape.37.index_ref, f32[1024,512]{1,0:T(8,128)} %spread.2.first_hbm.after_ref, f32[1024,512]{1,0:T(8,128)} %spread.3.second_hbm.after_ref, bf16[1024,512]{1,0:T(8,128)(2,1)S(1)} %bitcast.9), custom_call_target="tpu_custom_call" | custom-call | tf_op jit(solution)/shard_map/give_back/pallas_call | solution.py:343
  92.0 0.1 collective-permute-start.9
  92.1 0.8 place.2.refs_0_
  92.9 0.7 collective-permute-done.9.half_ref
  93.6 0.8 place.3
  (22 shorter events, 0.2 us)
Async XLA Ops:
  0.6 12.5 %copy-start = (bf16[2048,512]{1,0:T(8,128)(2,1)S(1)}, bf16[2048,512]{1,0:T(8,128)(2,1)}, u32[]{:S(2)}) copy-start(bf16[2048,512]{1,0:T(8,128)(2,1)} %x_ref.3) | copy-start | bytes 6291460
  0.6 12.5 %copy-start.1 = (s32[256]{0:T(256)S(1)}, s32[256]{0:T(256)}, u32[]{:S(2)}) copy-start(s32[256]{0:T(256)} %rows_ref.1) | copy-start | bytes 3076
  0.7 12.5 %copy-start.2 = (s32[256]{0:T(256)S(1)}, s32[256]{0:T(256)}, u32[]{:S(2)}) copy-start(s32[256]{0:T(256)} %cols_ref.1) | copy-start | bytes 3076
  5.8 32.4 %all-to-all-start = ((bf16[32,32,512]{2,1,0:T(8,128)(2,1)}), bf16[32,32,512]{2,1,0:T(8,128)(2,1)S(1)}, u32[]{:S(2)}, u32[]{:S(2)}) async-start(bf16[32,32,512]{2,1,0:T(8,128)(2,1)} %bitcast.11), calls=%async_computation | async-start | bytes 2097152 | tf_op jit(solution)/shard_map/all_to_all | solution.py:360
  50.1 37.3 %all-to-all-start.1 = ((bf16[32,32,512]{2,1,0:T(8,128)(2,1)}), bf16[32,32,512]{2,1,0:T(8,128)(2,1)S(1)}, u32[]{:S(2)}, u32[]{:S(2)}) async-start(bf16[32,32,512]{2,1,0:T(8,128)(2,1)} %bitcast.12), calls=%async_computation.1 | async-start | bytes 2097152 | tf_op jit(solution)/shard_map/all_to_all | solution.py:360
  57.7 1.6 %collective-permute-start = (bf16[256,512]{1,0:T(8,128)(2,1)S(1)}, bf16[256,512]{1,0:T(8,128)(2,1)S(1)}, u32[]{:S(2)}, u32[]{:S(2)}) collective-permute-start(bf16[256,512]{1,0:T(8,128)(2,1)S(1)} %get-tuple-element.26), channel_id=1, source_target_pairs={{0,1},{1,0},{2,3},{3,2},{4,5},{5,4},{6,7},{7,6},{8,9},{9,8},{10,11... | collective-permute-start | bytes 786440 | tf_op jit(solution)/shard_map/ppermute | solution.py:442
  59.3 9.4 %collective-permute-start.1 = (bf16[64,512]{1,0:T(8,128)(2,1)S(1)}, bf16[64,512]{1,0:T(8,128)(2,1)S(1)}, u32[]{:S(2)}, u32[]{:S(2)}) collective-permute-start(bf16[64,512]{1,0:T(8,128)(2,1)S(1)} %get-tuple-element.28), channel_id=1, source_target_pairs={{0,2},{1,3},{2,0},{3,1},{4,6},{5,7},{6,4},{7,5},{8,10},{9,11},{10,... | collective-permute-start | bytes 196616 | tf_op jit(solution)/shard_map/ppermute | solution.py:442
  61.0 8.2 %collective-permute-start.2 = (bf16[64,512]{1,0:T(8,128)(2,1)S(1)}, bf16[64,512]{1,0:T(8,128)(2,1)S(1)}, u32[]{:S(2)}, u32[]{:S(2)}) collective-permute-start(bf16[64,512]{1,0:T(8,128)(2,1)S(1)} %get-tuple-element.29), channel_id=1, source_target_pairs={{0,4},{1,5},{2,6},{3,7},{4,0},{5,1},{6,2},{7,3},{8,12},{9,13},{10,... | collective-permute-start | bytes 196616 | tf_op jit(solution)/shard_map/ppermute | solution.py:442
  62.5 6.8 %collective-permute-start.3 = (bf16[64,512]{1,0:T(8,128)(2,1)S(1)}, bf16[64,512]{1,0:T(8,128)(2,1)S(1)}, u32[]{:S(2)}, u32[]{:S(2)}) collective-permute-start(bf16[64,512]{1,0:T(8,128)(2,1)S(1)} %get-tuple-element.30), channel_id=1, source_target_pairs={{0,6},{1,7},{2,4},{3,5},{4,2},{5,3},{6,0},{7,1},{8,14},{9,15},{10,... | collective-permute-start | bytes 196616 | tf_op jit(solution)/shard_map/ppermute | solution.py:442
  69.3 6.9 %collective-permute-start.4 = (bf16[64,512]{1,0:T(8,128)(2,1)S(1)}, bf16[64,512]{1,0:T(8,128)(2,1)S(1)}, u32[]{:S(2)}, u32[]{:S(2)}) collective-permute-start(bf16[64,512]{1,0:T(8,128)(2,1)S(1)} %add.7.refs_0_), channel_id=1, source_target_pairs={{0,8},{8,0},{16,24},{24,16},{1,9},{9,1},{17,25},{25,17},{2,10},{10... | collective-permute-start | bytes 196616 | tf_op jit(solution)/shard_map/ppermute | solution.py:442
  76.2 4.5 %copy-start.4 = (s32[1,32]{1,0:T(1,128)S(1)}, s32[1,32]{1,0:T(1,128)}, u32[]{:S(2)}) copy-start(s32[1,32]{1,0:T(1,128)} %counts_ref.1) | copy-start | bytes 388
  76.2 11.0 %copy-start.3 = (s32[1,32,32]{2,1,0:T(8,128)S(1)}, s32[1,32,32]{2,1,0:T(8,128)}, u32[]{:S(2)}) copy-start(s32[1,32,32]{2,1,0:T(8,128)} %param.14) | copy-start | bytes 12292
  76.2 7.4 %collective-permute-start.5 = (bf16[64,512]{1,0:T(8,128)(2,1)S(1)}, bf16[64,512]{1,0:T(8,128)(2,1)S(1)}, u32[]{:S(2)}, u32[]{:S(2)}) collective-permute-start(bf16[64,512]{1,0:T(8,128)(2,1)S(1)} %add.8.refs_0_), channel_id=1, source_target_pairs={{0,16},{8,24},{16,0},{24,8},{1,17},{9,25},{17,1},{25,9},{2,18},{10... | collective-permute-start | bytes 196616 | tf_op jit(solution)/shard_map/ppermute | solution.py:442
  83.7 8.3 %collective-permute-start.6 = (bf16[64,512]{1,0:T(8,128)(2,1)S(1)}, bf16[64,512]{1,0:T(8,128)(2,1)S(1)}, u32[]{:S(2)}, u32[]{:S(2)}) collective-permute-start(bf16[64,512]{1,0:T(8,128)(2,1)S(1)} %add.9.refs_0_), channel_id=1, source_target_pairs={{0,2},{1,3},{2,0},{3,1},{4,6},{5,7},{6,4},{7,5},{8,10},{9,11},{10,... | collective-permute-start | bytes 196616 | tf_op jit(solution)/shard_map/ppermute | solution.py:442
  85.2 6.7 %collective-permute-start.7 = (bf16[64,512]{1,0:T(8,128)(2,1)S(1)}, bf16[64,512]{1,0:T(8,128)(2,1)S(1)}, u32[]{:S(2)}, u32[]{:S(2)}) collective-permute-start(bf16[64,512]{1,0:T(8,128)(2,1)S(1)} %add.9.refs_0_), channel_id=1, source_target_pairs={{0,4},{1,5},{2,6},{3,7},{4,0},{5,1},{6,2},{7,3},{8,12},{9,13},{10,... | collective-permute-start | bytes 196616 | tf_op jit(solution)/shard_map/ppermute | solution.py:442
  86.7 5.3 %collective-permute-start.8 = (bf16[64,512]{1,0:T(8,128)(2,1)S(1)}, bf16[64,512]{1,0:T(8,128)(2,1)S(1)}, u32[]{:S(2)}, u32[]{:S(2)}) collective-permute-start(bf16[64,512]{1,0:T(8,128)(2,1)S(1)} %add.9.refs_0_), channel_id=1, source_target_pairs={{0,6},{1,7},{2,4},{3,5},{4,2},{5,3},{6,0},{7,1},{8,14},{9,15},{10,... | collective-permute-start | bytes 196616 | tf_op jit(solution)/shard_map/ppermute | solution.py:442
  92.0 1.6 %collective-permute-start.9 = (bf16[256,512]{1,0:T(8,128)(2,1)S(1)}, bf16[256,512]{1,0:T(8,128)(2,1)S(1)}, u32[]{:S(2)}, u32[]{:S(2)}) collective-permute-start(bf16[256,512]{1,0:T(8,128)(2,1)S(1)} %relay.1.half_ref), channel_id=1, source_target_pairs={{0,1},{1,0},{2,3},{3,2},{4,5},{5,4},{6,7},{7,6},{8,9},{9,8},{10,11... | collective-permute-start | bytes 786440 | tf_op jit(solution)/shard_map/ppermute | solution.py:442

commit v12 on v10

--- a/solution.py
+++ b/solution.py
@@ -464,10 +464,7 @@
     mine, other = partial_grad(keep, me, hidden, slope)
     pieces = cut(me, mine, swap(other, "local", locals_, 1), chips)
     piece = add(first, [pieces[0]] + [swap(pieces[k], "local", locals_, 2 * k) for k in range(1, chips)])
-    step, after = 1, second
-    while step < groups:
-        piece = add(after, [piece, swap(piece, "group", groups, step)])
-        step, after = 2 * step, second
+    piece = add(second, [piece] + [swap(piece, "group", groups, k) for k in range(1, groups)])
     pieces = [piece] + [swap(piece, "local", locals_, 2 * k) for k in range(1, chips)]
     half = relay(feature_grad, pieces)
     weight_grad = place(me, swap(half, "local", locals_, 1), chips, [place(me, half, chips)])

time: 95 us -> 96.8 us (1.019)
  waiting for transfers between devices: 10.3 us -> 12.2 us
    ppermute x10 -> x11, waiting for transfers between devices: 4.77 us -> 6.74 us  [swap(): return lax.ppermute(x, axis, [(i, i ^ k) for i in range(size)])]
    ppermute x10 -> x11, starting transfers between devices: 12.4 us -> 12.4 us  [swap(): return lax.ppermute(x, axis, [(i, i ^ k) for i in range(size)])]
  transfers between devices with their start and end apart: 12 -> 13, of which waited for: 5 -> 5; matrix products, arithmetic and copies ran while one was open for 2% -> 2% of each run, Pallas kernels for 42% -> 41%
where the time goes in v12:
time: 96.8 us; the launch traced here: 96.5 us
  Pallas kernels  57.5 us (59%)
  starting transfers between devices  24.3 us (25%)
  waiting for transfers between devices  12.2 us (13%)
  between operations  0.97 us (1%)
    pallas_call x1, Pallas kernels, build(): pl.pallas_call(build_kernel, grid_spec=pltpu.PrefetchScalarGridSpec(num_s...  19.5 us
    ppermute x11, starting transfers between devices, swap(): return lax.ppermute(x, axis, [(i, i ^ k) for i in range(size)])  12.4 us
    all_to_all x2, starting transfers between devices, exchange(): return lax.all_to_all(x, axes, split_axis=0, concat_axis=0, tiled=True)  11.9 us
    pallas_call x1, Pallas kernels, layer(): pl.pallas_call(functools.partial(layer_kernel, order), in_specs=[HBM] * 4...  11.9 us
    pallas_call x2, Pallas kernels, spread(): pl.pallas_call(spread_kernel, grid=(blocks,), in_specs=[pl.BlockSpec((own...  11.6 us
    ppermute x11, waiting for transfers between devices, swap(): return lax.ppermute(x, axis, [(i, i ^ k) for i in range(size)])  6.74 us
    all_to_all x2, waiting for transfers between devices, exchange(): return lax.all_to_all(x, axes, split_axis=0, concat_axis=0, tiled=True)  5.49 us
    pallas_call x1, Pallas kernels, collect(): pl.pallas_call(functools.partial(collect_kernel, order), in_specs=[SMEM,...  5.17 us
  transfers between devices with their start and end apart: 13, of which 5 were waited for; matrix products, arithmetic and copies ran while one was open for 2% of the time, Pallas kernels for 41%

profile of v12, /device:TPU:0, one launch (start us, length us, event | category | flops | bytes accessed | tf_op | source)
XLA Modules:
  0.0 96.5 jit_solution(3915864212992110524)
XLA Ops:
  0.7 5.2 %collect.1 = bf16[1024,512]{1,0:T(8,128)(2,1)} custom-call(s32[1,32]{1,0:T(1,128)} %counts_ref.1, s32[32,32]{1,0:T(8,128)} %bitcast.13, bf16[2048,512]{1,0:T(8,128)(2,1)} %x_ref.3), custom_call_target="tpu_custom_call" | custom-call | tf_op jit(solution)/shard_map/collect/pallas_call | solution.py:71
  5.8 7.3 %all-to-all-start = ((bf16[32,32,512]{2,1,0:T(8,128)(2,1)}), bf16[32,32,512]{2,1,0:T(8,128)(2,1)S(1)}, u32[]{:S(2)}, u32[]{:S(2)}) async-start(bf16[32,32,512]{2,1,0:T(8,128)(2,1)} %bitcast.11), calls=%async_computation | async-start | bytes 2097152 | tf_op jit(solution)/shard_map/all_to_all | solution.py:360
  13.2 19.5 %build.1 = (bf16[2048,2048]{1,0:T(8,128)(2,1)}, bf16[2048,1024]{1,0:T(8,128)(2,1)}, f32[2048,512]{1,0:T(8,128)}) custom-call(s32[256]{0:T(256)S(1)} %copy-done.1, s32[256]{0:T(256)S(1)} %copy-done.2, bf16[256,128,128]{2,1,0:T(8,128)(2,1)} %tiles_ref.1, bf16[2048,512]{1,0:T(8,128)(2,1)S(1)} %copy-done), custom_call_target="tpu_custom_call" | custom-call | flops 4294967296 | bytes 41943040 | tf_op jit(solution)/shard_map/build/pallas_call | solution.py:139
  32.7 5.5 %all-to-all-done = bf16[32,32,512]{2,1,0:T(8,128)(2,1)S(1)} async-done(((bf16[32,32,512]{2,1,0:T(8,128)(2,1)}), bf16[32,32,512]{2,1,0:T(8,128)(2,1)S(1)}, u32[]{:S(2)}, u32[]{:S(2)}) %all-to-all-start) | async-done | bytes 1048608 | tf_op jit(solution)/shard_map/all_to_all | solution.py:360
  38.2 11.9 %layer.1 = (bf16[2048,512]{1,0:T(8,128)(2,1)}, bf16[2048,512]{1,0:T(8,128)(2,1)}, bf16[2048,512]{1,0:T(8,128)(2,1)}, bf16[2048,512]{1,0:T(8,128)(2,1)}, bf16[1024,512]{1,0:T(8,128)(2,1)}) custom-call(bf16[2048,1024]{1,0:T(8,128)(2,1)} %get-tuple-element.17.far_hbm, f32[2048,512]{1,0:T(8,128)} %get-tuple-element.18.own_hbm, bf16[2048,512]{1,0:T(8,128)(2,1)} %cot_hbm.1, ...), custom_call_target="tpu_custom_call" | custom-call | tf_op jit(solution)/shard_map/layer/pallas_call | solution.py:233
  50.1 4.6 %all-to-all-start.1 = ((bf16[32,32,512]{2,1,0:T(8,128)(2,1)}), bf16[32,32,512]{2,1,0:T(8,128)(2,1)S(1)}, u32[]{:S(2)}, u32[]{:S(2)}) async-start(bf16[32,32,512]{2,1,0:T(8,128)(2,1)} %bitcast.12), calls=%async_computation.1 | async-start | bytes 2097152 | tf_op jit(solution)/shard_map/all_to_all | solution.py:360
  54.8 2.9 %partial_grad.1 = (f32[256,512]{1,0:T(8,128)S(1)}, bf16[256,512]{1,0:T(8,128)(2,1)S(1)}) custom-call(s32[1]{0:T(128)} %bitcast.7.me_ref, bf16[2048,512]{1,0:T(8,128)(2,1)} %get-tuple-element.23.hid_hbm, bf16[2048,512]{1,0:T(8,128)(2,1)} %get-tuple-element.24.slope_hbm), custom_call_target="tpu_custom_call" | custom-call | tf_op jit(solution)/shard_map/partial_grad/pallas_call | solution.py:278
  57.7 0.1 collective-permute-start
  57.8 0.5 broadcast.9
  58.3 0.7 reduce.3
  59.0 0.1 lt.17
  59.1 0.1 copy.12
  59.2 0.1 collective-permute-done.got_ref
  59.3 1.7 %collective-permute-start.1 = (bf16[64,512]{1,0:T(8,128)(2,1)S(1)}, bf16[64,512]{1,0:T(8,128)(2,1)S(1)}, u32[]{:S(2)}, u32[]{:S(2)}) collective-permute-start(bf16[64,512]{1,0:T(8,128)(2,1)S(1)} %get-tuple-element.28), channel_id=1, source_target_pairs={{0,2},{1,3},{2,0},{3,1},{4,6},{5,7},{6,4},{7,5},{8,10},{9,11},{10,... | collective-permute-start | bytes 196616 | tf_op jit(solution)/shard_map/ppermute | solution.py:442
  61.0 1.5 %collective-permute-start.2 = (bf16[64,512]{1,0:T(8,128)(2,1)S(1)}, bf16[64,512]{1,0:T(8,128)(2,1)S(1)}, u32[]{:S(2)}, u32[]{:S(2)}) collective-permute-start(bf16[64,512]{1,0:T(8,128)(2,1)S(1)} %get-tuple-element.29), channel_id=1, source_target_pairs={{0,4},{1,5},{2,6},{3,7},{4,0},{5,1},{6,2},{7,3},{8,12},{9,13},{10,... | collective-permute-start | bytes 196616 | tf_op jit(solution)/shard_map/ppermute | solution.py:442
  62.5 0.4 collective-permute-start.3
  62.9 5.8 %spread.2.first_hbm.after_ref = f32[1024,512]{1,0:T(8,128)} custom-call(bf16[2048,2048]{1,0:T(8,128)(2,1)} %get-tuple-element.20.adj_ref, bf16[2048,512]{1,0:T(8,128)(2,1)} %get-tuple-element.21.grad_ref), custom_call_target="tpu_custom_call" | custom-call | flops 4294967296 | bytes 16777216 | tf_op jit(solution)/shard_map/spread/pallas_call | solution.py:301
  68.7 0.5 collective-permute-done.2.refs_2_
  69.3 1.1 %collective-permute-start.4 = (bf16[64,512]{1,0:T(8,128)(2,1)S(1)}, bf16[64,512]{1,0:T(8,128)(2,1)S(1)}, u32[]{:S(2)}, u32[]{:S(2)}) collective-permute-start(bf16[64,512]{1,0:T(8,128)(2,1)S(1)} %add.6.refs_0_), channel_id=1, source_target_pairs={{0,8},{8,0},{16,24},{24,16},{1,9},{9,1},{17,25},{25,17},{2,10},{10... | collective-permute-start | bytes 196616 | tf_op jit(solution)/shard_map/ppermute | solution.py:442
  70.4 3.9 %collective-permute-start.5 = (bf16[64,512]{1,0:T(8,128)(2,1)S(1)}, bf16[64,512]{1,0:T(8,128)(2,1)S(1)}, u32[]{:S(2)}, u32[]{:S(2)}) collective-permute-start(bf16[64,512]{1,0:T(8,128)(2,1)S(1)} %add.6.refs_0_), channel_id=1, source_target_pairs={{0,16},{8,24},{16,0},{24,8},{1,17},{9,25},{17,1},{25,9},{2,18},{10... | collective-permute-start | bytes 196616 | tf_op jit(solution)/shard_map/ppermute | solution.py:442
  74.3 5.8 %spread.3.second_hbm.after_ref = f32[1024,512]{1,0:T(8,128)} custom-call(bf16[2048,2048]{1,0:T(8,128)(2,1)} %get-tuple-element.20.adj_ref, bf16[2048,512]{1,0:T(8,128)(2,1)} %get-tuple-element.21.grad_ref), custom_call_target="tpu_custom_call" | custom-call | flops 4294967296 | bytes 16777216 | tf_op jit(solution)/shard_map/spread/pallas_call | solution.py:301
  80.1 5.4 %collective-permute-done.5.refs_2_ = bf16[64,512]{1,0:T(8,128)(2,1)S(1)} collective-permute-done((bf16[64,512]{1,0:T(8,128)(2,1)S(1)}, bf16[64,512]{1,0:T(8,128)(2,1)S(1)}, u32[]{:S(2)}, u32[]{:S(2)}) %collective-permute-start.5) | collective-permute-done | bytes 65568 | tf_op jit(solution)/shard_map/ppermute | solution.py:442
  85.6 1.5 %collective-permute-start.7 = (bf16[64,512]{1,0:T(8,128)(2,1)S(1)}, bf16[64,512]{1,0:T(8,128)(2,1)S(1)}, u32[]{:S(2)}, u32[]{:S(2)}) collective-permute-start(bf16[64,512]{1,0:T(8,128)(2,1)S(1)} %add.7.refs_0_), channel_id=1, source_target_pairs={{0,2},{1,3},{2,0},{3,1},{4,6},{5,7},{6,4},{7,5},{8,10},{9,11},{10,... | collective-permute-start | bytes 196616 | tf_op jit(solution)/shard_map/ppermute | solution.py:442
  87.1 1.5 %collective-permute-start.8 = (bf16[64,512]{1,0:T(8,128)(2,1)S(1)}, bf16[64,512]{1,0:T(8,128)(2,1)S(1)}, u32[]{:S(2)}, u32[]{:S(2)}) collective-permute-start(bf16[64,512]{1,0:T(8,128)(2,1)S(1)} %add.7.refs_0_), channel_id=1, source_target_pairs={{0,4},{1,5},{2,6},{3,7},{4,0},{5,1},{6,2},{7,3},{8,12},{9,13},{10,... | collective-permute-start | bytes 196616 | tf_op jit(solution)/shard_map/ppermute | solution.py:442
  88.6 0.5 collective-permute-start.9
  89.1 0.1 fusion
  89.2 0.1 reshape.37.index_ref
  89.3 4.5 %give_back.1.after_ref = bf16[2048,512]{1,0:T(8,128)(2,1)} custom-call(s32[1,1024]{1,0:T(1,128)S(1)} %reshape.37.index_ref, f32[1024,512]{1,0:T(8,128)} %spread.2.first_hbm.after_ref, f32[1024,512]{1,0:T(8,128)} %spread.3.second_hbm.after_ref, bf16[1024,512]{1,0:T(8,128)(2,1)S(1)} %bitcast.9), custom_call_target="tpu_custom_call" | custom-call | tf_op jit(solution)/shard_map/give_back/pallas_call | solution.py:343
  93.9 0.1 collective-permute-start.10
  94.0 0.8 place.2.refs_0_
  94.8 0.7 collective-permute-done.10.half_ref
  95.5 0.8 place.3
  (23 shorter events, 0.2 us)
Async XLA Ops:
  0.6 12.5 %copy-start = (bf16[2048,512]{1,0:T(8,128)(2,1)S(1)}, bf16[2048,512]{1,0:T(8,128)(2,1)}, u32[]{:S(2)}) copy-start(bf16[2048,512]{1,0:T(8,128)(2,1)} %x_ref.3) | copy-start | bytes 6291460
  0.6 12.5 %copy-start.1 = (s32[256]{0:T(256)S(1)}, s32[256]{0:T(256)}, u32[]{:S(2)}) copy-start(s32[256]{0:T(256)} %rows_ref.1) | copy-start | bytes 3076
  0.7 12.5 %copy-start.2 = (s32[256]{0:T(256)S(1)}, s32[256]{0:T(256)}, u32[]{:S(2)}) copy-start(s32[256]{0:T(256)} %cols_ref.1) | copy-start | bytes 3076
  5.8 32.4 %all-to-all-start = ((bf16[32,32,512]{2,1,0:T(8,128)(2,1)}), bf16[32,32,512]{2,1,0:T(8,128)(2,1)S(1)}, u32[]{:S(2)}, u32[]{:S(2)}) async-start(bf16[32,32,512]{2,1,0:T(8,128)(2,1)} %bitcast.11), calls=%async_computation | async-start | bytes 2097152 | tf_op jit(solution)/shard_map/all_to_all | solution.py:360
  50.1 39.2 %all-to-all-start.1 = ((bf16[32,32,512]{2,1,0:T(8,128)(2,1)}), bf16[32,32,512]{2,1,0:T(8,128)(2,1)S(1)}, u32[]{:S(2)}, u32[]{:S(2)}) async-start(bf16[32,32,512]{2,1,0:T(8,128)(2,1)} %bitcast.12), calls=%async_computation.1 | async-start | bytes 2097152 | tf_op jit(solution)/shard_map/all_to_all | solution.py:360
  54.8 3.6 %copy-start.4 = (s32[1,32]{1,0:T(1,128)S(1)}, s32[1,32]{1,0:T(1,128)}, u32[]{:S(2)}) copy-start(s32[1,32]{1,0:T(1,128)} %counts_ref.1) | copy-start | bytes 388
  57.7 1.6 %collective-permute-start = (bf16[256,512]{1,0:T(8,128)(2,1)S(1)}, bf16[256,512]{1,0:T(8,128)(2,1)S(1)}, u32[]{:S(2)}, u32[]{:S(2)}) collective-permute-start(bf16[256,512]{1,0:T(8,128)(2,1)S(1)} %get-tuple-element.26), channel_id=1, source_target_pairs={{0,1},{1,0},{2,3},{3,2},{4,5},{5,4},{6,7},{7,6},{8,9},{9,8},{10,11... | collective-permute-start | bytes 786440 | tf_op jit(solution)/shard_map/ppermute | solution.py:442
  59.3 9.3 %collective-permute-start.1 = (bf16[64,512]{1,0:T(8,128)(2,1)S(1)}, bf16[64,512]{1,0:T(8,128)(2,1)S(1)}, u32[]{:S(2)}, u32[]{:S(2)}) collective-permute-start(bf16[64,512]{1,0:T(8,128)(2,1)S(1)} %get-tuple-element.28), channel_id=1, source_target_pairs={{0,2},{1,3},{2,0},{3,1},{4,6},{5,7},{6,4},{7,5},{8,10},{9,11},{10,... | collective-permute-start | bytes 196616 | tf_op jit(solution)/shard_map/ppermute | solution.py:442
  61.0 8.2 %collective-permute-start.2 = (bf16[64,512]{1,0:T(8,128)(2,1)S(1)}, bf16[64,512]{1,0:T(8,128)(2,1)S(1)}, u32[]{:S(2)}, u32[]{:S(2)}) collective-permute-start(bf16[64,512]{1,0:T(8,128)(2,1)S(1)} %get-tuple-element.29), channel_id=1, source_target_pairs={{0,4},{1,5},{2,6},{3,7},{4,0},{5,1},{6,2},{7,3},{8,12},{9,13},{10,... | collective-permute-start | bytes 196616 | tf_op jit(solution)/shard_map/ppermute | solution.py:442
  62.5 6.8 %collective-permute-start.3 = (bf16[64,512]{1,0:T(8,128)(2,1)S(1)}, bf16[64,512]{1,0:T(8,128)(2,1)S(1)}, u32[]{:S(2)}, u32[]{:S(2)}) collective-permute-start(bf16[64,512]{1,0:T(8,128)(2,1)S(1)} %get-tuple-element.30), channel_id=1, source_target_pairs={{0,6},{1,7},{2,4},{3,5},{4,2},{5,3},{6,0},{7,1},{8,14},{9,15},{10,... | collective-permute-start | bytes 196616 | tf_op jit(solution)/shard_map/ppermute | solution.py:442
  69.3 10.9 %collective-permute-start.4 = (bf16[64,512]{1,0:T(8,128)(2,1)S(1)}, bf16[64,512]{1,0:T(8,128)(2,1)S(1)}, u32[]{:S(2)}, u32[]{:S(2)}) collective-permute-start(bf16[64,512]{1,0:T(8,128)(2,1)S(1)} %add.6.refs_0_), channel_id=1, source_target_pairs={{0,8},{8,0},{16,24},{24,16},{1,9},{9,1},{17,25},{25,17},{2,10},{10... | collective-permute-start | bytes 196616 | tf_op jit(solution)/shard_map/ppermute | solution.py:442
  70.4 15.1 %collective-permute-start.5 = (bf16[64,512]{1,0:T(8,128)(2,1)S(1)}, bf16[64,512]{1,0:T(8,128)(2,1)S(1)}, u32[]{:S(2)}, u32[]{:S(2)}) collective-permute-start(bf16[64,512]{1,0:T(8,128)(2,1)S(1)} %add.6.refs_0_), channel_id=1, source_target_pairs={{0,16},{8,24},{16,0},{24,8},{1,17},{9,25},{17,1},{25,9},{2,18},{10... | collective-permute-start | bytes 196616 | tf_op jit(solution)/shard_map/ppermute | solution.py:442
  74.3 11.2 %collective-permute-start.6 = (bf16[64,512]{1,0:T(8,128)(2,1)S(1)}, bf16[64,512]{1,0:T(8,128)(2,1)S(1)}, u32[]{:S(2)}, u32[]{:S(2)}) collective-permute-start(bf16[64,512]{1,0:T(8,128)(2,1)S(1)} %add.6.refs_0_), channel_id=1, source_target_pairs={{0,24},{8,16},{16,8},{24,0},{1,25},{9,17},{17,9},{25,1},{2,26},{10... | collective-permute-start | bytes 196616 | tf_op jit(solution)/shard_map/ppermute | solution.py:442
  80.1 9.0 %copy-start.3 = (s32[1,32,32]{2,1,0:T(8,128)S(1)}, s32[1,32,32]{2,1,0:T(8,128)}, u32[]{:S(2)}) copy-start(s32[1,32,32]{2,1,0:T(8,128)} %param.14) | copy-start | bytes 12292
  85.6 8.3 %collective-permute-start.7 = (bf16[64,512]{1,0:T(8,128)(2,1)S(1)}, bf16[64,512]{1,0:T(8,128)(2,1)S(1)}, u32[]{:S(2)}, u32[]{:S(2)}) collective-permute-start(bf16[64,512]{1,0:T(8,128)(2,1)S(1)} %add.7.refs_0_), channel_id=1, source_target_pairs={{0,2},{1,3},{2,0},{3,1},{4,6},{5,7},{6,4},{7,5},{8,10},{9,11},{10,... | collective-permute-start | bytes 196616 | tf_op jit(solution)/shard_map/ppermute | solution.py:442
  87.1 6.7 %collective-permute-start.8 = (bf16[64,512]{1,0:T(8,128)(2,1)S(1)}, bf16[64,512]{1,0:T(8,128)(2,1)S(1)}, u32[]{:S(2)}, u32[]{:S(2)}) collective-permute-start(bf16[64,512]{1,0:T(8,128)(2,1)S(1)} %add.7.refs_0_), channel_id=1, source_target_pairs={{0,4},{1,5},{2,6},{3,7},{4,0},{5,1},{6,2},{7,3},{8,12},{9,13},{10,... | collective-permute-start | bytes 196616 | tf_op jit(solution)/shard_map/ppermute | solution.py:442
  88.6 5.3 %collective-permute-start.9 = (bf16[64,512]{1,0:T(8,128)(2,1)S(1)}, bf16[64,512]{1,0:T(8,128)(2,1)S(1)}, u32[]{:S(2)}, u32[]{:S(2)}) collective-permute-start(bf16[64,512]{1,0:T(8,128)(2,1)S(1)} %add.7.refs_0_), channel_id=1, source_target_pairs={{0,6},{1,7},{2,4},{3,5},{4,2},{5,3},{6,0},{7,1},{8,14},{9,15},{10,... | collective-permute-start | bytes 196616 | tf_op jit(solution)/shard_map/ppermute | solution.py:442
  93.9 1.6 %collective-permute-start.10 = (bf16[256,512]{1,0:T(8,128)(2,1)S(1)}, bf16[256,512]{1,0:T(8,128)(2,1)S(1)}, u32[]{:S(2)}, u32[]{:S(2)}) collective-permute-start(bf16[256,512]{1,0:T(8,128)(2,1)S(1)} %relay.1.half_ref), channel_id=1, source_target_pairs={{0,1},{1,0},{2,3},{3,2},{4,5},{5,4},{6,7},{7,6},{8,9},{9,8},{10,11... | collective-permute-start | bytes 786440 | tf_op jit(solution)/shard_map/ppermute | solution.py:442
